TPU v7x, 32 devices: a whole 2x2x4 slice. The times are simulated.
32 devices in a mesh: rep: 4 (over y, core), shard: 8 (over z, x).
Axes of the slice: x: 2, y: 2, z: 4, core: 2. Of those that a mesh axis runs over, the one named last changes fastest.
Arguments:
- tokens: bfloat16 [8192, 1280], P(('rep', 'shard')), may hold values from -6 to 6
- lengths: int32 [4, 13], P('rep'), may hold values from 1 to 512, 2048 in all within a row
- parents: int32 [4, 13], P('rep'), may hold values from 0 to 11, as said below
- w_query: bfloat16 [1280, 1280], P('shard'), may hold values from -0.15625 to 0.15625
- w_key: bfloat16 [1280, 1280], P('shard'), may hold values from -0.15625 to 0.15625
- w_value: bfloat16 [1280, 1280], P('shard'), may hold values from -0.15625 to 0.15625
- w_out: bfloat16 [1280, 1280], P('shard'), may hold values from -1 to 1
- w_up: bfloat16 [1280, 1280], P('shard'), may hold values from -0.15625 to 0.15625
- w_down: bfloat16 [1280, 1280], P('shard'), may hold values from -0.15625 to 0.15625
- gain_attn: float32 [1280], replicated, may hold values from 0.1 to 1.9
- gain_ff: float32 [1280], replicated, may hold values from 0.1 to 1.9
- query_scale: float32 [80], replicated, may hold values from 0 to 2
- bias_query: float32 [1280], replicated, may hold values from -3 to 3
- bias_value: float32 [1280], replicated, may hold values from -3 to 3
- bias_out: float32 [1280], replicated, may hold values from -3 to 3
- bias_up: float32 [1280], replicated, may hold values from -3 to 3
- bias_down: float32 [1280], replicated, may hold values from -3 to 3
- cotangent: bfloat16 [8192, 1280], P(('rep', 'shard')), may hold values from -6 to 6
Outputs:
- output: bfloat16 [8192, 1280], P(('rep', 'shard'))
- grad_tokens: bfloat16 [8192, 1280], P(('rep', 'shard'))
- grad_query: float32 [1280, 1280], P('shard')
- grad_key: float32 [1280, 1280], P('shard')
- grad_value: float32 [1280, 1280], P('shard')
- grad_out: float32 [1280, 1280], P('shard')
- grad_up: float32 [1280, 1280], P('shard')
- grad_down: float32 [1280, 1280], P('shard')
- grad_gain_attn: float32 [1280], replicated
- grad_gain_ff: float32 [1280], replicated
- grad_query_scale: float32 [80], replicated
- grad_bias_query: float32 [1280], replicated
- grad_bias_value: float32 [1280], replicated
- grad_bias_out: float32 [1280], replicated
- grad_bias_up: float32 [1280], replicated
- grad_bias_down: float32 [1280], replicated
Inputs may be any that keep to these rules, and one draw needn't show every extreme that they name: parents[g, 0] = 0 and parents[g, s] < s for s >= 1; the last segment's parent is the segment before it. `lengths`: each row sums to 2048.
All inputs are finite; a program needn't handle non-finite values.
Results may differ from a plain program's by a relative error of at most 0.02.
Values may be sent and summed in bfloat16 or wider, within the bound.
A program may use at most 256 MiB of HBM per device.

v0:
```python
import math

import jax
import jax.numpy as jnp
from jax import lax
from jax.sharding import PartitionSpec as P

HEADS = 16
HEAD_DIM = 80


norm_eps = 1e-06
query_base = 1.442695
masked_score = -1e30


def tree_tables(lengths, parents):
    seg_ends = jnp.cumsum(lengths, dtype=jnp.int32)
    segments = lengths.shape[0]
    labels = jnp.arange(segments, dtype=jnp.int32)
    link = ((parents[:, None] == labels[None, :]) & (labels[:, None] > 0)).astype(jnp.float32)
    identity = jnp.eye(segments, dtype=jnp.float32)
    ancestry = identity
    for depth_step in range(segments):
        ancestry = jnp.minimum(identity + jnp.dot(link, ancestry), 1.0)
    return (seg_ends, ancestry)


def segment_onehot(positions, seg_ends):
    labels = jnp.sum((positions[:, None] >= seg_ends[None, :]).astype(jnp.int32), axis=1)
    return (labels[:, None] == jnp.arange(seg_ends.shape[0], dtype=jnp.int32)[None, :]).astype(
        jnp.float32
    )


def pair_mask(query_reach, query_pos, key_pos, seg_ends):
    linked = jnp.dot(query_reach, segment_onehot(key_pos, seg_ends).T) > 0.5
    return linked & (key_pos[None, :] <= query_pos[:, None])


def block_grads(
    queries,
    out_grad,
    log_total,
    row_delta,
    query_reach,
    query_pos,
    key_rows,
    value_rows,
    key_pos,
    seg_ends,
):
    allowed = pair_mask(query_reach, query_pos, key_pos, seg_ends)
    scores = jnp.einsum("qhd,khd->hqk", queries, key_rows, preferred_element_type=jnp.float32)
    weights = jnp.where(allowed[None], jnp.exp(scores - log_total[:, :, None]), 0.0)
    prob_grad = jnp.einsum("qhd,khd->hqk", out_grad, value_rows, preferred_element_type=jnp.float32)
    score_grad = (weights * (prob_grad - row_delta[:, :, None])).astype(jnp.bfloat16)
    query_grad = jnp.einsum(
        "hqk,khd->qhd", score_grad, key_rows, preferred_element_type=jnp.float32
    )
    key_grad = jnp.einsum("hqk,qhd->khd", score_grad, queries, preferred_element_type=jnp.float32)
    value_grad = jnp.einsum(
        "hqk,qhd->khd", weights.astype(jnp.bfloat16), out_grad, preferred_element_type=jnp.float32
    )
    return (query_grad, key_grad, value_grad)


def norm_back(grad_normed, normed, inv_root, gain):
    scaled = grad_normed * gain
    return inv_root * (scaled - normed * jnp.mean(scaled * normed, axis=-1, keepdims=True))


def shards(
    tokens,
    lengths,
    parents,
    w_query,
    w_key,
    w_value,
    w_out,
    w_up,
    w_down,
    gain_attn,
    gain_ff,
    query_scale,
    bias_query,
    bias_value,
    bias_out,
    bias_up,
    bias_down,
    cotangent,
):
    local_rows, model_width = tokens.shape
    head_count = HEADS
    head_width = HEAD_DIM
    shard_index = lax.axis_index("shard")
    seg_ends, ancestry = tree_tables(lengths[0], parents[0])
    query_pos = shard_index * local_rows + jnp.arange(local_rows, dtype=jnp.int32)
    query_reach = jnp.dot(segment_onehot(query_pos, seg_ends), ancestry)
    full_query, full_key, full_value, full_out, full_up, full_down = (
        lax.all_gather(w_query, "shard", axis=0, tiled=True),
        lax.all_gather(w_key, "shard", axis=0, tiled=True),
        lax.all_gather(w_value, "shard", axis=0, tiled=True),
        lax.all_gather(w_out, "shard", axis=0, tiled=True),
        lax.all_gather(w_up, "shard", axis=0, tiled=True),
        lax.all_gather(w_down, "shard", axis=0, tiled=True),
    )
    inputs = tokens.astype(jnp.float32)
    inv_attn = lax.rsqrt(jnp.mean(inputs * inputs, axis=-1, keepdims=True) + norm_eps)
    normed_attn = inputs * inv_attn
    attn_in = (normed_attn * gain_attn).astype(jnp.bfloat16)
    query_gain = query_base * jax.nn.softplus(query_scale) / math.sqrt(head_width)
    query_pre = (
        jnp.dot(attn_in, full_query, preferred_element_type=jnp.float32) + bias_query
    ).reshape(local_rows, head_count, head_width)
    queries = (query_pre * query_gain).astype(jnp.bfloat16)
    key_rows = jnp.dot(attn_in, full_key, preferred_element_type=jnp.float32).astype(jnp.bfloat16)
    value_rows = (
        jnp.dot(attn_in, full_value, preferred_element_type=jnp.float32) + bias_value
    ).astype(jnp.bfloat16)
    start_state = (
        jnp.full((head_count, local_rows), masked_score, jnp.float32),
        jnp.zeros((head_count, local_rows), jnp.float32),
        jnp.zeros((local_rows, head_count, head_width), jnp.float32),
    )
    running = start_state
    piece_keys = lax.all_gather(key_rows, "shard", axis=0, tiled=True)
    piece_values = lax.all_gather(value_rows, "shard", axis=0, tiled=True)
    piece_rows = piece_keys.shape[0]
    block_size = math.gcd(piece_rows, 512)
    block_count = piece_rows // block_size
    key_blocks = piece_keys.reshape(block_count, block_size, head_count, head_width)
    value_blocks = piece_values.reshape(block_count, block_size, head_count, head_width)
    pos_blocks = jnp.arange(piece_rows, dtype=jnp.int32).reshape(block_count, block_size)

    def key_step(carried, block_in):
        row_max, row_sum, accumulated = carried
        block_keys, block_values, key_pos = block_in
        allowed = pair_mask(query_reach, query_pos, key_pos, seg_ends)
        scores = jnp.einsum("qhd,khd->hqk", queries, block_keys, preferred_element_type=jnp.float32)
        scores = jnp.where(allowed[None], scores, masked_score)
        new_max = jnp.maximum(row_max, jnp.max(scores, axis=2))
        decay = jnp.exp(row_max - new_max)
        exponent = jnp.where(allowed[None], jnp.exp(scores - new_max[:, :, None]), 0.0)
        row_sum = row_sum * decay + jnp.sum(exponent, axis=2)
        accumulated = accumulated * decay.T[:, :, None] + jnp.einsum(
            "hqk,khd->qhd",
            exponent.astype(jnp.bfloat16),
            block_values,
            preferred_element_type=jnp.float32,
        )
        return ((new_max, row_sum, accumulated), None)

    running, unused = lax.scan(key_step, running, (key_blocks, value_blocks, pos_blocks))
    row_max, row_sum, accumulated = running
    mixed_rows = accumulated / row_sum.T[:, :, None]
    log_total = row_max + jnp.log(row_sum)
    attn_rows = mixed_rows.reshape(local_rows, model_width).astype(jnp.bfloat16)
    middle = inputs + jnp.dot(attn_rows, full_out, preferred_element_type=jnp.float32) + bias_out
    inv_ff = lax.rsqrt(jnp.mean(middle * middle, axis=-1, keepdims=True) + norm_eps)
    normed_ff = middle * inv_ff
    ff_in = (normed_ff * gain_ff).astype(jnp.bfloat16)
    up_pre = jnp.dot(ff_in, full_up, preferred_element_type=jnp.float32) + bias_up
    hidden = jax.nn.silu(up_pre).astype(jnp.bfloat16)
    output = middle + jnp.dot(hidden, full_down, preferred_element_type=jnp.float32) + bias_down
    back_out = cotangent.astype(jnp.float32)
    hidden_grad = jnp.einsum("tm,fm->tf", cotangent, full_down, preferred_element_type=jnp.float32)
    up_sigmoid = jax.nn.sigmoid(up_pre)
    up_grad = (hidden_grad * up_sigmoid * (1.0 + up_pre * (1.0 - up_sigmoid))).astype(jnp.bfloat16)
    ff_grad = jnp.einsum("tf,mf->tm", up_grad, full_up, preferred_element_type=jnp.float32)
    grad_gain_ff = jnp.sum(ff_grad * normed_ff, axis=0)
    middle_grad = back_out + norm_back(ff_grad, normed_ff, inv_ff, gain_ff)
    out_grad = middle_grad.astype(jnp.bfloat16)
    mixed_grad = jnp.einsum(
        "tm,em->te", out_grad, full_out, preferred_element_type=jnp.float32
    ).astype(jnp.bfloat16)
    mixed_grad = mixed_grad.reshape(local_rows, head_count, head_width)
    row_delta = jnp.sum(mixed_grad.astype(jnp.float32) * mixed_rows, axis=2).T
    whole_keys, whole_values = (
        lax.all_gather(key_rows, "shard", axis=0, tiled=True),
        lax.all_gather(value_rows, "shard", axis=0, tiled=True),
    )
    tree_rows = whole_keys.shape[0]
    block_size = min(512, tree_rows)
    block_count = tree_rows // block_size
    key_blocks = whole_keys.reshape(block_count, block_size, head_count, head_width)
    value_blocks = whole_values.reshape(block_count, block_size, head_count, head_width)
    pos_blocks = jnp.arange(tree_rows, dtype=jnp.int32).reshape(block_count, block_size)

    def back_step(query_sum, block_in):
        block_keys, block_values, key_pos = block_in
        query_term, key_term, value_term = block_grads(
            queries,
            mixed_grad,
            log_total,
            row_delta,
            query_reach,
            query_pos,
            block_keys,
            block_values,
            key_pos,
            seg_ends,
        )
        return (query_sum + query_term, (key_term, value_term))

    query_grad, (key_terms, value_terms) = lax.scan(
        back_step,
        jnp.zeros((local_rows, head_count, head_width), jnp.float32),
        (key_blocks, value_blocks, pos_blocks),
    )
    key_grad, value_grad = (
        lax.psum_scatter(
            key_terms.reshape(tree_rows, model_width).astype(jnp.bfloat16),
            "shard",
            scatter_dimension=0,
            tiled=True,
        ).astype(jnp.float32),
        lax.psum_scatter(
            value_terms.reshape(tree_rows, model_width).astype(jnp.bfloat16),
            "shard",
            scatter_dimension=0,
            tiled=True,
        ).astype(jnp.float32),
    )
    key_grad = key_grad.astype(jnp.bfloat16)
    value_grad = value_grad.astype(jnp.bfloat16)
    qpre_grad = (query_grad * query_gain).reshape(local_rows, model_width).astype(jnp.bfloat16)
    scale_terms = jnp.sum(query_grad * query_pre, axis=(0, 1))
    grad_query_scale = (
        scale_terms * query_base * jax.nn.sigmoid(query_scale) / math.sqrt(head_width)
    )
    attn_grad = jnp.einsum("te,me->tm", qpre_grad, full_query, preferred_element_type=jnp.float32)
    attn_grad = attn_grad + jnp.einsum(
        "te,me->tm", key_grad, full_key, preferred_element_type=jnp.float32
    )
    attn_grad = attn_grad + jnp.einsum(
        "te,me->tm", value_grad, full_value, preferred_element_type=jnp.float32
    )
    grad_gain_attn = jnp.sum(attn_grad * normed_attn, axis=0)
    grad_tokens = (middle_grad + norm_back(attn_grad, normed_attn, inv_attn, gain_attn)).astype(
        jnp.bfloat16
    )
    projection_grads = jnp.concatenate([qpre_grad, key_grad, value_grad], axis=1)
    pairings = (
        (attn_in, projection_grads),
        (attn_rows, out_grad),
        (ff_in, up_grad),
        (hidden, cotangent),
    )
    pieces = []
    for left_rows, right_rows in pairings:
        pieces.append(
            lax.dot_general(
                left_rows, right_rows, (((0,), (0,)), ((), ())), preferred_element_type=jnp.float32
            )
        )
    owned = lax.psum_scatter(
        jnp.concatenate(pieces, axis=1).astype(jnp.bfloat16),
        "shard",
        scatter_dimension=0,
        tiled=True,
    )
    summed = lax.psum(owned, "rep").astype(jnp.float32)
    small_grads = lax.psum(
        (
            grad_gain_attn,
            grad_gain_ff,
            grad_query_scale,
            jnp.sum(qpre_grad.astype(jnp.float32), axis=0),
            jnp.sum(value_grad.astype(jnp.float32), axis=0),
            jnp.sum(out_grad.astype(jnp.float32), axis=0),
            jnp.sum(up_grad.astype(jnp.float32), axis=0),
            jnp.sum(back_out, axis=0),
        ),
        ("rep", "shard"),
    )
    ff_width = w_up.shape[1]
    up_start = 4 * model_width
    down_start = up_start + ff_width
    return (
        output.astype(jnp.bfloat16),
        grad_tokens,
        summed[:, 0:model_width],
        summed[:, model_width : 2 * model_width],
        summed[:, 2 * model_width : 3 * model_width],
        summed[:, 3 * model_width : up_start],
        summed[:, up_start:down_start],
        summed[:, down_start : down_start + model_width],
        small_grads[0],
        small_grads[1],
        small_grads[2],
        small_grads[3],
        small_grads[4],
        small_grads[5],
        small_grads[6],
        small_grads[7],
    )


def solution(mesh):
    in_specs = (
        P(("rep", "shard"), None),
        P("rep", None),
        P("rep", None),
        P("shard", None),
        P("shard", None),
        P("shard", None),
        P("shard", None),
        P("shard", None),
        P("shard", None),
        P(),
        P(),
        P(),
        P(),
        P(),
        P(),
        P(),
        P(),
        P(("rep", "shard"), None),
    )
    out_specs = (
        P(("rep", "shard"), None),
        P(("rep", "shard"), None),
        P("shard", None),
        P("shard", None),
        P("shard", None),
        P("shard", None),
        P("shard", None),
        P("shard", None),
        P(),
        P(),
        P(),
        P(),
        P(),
        P(),
        P(),
        P(),
    )
    return jax.shard_map(shards, mesh=mesh, in_specs=in_specs, out_specs=out_specs, check_vma=False)
```

profile of v0, /device:TPU:1, one launch (start us, length us, event | category | flops | bytes accessed | tf_op | source)
XLA Modules:
  0.0 1295.1 jit_solution(16172364816454611549)
XLA Ops:
  9.7 63.7 %all-gather.9.cloned.1.call-done = bf16[1280,1280]{1,0:T(8,128)(2,1)} async-done(((bf16[160,1280]{1,0:T(8,128)(2,1)}), bf16[1280,1280]{1,0:T(8,128)(2,1)}) %all-gather.9.cloned.1.call-update) | async-done | bytes 3276816 | tf_op jit(solution)/shard_map/all_gather | solution.py:102
  73.4 3.8 convolution_convert_fusion.5
  77.3 58.9 %all-gather.15.cloned.1.call-done = bf16[1280,1280]{1,0:T(8,128)(2,1)} async-done(((bf16[160,1280]{1,0:T(8,128)(2,1)}), bf16[1280,1280]{1,0:T(8,128)(2,1)}) %all-gather.15.cloned.1.call-update) | async-done | bytes 3276816 | tf_op jit(solution)/shard_map/all_gather | solution.py:103
  136.2 3.8 fusion.58
  144.9 54.1 %all-gather.13.cloned.1.call-done = bf16[1280,1280]{1,0:T(8,128)(2,1)} async-done(((bf16[160,1280]{1,0:T(8,128)(2,1)}), bf16[1280,1280]{1,0:T(8,128)(2,1)}) %all-gather.13.cloned.1.call-update) | async-done | bytes 3276816 | tf_op jit(solution)/shard_map/all_gather | solution.py:101
  199.1 4.1 convolution_add_fusion.6
  205.0 81.5 %all-gather.11.cloned.1.call-done = bf16[2048,1280]{1,0:T(8,128)(2,1)} async-done(((bf16[256,1280]{1,0:T(8,128)(2,1)}), bf16[2048,1280]{1,0:T(8,128)(2,1)}) %all-gather.11.cloned.1.call-update) | async-done | bytes 5242896 | tf_op jit(solution)/shard_map/all_gather | solution.py:127
  286.6 15.8 %reshape.160 = bf16[4,512,16,80]{3,2,1,0:T(8,128)(2,1)} reshape(bf16[2048,1280]{1,0:T(8,128)(2,1)} %all-gather.11.cloned.1.call-done) | data formatting | bytes 10485760 | tf_op jit(solution)/shard_map/reshape | solution.py:132
  302.4 13.2 %copy.73 = bf16[4,512,16,80]{1,3,2,0:T(8,128)(2,1)} copy(bf16[4,512,16,80]{3,2,1,0:T(8,128)(2,1)} %reshape.160) | data formatting | bytes 10485760
  315.6 58.0 %all-gather.17.cloned.1.call-done = bf16[2048,1280]{1,0:T(8,128)(2,1)} async-done(((bf16[256,1280]{1,0:T(8,128)(2,1)}), bf16[2048,1280]{1,0:T(8,128)(2,1)}) %all-gather.17.cloned.1.call-update) | async-done | bytes 5242896 | tf_op jit(solution)/shard_map/all_gather | solution.py:128
  373.6 15.8 %reshape.161 = bf16[4,512,16,80]{3,2,1,0:T(8,128)(2,1)} reshape(bf16[2048,1280]{1,0:T(8,128)(2,1)} %all-gather.17.cloned.1.call-done) | data formatting | bytes 10485760 | tf_op jit(solution)/shard_map/reshape | solution.py:133
  389.4 13.3 %copy.74 = bf16[4,512,16,80]{1,3,2,0:T(8,128)(2,1)} copy(bf16[4,512,16,80]{3,2,1,0:T(8,128)(2,1)} %reshape.161) | data formatting | bytes 10485760
  402.7 63.5 %while.30 = (s32[]{:T(128)}, f32[16,256]{1,0:T(8,128)S(1)}, f32[16,256]{1,0:T(8,128)S(1)}, f32[256,16,80]{0,2,1:T(8,128)S(1)}, s32[4,512]{1,0:T(4,128)S(1)}, /*i...) while((s32[]{:T(128)}, f32[16,256]{1,0:T(8,128)S(1)}, ...), condition=%wide.region_7.8_spmd.clone, body=%wide.region_3.7_spmd.clone.sunk | while | flops 696895232 | bytes 65426160 | solution.py:154
  403.1 5.9 fusion.234
  409.1 5.2 fusion.236
  418.8 5.9 fusion.234
  424.8 5.4 fusion.236
  434.6 5.9 fusion.234
  440.5 5.2 fusion.236
  450.5 5.9 fusion.234
  456.5 5.2 fusion.236
  467.3 4.8 multiply_reduce_fusion.4
  472.1 26.5 %all-gather.21.cloned.1.call-done = bf16[1280,1280]{1,0:T(8,128)(2,1)} async-done(((bf16[160,1280]{1,0:T(8,128)(2,1)}), bf16[1280,1280]{1,0:T(8,128)(2,1)}) %all-gather.21.cloned.1.call-update) | async-done | bytes 3276816 | tf_op jit(solution)/shard_map/all_gather | solution.py:105
  498.6 4.4 convolution_add_fusion.3
  503.1 58.3 %all-gather.23.cloned.1.call-done = bf16[1280,1280]{1,0:T(8,128)(2,1)} async-done(((bf16[160,1280]{1,0:T(8,128)(2,1)}), bf16[1280,1280]{1,0:T(8,128)(2,1)}) %all-gather.23.cloned.1.call-update) | async-done | bytes 3276816 | tf_op jit(solution)/shard_map/all_gather | solution.py:106
  561.4 3.8 convert_reduce_fusion.3
  571.7 84.6 %while.31 = (s32[]{:T(128)}, f32[256,16,80]{0,2,1:T(8,128)S(1)}, bf16[4,512,16,80]{1,3,2,0:T(8,128)(2,1)}, bf16[4,512,16,80]{1,3,2,0:T(8,128)(2,1)}, bf16[4,512,...) while((s32[]{:T(128)}, f32[256,16,80]{0,2,1:T(8,128)S(1)}, ...), condition=%wide.region_13.14_spmd.clone, body=%wide.region_11.13_spmd.clone.sunk | while | flops 1698981632 | bytes 119739176 | solution.py:206
  575.0 6.8 fusion.252
  585.4 5.1 bitcast_dynamic-update-slice_fusion.4
  596.1 6.8 fusion.252
  606.5 5.1 bitcast_dynamic-update-slice_fusion.4
  617.1 6.8 fusion.252
  627.5 5.1 bitcast_dynamic-update-slice_fusion.4
  638.1 6.8 fusion.252
  648.5 5.1 bitcast_dynamic-update-slice_fusion.4
  656.3 6.9 copy.78
  663.2 4.5 copy.94
  668.1 6.9 copy.79
  675.0 4.6 copy.95
  690.0 80.3 %reduce-scatter.4.cloned.1.call-done = bf16[256,1280]{0,1:T(8,128)(2,1)} async-done(((bf16[2048,1280]{0,1:T(8,128)(2,1)}), bf16[256,1280]{0,1:T(8,128)(2,1)}) %reduce-scatter.4.cloned.1.call-update) | async-done | bytes 655376 | tf_op jit(solution)/shard_map/reduce_scatter | solution.py:212
  770.3 106.4 %reduce-scatter.6.cloned.1.call-done = bf16[256,1280]{0,1:T(8,128)(2,1)} async-done(((bf16[2048,1280]{0,1:T(8,128)(2,1)}), bf16[256,1280]{0,1:T(8,128)(2,1)}) %reduce-scatter.6.cloned.1.call-update) | async-done | bytes 655376 | tf_op jit(solution)/shard_map/reduce_scatter | solution.py:218
  876.7 8.3 convolution_convert_fusion
  885.0 14.8 %pad_maximum_fusion = bf16[1280,7680]{1,0:T(8,128)(2,1)} fusion(bf16[1280,1280]{1,0:T(8,128)(2,1)} %convolution_convert_fusion.1, bf16[1280,1280]{1,0:T(8,128)(2,1)} %convolution_convert_fusion.2, bf16[1280,1280]{1,0:T(8,128)(2,1)S(1)} %convolution_convert_fusion.3, bf16[1280,3840]{1,0:T(8,128)(2,1)} %convolution_convert_fusion), kind=kLoop, calls=%fused_computation.65 | loop fusion | flops 78643200 | bytes 39321600 | tf_op jit(solution)/shard_map/concatenate | solution.py:258
  909.1 314.9 %reduce-scatter.8.cloned.1.call-done = bf16[160,7680]{1,0:T(8,128)(2,1)} async-done(((bf16[1280,7680]{1,0:T(8,128)(2,1)}), bf16[160,7680]{1,0:T(8,128)(2,1)}) %reduce-scatter.8.cloned.1.call-update) | async-done | bytes 2457616 | tf_op jit(solution)/shard_map/reduce_scatter | solution.py:257
  1224.1 3.9 fusion.75
  1228.0 41.4 %all-reduce = (f32[1280]{0:T(1024)}, f32[1280]{0:T(1024)}, f32[80]{0:T(128)}, f32[1280]{0:T(1024)}, f32[1280]{0:T(1024)}, /*index=5*/f32[1280]{0:T(1024)}, f32[1280]{0:T(1024)}, f32[1280]{0:T(1024)}) all-reduce(f32[1280]{0:T(1024)S(1)} %get-tuple-element.319, ...), channel_id=1, replica_groups=mesh['rep'=4,'shard'=8] {'rep','shard'}, use_global_device_ids=true, to_apply=%region_20.21 | all-reduce | flops 9040 | bytes 72320 | tf_op jit(solution)/shard_map/psum | solution.py:264
  1270.6 13.2 %all-reduce.3.cloned.1.call-done = bf16[160,7680]{1,0:T(8,128)(2,1)} async-done(((bf16[160,7680]{1,0:T(8,128)(2,1)}), bf16[160,7680]{1,0:T(8,128)(2,1)}) %all-reduce.3.cloned.1.call-update) | async-done | bytes 2457616 | tf_op jit(solution)/shard_map/psum | solution.py:263
  1283.8 3.9 fusion.166
  (237 shorter events, 92.5 us)
Async XLA Ops:
  7.2 66.2 %copy-start.25 = (f32[1280]{0:T(1024)S(1)}, f32[1280]{0:T(1024)}, u32[]{:S(2)}) copy-start(f32[1280]{0:T(1024)} %param.31) | copy-start | bytes 15364
  7.2 66.2 %all-gather.9.cloned.1.call-start = ((), (), s32[]{:S(2)}) async-start(), calls=%async_computation.3 | async-start | bytes 3686400 | tf_op jit(solution)/shard_map/all_gather | solution.py:102
  7.9 128.3 %all-gather.15.cloned.1.call-start = ((), (), s32[]{:S(2)}) async-start(), calls=%async_computation.6 | async-start | bytes 3686400 | tf_op jit(solution)/shard_map/all_gather | solution.py:103
  8.7 190.4 %all-gather.13.cloned.1.call-start = ((), (), s32[]{:S(2)}) async-start(), calls=%async_computation.5 | async-start | bytes 3686400 | tf_op jit(solution)/shard_map/all_gather | solution.py:101
  9.4 277.1 %all-gather.11.cloned.1.call-start = ((), (), s32[]{:S(2)}) async-start(), calls=%async_computation.4 | async-start | bytes 5898240 | tf_op jit(solution)/shard_map/all_gather | solution.py:127
  9.7 189.4 %copy-start.27 = (f32[256]{0:T(256)}, f32[256]{0:T(256)S(1)}, u32[]{:S(2)}) copy-start(f32[256]{0:T(256)S(1)} %add_rsqrt_fusion.1) | copy-start | bytes 3076
  9.7 126.5 %copy-start.34 = (f32[1280]{0:T(1024)S(1)}, f32[1280]{0:T(1024)}, u32[]{:S(2)}) copy-start(f32[1280]{0:T(1024)} %param.35) | copy-start | bytes 15364
  77.3 296.4 %all-gather.17.cloned.1.call-start = ((), (), s32[]{:S(2)}) async-start(), calls=%async_computation.7 | async-start | bytes 5898240 | tf_op jit(solution)/shard_map/all_gather | solution.py:128
  140.1 4.3 copy-start.41
  140.1 327.2 %all-gather.19.cloned.1.call-start = ((), (), s32[]{:S(2)}) async-start(), calls=%async_computation.8 | async-start | bytes 3686400 | tf_op jit(solution)/shard_map/all_gather | solution.py:104
  140.7 58.4 %copy-start.35 = (f32[1280]{0:T(1024)S(1)}, f32[1280]{0:T(1024)}, u32[]{:S(2)}) copy-start(f32[1280]{0:T(1024)} %param.34) | copy-start | bytes 15364
  140.7 358.0 %all-gather.21.cloned.1.call-start = ((), (), s32[]{:S(2)}) async-start(), calls=%async_computation.9 | async-start | bytes 3686400 | tf_op jit(solution)/shard_map/all_gather | solution.py:105
  141.4 420.0 %all-gather.23.cloned.1.call-start = ((), (), s32[]{:S(2)}) async-start(), calls=%async_computation.10 | async-start | bytes 3686400 | tf_op jit(solution)/shard_map/all_gather | solution.py:106
  142.2 628.1 %reduce-scatter.4.cloned.1.call-start = ((), (), s32[]{:S(2)}) async-start(), calls=%async_computation.11 | async-start | bytes 5898240 | tf_op jit(solution)/shard_map/reduce_scatter | solution.py:212
  144.4 60.4 %copy-start.29 = (f32[80]{0:T(128)}, f32[80]{0:T(128)S(1)}, u32[]{:S(2)}) copy-start(f32[80]{0:T(128)S(1)} %fusion.150) | copy-start | bytes 964
  204.9 97.5 %copy-start.3 = (f32[256,1280]{0,1:T(8,128)}, f32[256,1280]{0,1:T(8,128)S(1)}, u32[]{:S(2)}) copy-start(f32[256,1280]{0,1:T(8,128)S(1)} %copy.71) | copy-start | bytes 3932164
  389.4 13.3 %copy-start.8 = (f32[256,16,80]{0,2,1:T(8,128)S(1)}, f32[256,16,80]{0,2,1:T(8,128)}, u32[]{:S(2)}) copy-start(f32[256,16,80]{0,2,1:T(8,128)} %custom-call.2) | copy-start | bytes 3932164
  409.1 5.8 copy-start.2
  424.7 5.9 copy-start.2
  440.5 6.0 copy-start.2
  456.5 5.8 copy-start.2
  466.2 5.9 copy-start.9
  467.3 31.3 %copy-start.24 = (f32[1280]{0:T(1024)S(1)}, f32[1280]{0:T(1024)}, u32[]{:S(2)}) copy-start(f32[1280]{0:T(1024)} %param.32) | copy-start | bytes 15364
  467.3 31.3 %copy-start.37 = (f32[1280]{0:T(1024)S(1)}, f32[1280]{0:T(1024)}, u32[]{:S(2)}) copy-start(f32[1280]{0:T(1024)} %param.37) | copy-start | bytes 15364
  503.1 62.1 %copy-start.10 = (f32[256,1280]{1,0:T(8,128)S(1)}, f32[256,1280]{1,0:T(8,128)}, u32[]{:S(2)}) copy-start(f32[256,1280]{1,0:T(8,128)} %get-tuple-element.396) | copy-start | bytes 3932164
  561.4 3.8 copy-start.33
  574.6 7.2 copy-start
  581.8 8.7 copy-start.1
  595.7 7.2 copy-start
  602.9 8.7 copy-start.1
  616.7 7.2 copy-start
  623.9 8.7 copy-start.1
  637.7 7.2 copy-start
  644.9 8.7 copy-start.1
  667.8 208.9 %reduce-scatter.6.cloned.1.call-start = ((), (), s32[]{:S(2)}) async-start(), calls=%async_computation.12 | async-start | bytes 5898240 | tf_op jit(solution)/shard_map/reduce_scatter | solution.py:218
  679.6 544.4 %reduce-scatter.8.cloned.1.call-start = ((), (), s32[]{:S(2)}) async-start(), calls=%async_computation.13 | async-start | bytes 22118400 | tf_op jit(solution)/shard_map/reduce_scatter | solution.py:257
  684.1 2.8 copy-start.21
  684.1 2.8 copy-start.43
  687.0 189.7 %copy-start.26 = (f32[1280]{0:T(1024)S(1)}, f32[1280]{0:T(1024)}, u32[]{:S(2)}) copy-start(f32[1280]{0:T(1024)} %param.31) | copy-start | bytes 15364
  687.0 189.7 %copy-start.28 = (f32[256]{0:T(256)S(1)}, f32[256]{0:T(256)}, u32[]{:S(2)}) copy-start(f32[256]{0:T(256)} %copy-done.27) | copy-start | bytes 3076
  899.8 4.3 copy-start.44
  899.9 384.0 %all-reduce.3.cloned.1.call-start = ((), (), s32[]{:S(2)}) async-start(), calls=%async_computation.14 | async-start | bytes 4915200 | tf_op jit(solution)/shard_map/psum | solution.py:263
  900.9 3.2 copy-start.12
  900.9 3.4 copy-start.31
  900.9 3.4 copy-start.38
  904.3 2.5 copy-start.17
  909.1 315.0 %copy-start.16 = (bf16[256,1280]{1,0:T(8,128)(2,1)S(1)}, bf16[256,1280]{1,0:T(8,128)(2,1)}, u32[]{:S(2)}) copy-start(bf16[256,1280]{1,0:T(8,128)(2,1)} %param.22) | copy-start | bytes 1966084
  1224.0 45.4 %copy-start.7 = (f32[256,1280]{1,0:T(8,128)S(1)}, f32[256,1280]{1,0:T(8,128)}, u32[]{:S(2)}) copy-start(f32[256,1280]{1,0:T(8,128)} %copy-done.5) | copy-start | bytes 3932164
  (18 other events, 29.1 us)
Sparse Core Ops, SparseCore 0:
  10.2 63.1 all-gather.8
  75.6 60.5 all-gather.14
  138.4 60.6 all-gather.12
  201.7 84.8 all-gather.10
  289.2 84.4 all-gather.16
  375.7 60.1 all-gather.18
  438.1 60.5 all-gather.20
  500.8 60.5 all-gather.22
  667.9 102.3 reduce-scatter.3
  773.7 102.9 reduce-scatter.5
  900.0 323.9 reduce-scatter.7
  1226.3 57.5 all-reduce.2
where the time goes:
time: 1310 us; the launch traced here: 1300 us
  waiting for transfers between devices  920 us (70%)
  matrix products  178 us (14%)
  local copies, waits for them, and re-layouts  94.8 us (7%)
  other arithmetic  43.2 us (3%)
  blocking collectives  41.4 us (3%)
  between operations  15.1 us (1%)
    reduce_scatter x1, waiting for transfers between devices, shards(): lax.psum_scatter(jnp.concatenate(pieces, axis=1).astype(jnp.bfloat16), 's...  315 us
    reduce_scatter x1, waiting for transfers between devices, shards(): lax.psum_scatter(value_terms.reshape(tree_rows, model_width).astype(jnp.b...  106 us
    all_gather x1, waiting for transfers between devices, shards(): piece_keys = lax.all_gather(key_rows, 'shard', axis=0, tiled=True)  81.5 us
    reduce_scatter x1, waiting for transfers between devices, shards(): lax.psum_scatter(key_terms.reshape(tree_rows, model_width).astype(jnp.bfl...  80.3 us
    all_gather x1, waiting for transfers between devices, shards(): lax.all_gather(w_key, 'shard', axis=0, tiled=True)  63.7 us
    all_gather x1, waiting for transfers between devices, shards(): lax.all_gather(w_value, 'shard', axis=0, tiled=True)  58.9 us
    all_gather x1, waiting for transfers between devices, shards(): lax.all_gather(w_down, 'shard', axis=0, tiled=True)  58.3 us
    all_gather x1, waiting for transfers between devices, shards(): piece_values = lax.all_gather(value_rows, 'shard', axis=0, tiled=True)  58 us
  transfers between devices with their start and end apart: 12, of which 11 were waited for; matrix products, arithmetic and copies ran while one was open for 14% of the time, Pallas kernels for 0%

commit v1 on v0

v1 whole, which is shorter than its diff:
```python
import functools
import math

import jax
import jax.numpy as jnp
from jax import lax
from jax.experimental import pallas as pl
from jax.experimental.pallas import tpu as pltpu
from jax.sharding import PartitionSpec as P

HEADS = 16
HEAD_DIM = 80
MESH = pl.DeviceIdType.MESH
F32 = jnp.float32
BF16 = jnp.bfloat16

norm_eps = 1e-06
query_base = 1.442695
masked_score = -1e30
LABELS = 16
COPIES = 700
VMEM_BYTES = 64 << 20


def dot(left, right):
    return jnp.dot(left, right, preferred_element_type=F32)


def dot_nt(left, right):
    return lax.dot_general(left, right, (((1,), (1,)), ((), ())), preferred_element_type=F32)


def when(condition, body):
    if condition is True:
        body()
    elif condition is not False:
        pl.when(condition)(body)


class Copy:
    def __init__(self, make, sends, receives):
        self.make, self.sends, self.receives = make, sends, receives

    def start(self):
        when(self.sends, lambda: self.make().start())

    def arrived(self):
        when(self.receives, lambda: self.make().wait_recv())

    def sent(self):
        when(self.sends, lambda: self.make().wait_send())


class Links:
    def __init__(self, send_sems, recv_sems):
        self.send_sems, self.recv_sems, self.used, self.copies = send_sems, recv_sems, 0, []

    def block(self, count):
        first = self.used
        self.used += count
        assert self.used <= COPIES
        return first

    def copy(self, src, dst, device, sends=True, receives=True, index=None, keep=True):
        if index is None:
            index = self.block(1)

        def make():
            return pltpu.make_async_remote_copy(
                src_ref=src,
                dst_ref=dst,
                send_sem=self.send_sems.at[index],
                recv_sem=self.recv_sems.at[index],
                device_id=device,
                device_id_type=MESH,
            )

        made = Copy(make, sends, receives)
        if keep:
            self.copies.append(made)
        return made


def layer_kernel(dims, refs):
    R, S, L, D = dims["R"], dims["S"], dims["L"], dims["D"]
    HG, E, CW, SR, H, SRH = (dims[k] for k in ("HG", "E", "CW", "SR", "H", "SRH"))
    q, U, A, T = S // R, R // 2, R, S * L
    HD = HEAD_DIM
    HALF, DH = L // 2, D // 2
    W = 256
    NW = D // W
    ref = refs
    r, s = lax.axis_index("rep"), lax.axis_index("shard")
    u, c, a, b = r // 2, r % 2, s // q, s % q

    def rho(i):
        return (i % 2) * (R // 2) + i // 2

    def rho_back(j):
        return (j % (R // 2)) * 2 + j // (R // 2)

    def device(r2, a2, b2):
        return (r2, a2 * q + b2)

    def peer(u2, c2, b2):
        return device(u2 * 2 + c2, a, b2)

    def block_of(u2, c2, b2):
        return rho(u2 * 2 + c2) * q + b2

    def rows_of(blk):
        return pl.ds(pl.multiple_of(blk * L, L), L)

    g = r * q + b
    blk = block_of(u, c, b)
    u_off = [(u + d) % U for d in range(U)]
    b_off = [(b + d) % q for d in range(q)]
    u_from = [(u + U - d) % U for d in range(U)]
    b_from = [(b + q - d) % q for d in range(q)]
    home_r, home_a = rho_back(a), rho(r)
    home = device(home_r, home_a, b)
    stays = jnp.logical_and(home_r == r, home_a == a)
    moves = jnp.logical_not(stays)
    sibling = peer(u, 1 - c, b)
    above = device(r, jnp.minimum(a + 1, A - 1), b)
    below = device(r, jnp.maximum(a - 1, 0), b)
    own_half = pl.ds(pl.multiple_of(c * DH, 128), DH)
    other_half = pl.ds(pl.multiple_of((1 - c) * DH, 128), DH)

    links = Links(ref["send_sems"], ref["recv_sems"])

    barrier = pltpu.get_barrier_semaphore()

    def greet(where):
        pl.semaphore_signal(barrier, inc=1, device_id=where, device_id_type=MESH)

    for k in range(1, S):
        g2 = (g + k) % S
        greet(device(g2 // q, a, g2 % q))
    for k in range(1, A):
        greet(device(r, (a + k) % A, b))
    pl.when(moves)(lambda: greet(home))
    pl.semaphore_wait(barrier, S - 1 + A - 1 + jnp.where(moves, 1, 0))

    swaps = []
    for name, there in (("tokens", "tok"), ("tab", "tabs"), ("cotangent", "cot")):
        swaps.append(links.copy(ref[name], ref[there], home, moves, moves))

    local_sems = ref["local_sems"]

    def local(src, dst, n):
        return pltpu.make_async_copy(src, dst, local_sems.at[n])

    def keep_rows():
        kept = [
            local(ref["tokens"], ref["tok"], 0),
            local(ref["tab"], ref["tabs"], 1),
            local(ref["cotangent"], ref["cot"], 2),
        ]
        for copy in kept:
            copy.start()
        for copy in kept:
            copy.wait()

    swaps[0].start()
    swaps[1].start()

    wq, wqt, wcat = ref["wq"], ref["wqt"], ref["wcat"]

    def wq_rows(a2, b2):
        return pl.ds(pl.multiple_of((a2 * q + b2) * SR, 16), SR)

    def near(src, name, n):
        if dims["fits"]:
            return src
        copy = local(src, ref[name], n)
        copy.start()
        copy.wait()
        return ref[name]

    own_wq = local(wcat.at[g], wq.at[wq_rows(a, b)], 3)
    own_wq.start()
    wcat_b = {}
    for db in range(1, q):
        wcat_b[db] = links.copy(
            wcat.at[r * q + b_off[db]], wq.at[wq_rows(a, b)], device(r, a, b_off[db])
        )
        wcat_b[db].start()
    up_q, down_q = {}, {}
    for k in range(A - 1):
        for db in range(q):
            low, high = jnp.maximum(a - k, 0), jnp.minimum(a + k, A - 1)
            slot = wq_rows(low, b_from[db])
            up_q[k, db] = links.copy(
                wq.at[slot], wq.at[slot], above,
                jnp.logical_and(a - k >= 0, a < A - 1), a - 1 - k >= 0,
            )
            slot = wq_rows(high, b_from[db])
            down_q[k, db] = links.copy(
                wq.at[slot], wq.at[slot], below,
                jnp.logical_and(a + k <= A - 1, a > 0), a + 1 + k <= A - 1,
            )
    own_wq.wait()
    up_q[0, 0].start()
    down_q[0, 0].start()

    def wq_pass(k):
        for db in range(q):
            up_q[k, db].arrived()
            down_q[k, db].arrived()
            if k + 1 < A - 1:
                up_q[k + 1, db].start()
                down_q[k + 1, db].start()

    w3 = ref["w3"]
    shards = (ref["w_out"], ref["w_up"], ref["w_down"])

    def shard_rows(a2, b2):
        return pl.ds(pl.multiple_of((a2 * q + b2) * SR, 16), SR)

    def piece_rows(a2, b2, u2):
        if H == 1:
            return shard_rows(a2, b2)
        return pl.ds(pl.multiple_of((a2 * q + b2) * SR + u2 * SRH, 16), SRH)

    own_shards = [local(shards[w], w3.at[w, shard_rows(a, b)], 4 + w) for w in range(3)]
    for copy in own_shards:
        copy.start()
    for copy in own_shards:
        copy.wait()
    pl.when(stays)(keep_rows)
    up_w, down_w, side_w, own_w, core_w, core_own = {}, {}, {}, {}, {}, {}
    slots = [sign * k for k in range(1, A) for sign in (1, -1)]
    for w in range(3):
        for k in range(A - 1):
            low, high = jnp.maximum(a - k, 0), jnp.minimum(a + k, A - 1)
            at = w3.at[w, piece_rows(low, b, u), own_half]
            up_w[w, k] = links.copy(
                at, at, above, jnp.logical_and(a - k >= 0, a < A - 1), a - 1 - k >= 0
            )
            at = w3.at[w, piece_rows(high, b, u), own_half]
            down_w[w, k] = links.copy(
                at, at, below, jnp.logical_and(a + k <= A - 1, a > 0), a + 1 + k <= A - 1
            )
        for slot in slots:
            valid = a + slot <= A - 1 if slot > 0 else a + slot >= 0
            a0 = jnp.clip(a + slot, 0, A - 1)
            at = w3.at[w, piece_rows(a0, b, u), own_half]
            for db in range(1, q):
                side_w[w, slot, 0, db] = links.copy(at, at, peer(u, c, b_off[db]), valid, valid)
            if H > 1:
                for du in range(1, U):
                    side_w[w, slot, du, 0] = links.copy(at, at, peer(u_off[du], c, b), valid, valid)
                    for db in range(1, q):
                        passed = w3.at[w, piece_rows(a0, b_from[db], u), own_half]
                        side_w[w, slot, du, db] = links.copy(
                            passed, passed, peer(u_off[du], c, b), valid, valid
                        )
            at = w3.at[w, pl.ds(pl.multiple_of(a0 * q * SR, 16), q * SR), own_half]
            core_w[w, slot] = links.copy(at, at, sibling, valid, valid)
        for db in range(1, q):
            at = w3.at[w, shard_rows(a, b), own_half]
            own_w[w, db] = links.copy(at, at, peer(u, c, b_off[db]))
            at = w3.at[w, shard_rows(a, b_from[db]), own_half]
            core_own[w, db] = links.copy(at, at, sibling)

    def w3_line(w, k):
        if k < 0:
            up_w[w, 0].start()
            down_w[w, 0].start()
            for db in range(1, q):
                own_w[w, db].start()
            return
        up_w[w, k].arrived()
        down_w[w, k].arrived()
        if k + 1 < A - 1:
            up_w[w, k + 1].start()
            down_w[w, k + 1].start()
        for slot in (-(k + 1), k + 1):
            for (w2, slot2, du, db), moved in side_w.items():
                if (w2, slot2) == (w, slot) and (du == 0 or db == 0):
                    moved.start()

    def w3_side(w, k):
        if k < 0:
            for db in range(1, q):
                own_w[w, db].arrived()
                core_own[w, db].start()
            return
        for slot in (-(k + 1), k + 1):
            for db in range(1, q):
                side_w[w, slot, 0, db].arrived()
                if H > 1:
                    for du in range(1, U):
                        side_w[w, slot, du, db].start()

    def w3_core(w, k):
        for slot in (-(k + 1), k + 1):
            if H > 1:
                for du in range(1, U):
                    side_w[w, slot, du, 0].arrived()
                    for db in range(1, q):
                        side_w[w, slot, du, db].arrived()
            core_w[w, slot].start()

    def w3_whole(w):
        for db in range(1, q):
            core_own[w, db].arrived()
        for slot in slots:
            core_w[w, slot].arrived()

    tok, cot, xa = ref["tok"], ref["cot"], ref["xa"]
    gains = ref["gains"]
    gain_attn, gain_ff = gains[0:1, :], gains[1:2, :]
    STEP = 32

    def unit(x):
        return lax.rsqrt(jnp.mean(x * x, axis=-1, keepdims=True) + norm_eps)

    def half_rows(block, h):
        return pl.ds(pl.multiple_of(block * L + h * HALF, HALF), HALF)

    own_x, pass_x, sib_x = {}, {}, {}
    for h in range(2):
        at = xa.at[half_rows(blk, h)]
        for db in range(1, q):
            own_x[h, 0, db] = links.copy(at, at, peer(u, c, b_off[db]))
        for du in range(1, U):
            own_x[h, du, 0] = links.copy(at, at, peer(u_off[du], c, b))
        for du in range(1, U):
            for db in range(1, q):
                if h == 0:
                    at = xa.at[half_rows(block_of(u, c, b_from[db]), h)]
                    pass_x[h, du, db] = links.copy(at, at, peer(u_off[du], c, b))
                else:
                    at = xa.at[half_rows(block_of(u_from[du], c, b), h)]
                    pass_x[h, du, db] = links.copy(at, at, peer(u, c, b_off[db]))
        for du in range(U):
            for db in range(q):
                at = xa.at[half_rows(block_of(u_from[du], c, b_from[db]), h)]
                sib_x[h, du, db] = links.copy(at, at, sibling)

    swaps[0].arrived()
    for h in range(2):

        def norm_step(i, carried, h=h):
            here = pl.ds(pl.multiple_of(h * HALF + i * STEP, STEP), STEP)
            x = tok[here, :].astype(F32)
            there = pl.ds(pl.multiple_of(blk * L + h * HALF + i * STEP, STEP), STEP)
            row = (x * unit(x) * gain_attn).astype(BF16)
            if dims["fits"]:
                xa[there, :] = row
            else:
                ref["x_rows"][here, :] = row
            return carried

        lax.fori_loop(0, HALF // STEP, norm_step, 0)
        if not dims["fits"]:
            here = pl.ds(h * HALF, HALF)
            out_of = local(ref["x_rows"].at[here], xa.at[half_rows(blk, h)], 7)
            out_of.start()
            out_of.wait()
        for moved in [m for (h2, *_), m in own_x.items() if h2 == h]:
            moved.start()
        sib_x[h, 0, 0].start()

    for db in range(1, q):
        wcat_b[db].arrived()
        up_q[0, db].start()
        down_q[0, db].start()
    swaps[2].start()
    for w in range(3):
        w3_line(w, -1)

    swaps[1].arrived()
    lane = lax.broadcasted_iota(jnp.int32, (LABELS, 128), 1)
    row = lax.broadcasted_iota(jnp.int32, (LABELS, 128), 0)
    lengths = jnp.broadcast_to(ref["tabs"][0:1, :], (LABELS, 128))
    seg_start = jnp.sum(jnp.where(lane < row, lengths, 0.0), axis=1, keepdims=True)
    seg_end = jnp.sum(jnp.where(lane <= row, lengths, 0.0), axis=1, keepdims=True)
    lane = lax.broadcasted_iota(jnp.int32, (128, 128), 1)
    row = lax.broadcasted_iota(jnp.int32, (128, 128), 0)
    parents = jnp.broadcast_to(ref["tabs"][1:2, :], (128, 128))
    segments = dims["segments"]
    is_parent = (parents == row.astype(F32)) & (lane > 0) & (lane < segments)
    reach = jnp.where((lane == row) | is_parent, 1.0, 0.0)
    for _ in range(max(1, (segments - 1).bit_length())):
        reach = jnp.minimum(dot(reach.astype(BF16), reach.astype(BF16)), 1.0)
    blocked = ((1.0 - reach[:LABELS, :LABELS]) * masked_score).astype(BF16)

    for db in range(1, q):
        own_x[0, 0, db].arrived()
        for du in range(1, U):
            pass_x[0, du, db].start()
        sib_x[0, 0, db].start()
    for du in range(1, U):
        own_x[1, du, 0].arrived()
        for db in range(1, q):
            pass_x[1, du, db].start()
        sib_x[1, du, 0].start()
    wq_pass(0)
    for db in range(1, q):
        own_x[1, 0, db].arrived()
        sib_x[1, 0, db].start()
    for du in range(1, U):
        own_x[0, du, 0].arrived()
        sib_x[0, du, 0].start()
    for k in range(1, A - 1):
        wq_pass(k)
    for w in range(3):
        w3_side(w, -1)
    w3_line(0, 0)
    for h in range(2):
        for du in range(1, U):
            for db in range(1, q):
                pass_x[h, du, db].arrived()
                sib_x[h, du, db].start()
    w3_line(1, 0)
    w3_line(2, 0)

    def turn_wq(i, carried):
        here = pl.ds(pl.multiple_of(i * W, W), W)
        wqt[:, here] = wq[here, :].T
        return carried

    lax.fori_loop(0, NW, turn_wq, 0)
    bias_col = jnp.transpose(ref["biascat"][g])[:, 0:1]
    qgain_col = jnp.transpose(ref["qgain"][...])[:, 0:1]
    qkvf, qpre, qt, keys, kt, vals, vt = (
        ref[k] for k in ("qkvf", "qpre", "qt", "keys", "kt", "vals", "vt")
    )

    def project(k, carried):
        for j in range(S):

            def wait_rows(j=j):
                du, db, other = (j // 2) // q, (j // 2) % q, j % 2
                if other:
                    for h in range(2):
                        sib_x[h, du, db].arrived()

            pl.when(k == j)(wait_rows)
        du, db, other = (k // 2) // q, (k // 2) % q, k % 2
        block = block_of((u + U - du) % U, (c + other) % 2, (b + q - db) % q)
        cols = rows_of(block)
        x = near(xa.at[cols], "x_rows", 7)[...]
        qkvf[...] = dot_nt(wqt[...], x) + bias_col
        place = block * L + lax.broadcasted_iota(jnp.int32, (LABELS, L), 1)
        place = place.astype(F32)
        onehot = jnp.where((place >= seg_start) & (place < seg_end), 1.0, 0.0)
        far = dot(blocked, onehot.astype(BF16)).astype(BF16)
        for hd in range(HG):
            head = pl.ds(hd * HD, HD)
            pre = qkvf[head, :]
            qpre[head, cols] = pre
            qt[hd, 0:HD, cols] = (pre * qgain_col[hd * HD : (hd + 1) * HD]).astype(BF16)
            qt[hd, HD : HD + LABELS, cols] = far
            qt[hd, HD + LABELS : 128, cols] = jnp.zeros((128 - HD - LABELS, L), BF16)
            key = qkvf[pl.ds(E + hd * HD, HD), :]
            kt[hd, :, cols] = key.astype(BF16)
            wide = jnp.concatenate([key, onehot, jnp.zeros((128 - HD - LABELS, L), F32)], axis=0)
            keys[hd, cols, :] = wide.T.astype(BF16)
            value = qkvf[pl.ds(2 * E + hd * HD, HD), :]
            vt[hd, :, cols] = value.astype(BF16)
            wide = jnp.concatenate([value, jnp.zeros((128 - HD, L), F32)], axis=0)
            vals[hd, cols, :] = wide.T.astype(BF16)
        return carried

    lax.fori_loop(0, S, project, 0)

    ot, otb, lse, oa = ref["ot"], ref["otb"], ref["lse"], ref["oa"]
    first_o = links.block(S)
    diagonal = lax.broadcasted_iota(jnp.int32, (L, L), 0) <= lax.broadcasted_iota(
        jnp.int32, (L, L), 1
    )
    o_slot = pl.ds(pl.multiple_of(g * E, 16), E)

    def o_copy(block):
        r2, b2 = rho_back(block // q), block % q
        index = first_o + (r2 * q + b2 + S - g) % S
        return links.copy(
            otb.at[:, rows_of(block)], oa.at[o_slot], device(r2, a, b2), index=index, keep=False
        )

    services = {}

    def serve(at, job):
        services.setdefault(at, []).append(job)

    for k in range(A - 1):
        for w in range(3):
            at = min(S - 1, 2 * k + (w + 1) // 2)
            serve(at, functools.partial(w3_side, w, k))
            if k + 1 < A - 1:
                serve(at, functools.partial(w3_line, w, k + 1))
            serve(min(S - 1, at + 1), functools.partial(w3_core, w, k))

    def attend(i, carried):
        cols = rows_of(i)
        query = [qt[hd, :, cols] for hd in range(HG)]

        def key_block(j, state, on_diagonal):
            here = rows_of(j)
            result = []
            for hd in range(HG):
                top, total, acc = state[hd]
                score = dot(keys[hd, here, :], query[hd])
                if on_diagonal:
                    score = jnp.where(diagonal, score, masked_score)
                new_top = jnp.maximum(top, jnp.max(score, axis=0, keepdims=True))
                p = jnp.exp(score - new_top)
                fade = jnp.exp(top - new_top)
                total = total * fade + jnp.sum(p, axis=0, keepdims=True)
                acc = acc * fade + dot(vt[hd, :, here], p.astype(BF16))
                result.append((new_top, total, acc))
            return tuple(result)

        start = tuple(
            (
                jnp.full((1, L), masked_score, F32),
                jnp.zeros((1, L), F32),
                jnp.zeros((HD, L), F32),
            )
            for _ in range(HG)
        )
        state = lax.fori_loop(0, i, functools.partial(key_block, on_diagonal=False), start)
        state = key_block(i, state, True)
        for hd in range(HG):
            top, total, acc = state[hd]
            mixed = acc / total
            head = pl.ds(hd * HD, HD)
            ot[head, cols] = mixed
            otb[head, cols] = mixed.astype(BF16)
            lse[hd, :, cols] = jnp.broadcast_to(top + jnp.log(total), (8, L))

        def keep_block():
            oa[o_slot, :] = otb[:, cols]

        pl.when(i == blk)(keep_block)
        pl.when(i != blk)(lambda: o_copy(i).start())
        for j in sorted(services):

            def run(j=j):
                for job in services[j]:
                    job()

            pl.when(i == j)(run)
        return carried

    lax.fori_loop(0, S, attend, 0)

    def o_arrived(k, carried):
        links.copy(
            otb.at[:, rows_of(0)], oa.at[o_slot], sibling, index=first_o + k, keep=False
        ).make().wait_recv()
        return carried

    lax.fori_loop(1, S, o_arrived, 0)

    def o_sent(i, carried):
        pl.when(i != blk)(lambda: o_copy(i).sent())
        return carried

    otok, mid, ffin, up, hid, outb = (ref[k] for k in ("otok", "mid", "ffin", "up", "hid", "outb"))
    ug, fg, mg, og, mgt = (ref[k] for k in ("ug", "fg", "mg", "og", "mgt"))
    small = ref["small"]

    def tile(n):
        return pl.ds(pl.multiple_of(n * W, W), W)

    def turn_o(n, carried):
        otok[:, tile(n)] = oa[tile(n), :].T
        return carried

    lax.fori_loop(0, NW, turn_o, 0)
    w3_whole(0)

    def out_step(n, carried):
        added = dot(otok[...], w3[0, :, tile(n)]) + gains[2:3, tile(n)]
        mid[:, tile(n)] = tok[:, tile(n)].astype(F32) + added
        return carried

    lax.fori_loop(0, NW, out_step, 0)

    def strip(i):
        return pl.ds(pl.multiple_of(i * STEP, STEP), STEP)

    def ff_norm(i, carried):
        x = mid[strip(i), :]
        ffin[strip(i), :] = (x * unit(x) * gain_ff).astype(BF16)
        return carried

    lax.fori_loop(0, L // STEP, ff_norm, 0)
    w3_whole(1)

    def up_step(n, carried):
        pre = dot(ffin[...], w3[1, :, tile(n)]) + gains[3:4, tile(n)]
        up[:, tile(n)] = pre
        hid[:, tile(n)] = (pre * jax.nn.sigmoid(pre)).astype(BF16)
        return carried

    lax.fori_loop(0, NW, up_step, 0)
    w3_whole(2)

    def down_step(n, carried):
        added = dot(hid[...], w3[2, :, tile(n)]) + gains[4:5, tile(n)]
        outb[:, tile(n)] = (mid[:, tile(n)] + added).astype(BF16)
        return carried

    lax.fori_loop(0, NW, down_step, 0)
    back_out = links.copy(outb, ref["out"], home, moves, moves)
    back_out.start()

    def keep_out():
        ref["out"][...] = outb[...]

    pl.when(stays)(keep_out)
    swaps[2].arrived()
    small[...] = jnp.zeros_like(small)

    def up_back(n, carried):
        pre = up[:, tile(n)]
        gate = jax.nn.sigmoid(pre)
        grad = dot_nt(cot[...], w3[2, tile(n), :]) * gate * (1.0 + pre * (1.0 - gate))
        grad = grad.astype(BF16)
        ug[:, tile(n)] = grad
        small[3:4, tile(n)] = jnp.sum(grad.astype(F32), axis=0, keepdims=True)
        return carried

    lax.fori_loop(0, NW, up_back, 0)

    def ff_back(n, carried):
        fg[:, tile(n)] = dot_nt(ug[...], w3[1, tile(n), :])
        return carried

    lax.fori_loop(0, NW, ff_back, 0)

    def mid_back(i, carried):
        x, grad, above_grad = mid[strip(i), :], fg[strip(i), :], cot[strip(i), :].astype(F32)
        inverse = unit(x)
        normed = x * inverse
        small[1:2, :] += jnp.sum(grad * normed, axis=0, keepdims=True)
        scaled = grad * gain_ff
        mean = jnp.mean(scaled * normed, axis=-1, keepdims=True)
        total = above_grad + inverse * (scaled - normed * mean)
        mg[strip(i), :] = total
        rounded = total.astype(BF16)
        og[strip(i), :] = rounded
        small[2:3, :] += jnp.sum(rounded.astype(F32), axis=0, keepdims=True)
        small[4:5, :] += jnp.sum(above_grad, axis=0, keepdims=True)
        return carried

    lax.fori_loop(0, L // STEP, mid_back, 0)

    dot_t = ref["dot_t"]
    first_m = links.block(S)

    def m_copy(k):
        g2 = (g + k) % S
        at = pl.ds(pl.multiple_of(g2 * E, 16), E)
        return links.copy(
            mgt.at[at], dot_t.at[:, rows_of(blk)], device(g2 // q, a, g2 % q),
            index=first_m + k, keep=False,
        )

    def mixed_step(k, carried):
        at = pl.ds(pl.multiple_of(((g + k) % S) * E, 16), E)
        mgt[at, :] = dot_nt(w3[0, at, :], og[...]).astype(BF16)
        pl.when(k < S)(lambda: m_copy(k).start())
        return carried

    lax.fori_loop(1, S + 1, mixed_step, 0)
    dot_t[:, rows_of(blk)] = mgt[pl.ds(pl.multiple_of(g * E, 16), E), :]

    freed, freed_again = ref["freed"], ref["freed_again"]
    writers = [sibling] + [peer(u, c, v) for v in b_off[1:]] + [peer(v, c, b) for v in u_off[1:]]

    def release(sem):
        for where in writers:
            pl.semaphore_signal(sem, inc=1, device_id=where, device_id_type=MESH)

    for group in (up_w, down_w, side_w, own_w, core_w, core_own):
        for moved in group.values():
            moved.sent()
            links.copies.remove(moved)
    release(freed)

    gp, rc = ref["gp"], ref["rc"]
    rcin = [w3.at[0, :, 0:DH], w3.at[0, :, DH:D], w3.at[1, :, 0:DH]]
    core_g = [links.copy(gp.at[w], rcin[w], sibling) for w in range(3)]

    def weight_grad(w, left, right):
        if left is not None:

            def turn(n, carried):
                oa[tile(n), :] = left[:, tile(n)].T
                return carried

            lax.fori_loop(0, NW, turn, 0)

        def step(n, carried):
            here = pl.ds(pl.multiple_of(n * SR, 16), SR)
            side = oa[here, :]
            gp[w, here, :] = dot(side, right[:, other_half]).astype(BF16)
            rc[w, n // q, n % q] = dot(side, right[:, own_half]).astype(BF16)
            return carried

        lax.fori_loop(0, S, step, 0)

    weight_grad(0, None, og)
    pl.semaphore_wait(freed, len(writers))
    core_g[0].start()
    weight_grad(2, hid, cot)
    core_g[2].start()
    weight_grad(1, ffin, ug)
    core_g[1].start()

    def m_arrived(k, carried):
        m_copy(k).arrived()
        return carried

    lax.fori_loop(1, S, m_arrived, 0)

    A2 = A // 2
    u_rows = [pl.ds(pl.multiple_of(v * SRH, 16), SRH) for v in u_off]
    my_rows = u_rows[0]
    qm, um = q - 1, U - 1

    def t1b(w, db, a2):
        at = ((w * qm + db - 1) * A2 + a2) * SR
        assert at + SR <= D
        return w3.at[1, at : at + SR, DH:D]

    def t1u(w, du, a2, b2):
        at = (((w * um + du - 1) * A2 + a2) * q + b2) * SRH
        assert at + SRH <= D
        return w3.at[2, at : at + SRH, 0:DH]

    def t2b(w, db, a2):
        at = ((w * qm + db - 1) * A2 + a2) * SRH
        return w3.at[2, at : at + SRH, DH:D]

    def t2u(w, du, a2):
        at = (3 * qm * A2 + (w * um + du - 1) * A2 + a2) * SRH
        assert at + SRH <= D
        return w3.at[2, at : at + SRH, DH:D]

    first_b, first_u, second_b, second_u = {}, {}, {}, {}
    for w in range(3):
        for a2 in range(A2):
            for db in range(1, q):
                to = peer(u, c, b_off[db])
                first_b[w, db, a2] = links.copy(rc.at[w, a2, b_off[db]], t1b(w, db, a2), to)
                second_b[w, db, a2] = links.copy(
                    rc.at[w, A2 + a2, b_off[db], my_rows], t2b(w, db, a2), to
                )
            if H > 1:
                for du in range(1, U):
                    to = peer(u_off[du], c, b)
                    for b2 in range(q):
                        first_u[w, du, a2, b2] = links.copy(
                            rc.at[w, A2 + a2, b2, u_rows[du]], t1u(w, du, a2, b2), to
                        )
                    second_u[w, du, a2] = links.copy(
                        rc.at[w, a2, b, u_rows[du]], t2u(w, du, a2), to
                    )

    def add_into(target, *more):
        total = target[...].astype(F32)
        for other in more:
            total = total + other[...].astype(F32)
        target[...] = total.astype(BF16)

    def core_sum(w):
        core_g[w].arrived()

        def step(n, carried):
            a2, b2 = n // q, n % q
            here = pl.ds(pl.multiple_of(n * SR, 16), SR)
            add_into(rc.at[w, a2, b2], rcin[w].at[here])
            return carried

        lax.fori_loop(0, S, step, 0)
        for key, moved in list(first_b.items()) + list(first_u.items()):
            if key[0] == w:
                moved.start()

    def side_sum_1(w):
        for db in range(1, q):
            for a2 in range(A2):
                first_b[w, db, a2].arrived()
                add_into(rc.at[w, a2, b], t1b(w, db, a2))
        if H > 1:
            for du in range(1, U):
                for a2 in range(A2):
                    for b2 in range(q):
                        first_u[w, du, a2, b2].arrived()
                        add_into(rc.at[w, A2 + a2, b2, my_rows], t1u(w, du, a2, b2))
        for key, moved in list(second_b.items()) + list(second_u.items()):
            if key[0] == w:
                moved.start()

    def side_sum_2(w):
        for db in range(1, q):
            for a2 in range(A2):
                second_b[w, db, a2].arrived()
                add_into(rc.at[w, A2 + a2, b, my_rows], t2b(w, db, a2))
        if H > 1:
            for du in range(1, U):
                for a2 in range(A2):
                    second_u[w, du, a2].arrived()
                    add_into(rc.at[w, a2, b, my_rows], t2u(w, du, a2))

    cu = ref["cu"]
    up_g, down_g = {}, {}
    for d in range(A):
        at = rc.at[:, d, b, my_rows]
        if d > 0:
            slot = jnp.where(a + 1 == d, A, d)
            up_g[d] = links.copy(at, cu.at[slot], above, a < d, jnp.logical_and(a > 0, a <= d))
        if d < A - 1:
            down_g[d] = links.copy(
                at, cu.at[d], below, a > d, jnp.logical_and(a < A - 1, a >= d)
            )

    def line_sum(d):
        def from_below():
            up_g[d].make().wait_recv()
            slot = jnp.where(a == d, A, d)
            other = near(cu.at[slot], "c_rows", 7)
            for w in range(3):
                add_into(rc.at[w, d, b, my_rows], other.at[w])

        def from_above():
            down_g[d].make().wait_recv()
            other = near(cu.at[d], "c_rows", 7)
            for w in range(3):
                add_into(rc.at[w, d, b, my_rows], other.at[w])

        if d > 0:
            pl.when(jnp.logical_and(a > 0, a <= d))(from_below)
            up_g[d].start()
        if d < A - 1:
            pl.when(jnp.logical_and(a < A - 1, a >= d))(from_above)
            down_g[d].start()

    line_order = sorted(range(A), key=lambda d: -abs(2 * d - (A - 1)))

    delta, dqt, dqkvt = ref["delta"], ref["dqt"], ref["dqkvt"]
    for hd in range(HG):
        head = slice(hd * HD, (hd + 1) * HD)
        total = jnp.sum(dot_t[head, :].astype(F32) * ot[head, :], axis=0, keepdims=True)
        delta[hd, :, :] = jnp.broadcast_to(total, (8, T))
    dqt[...] = jnp.zeros_like(dqt)
    back_services = {}
    for w, at in ((2, 0), (1, 1), (0, 1)):
        back_services.setdefault(at, []).append(functools.partial(core_sum, w))
    for w, at in ((2, 2), (1, 3), (0, 4)):
        back_services.setdefault(min(at, S - 1), []).append(functools.partial(side_sum_1, w))
    for w, at in ((2, 4), (1, 5), (0, 6)):
        back_services.setdefault(min(at, S - 1), []).append(functools.partial(side_sum_2, w))

    def attend_back(j, carried):
        here = rows_of(j)

        def query_block(i, state, on_diagonal):
            cols = rows_of(i)
            result = []
            for hd in range(HG):
                dk, dv = state[hd]
                head = pl.ds(hd * HD, HD)
                score = dot(keys[hd, here, :], qt[hd, :, cols])
                if on_diagonal:
                    score = jnp.where(diagonal, score, masked_score)
                p = jnp.exp(score - lse[hd, 0:1, cols])
                d_out = dot_t[head, cols]
                dp = dot(vals[hd, here, 0:HD], d_out)
                ds = (p * (dp - delta[hd, 0:1, cols])).astype(BF16)
                dv = dv + dot_nt(d_out, p.astype(BF16))
                dk = dk + dot_nt(qt[hd, 0:HD, cols], ds)
                dqt[head, cols] += dot(kt[hd, :, here], ds)
                result.append((dk, dv))
            return tuple(result)

        zero = jnp.zeros((HD, L), F32)
        state = query_block(j, tuple((zero, zero) for _ in range(HG)), True)
        state = lax.fori_loop(j + 1, S, functools.partial(query_block, on_diagonal=False), state)
        for hd in range(HG):
            dk, dv = state[hd]
            dqkvt[pl.ds(E + hd * HD, HD), here] = dk.astype(BF16)
            dqkvt[pl.ds(2 * E + hd * HD, HD), here] = dv.astype(BF16)
        for n in sorted(back_services):

            def run(n=n):
                for job in back_services[n]:
                    job()

            pl.when(j == n)(run)
        return carried

    lax.fori_loop(0, S, attend_back, 0)
    if CW > 3 * E:
        dqkvt[3 * E :, :] = jnp.zeros((CW - 3 * E, T), BF16)

    def query_part(i, carried):
        cols = rows_of(i)
        dqkvt[0:E, cols] = (dqt[:, cols] * qgain_col[0:E]).astype(BF16)
        return carried + jnp.sum(dqt[:, cols] * qpre[:, cols], axis=1, keepdims=True)

    scale_terms = lax.fori_loop(0, S, query_part, jnp.zeros((E, 1), F32))

    ags, arc = ref["ags"], ref["arc"]

    def slot_of(n, rows):
        page, row = divmod(n * HALF, D)
        return w3.at[page, row : row + rows]

    order = [(u2, b2) for u2 in range(U) for b2 in range(q)]
    slots_used = 2 * U * q
    core_a = {}
    for n, (u2, b2) in enumerate(order):
        core_a[u2, b2] = links.copy(ags.at[u2, b2], slot_of(2 * n, L), sibling)
    dtok = ref["dtok"]
    release(freed_again)
    pl.semaphore_wait(freed_again, len(writers))

    def partial_rows(m, carried, others):
        block = block_of(m // q, 1 - c if others else c, m % q)
        dtok[...] = dqkvt[:, rows_of(block)].T
        for k in range(NW):
            at = slice(k * W, (k + 1) * W)
            part = dot_nt(dtok[...], wq[at, :]).astype(BF16)
            if others:
                ags[m // q, m % q, :, at] = part
            else:
                arc[m // q, m % q, :, at] = part
        if others:
            for j, key in enumerate(order):
                pl.when(m == j)(core_a[key].start)
        return carried

    lax.fori_loop(0, U * q, functools.partial(partial_rows, others=True), 0)
    lax.fori_loop(0, U * q, functools.partial(partial_rows, others=False), 0)

    HA, HB = pl.ds(0, HALF), pl.ds(HALF, HALF)
    afb, afu, asb, asu, landing = {}, {}, {}, {}, {}

    def land(key):
        nonlocal slots_used
        landing[key] = slot_of(slots_used, HALF)
        slots_used += 1
        assert slots_used * HALF <= 3 * D
        return landing[key]

    for db in range(1, q):
        to = peer(u, c, b_off[db])
        for u2 in range(U):
            afb[db, u2] = links.copy(arc.at[u2, b_off[db], HA], land(("fb", db, u2)), to)
        asb[db] = links.copy(arc.at[u, b_off[db], HB], land(("sb", db)), to)
    for du in range(1, U):
        to = peer(u_off[du], c, b)
        for b2 in range(q):
            afu[du, b2] = links.copy(arc.at[u_off[du], b2, HB], land(("fu", du, b2)), to)
        asu[du] = links.copy(arc.at[u_off[du], b, HA], land(("su", du)), to)

    def add_rows(target, other, count):
        def step(i, carried):
            add_into(target.at[strip(i)], other.at[strip(i)])
            return carried

        lax.fori_loop(0, count // STEP, step, 0)

    for u2, b2 in order:
        core_a[u2, b2].arrived()

        add_rows(arc.at[u2, b2], slot_of(2 * order.index((u2, b2)), L), L)
    for moved in list(afb.values()) + list(afu.values()):
        moved.start()

    gq, cqu, gall = ref["gq"], ref["cqu"], ref["gall"]

    def qkv_grad(n, carried):
        gq[tile(n), :] = dot(dqkvt[...], near(xa.at[:, tile(n)], "x_cols", 7)[...]).T.astype(BF16)
        return carried

    lax.fori_loop(0, NW, qkv_grad, 0)
    QR = q * SR
    up_gq, down_gq = {}, {}
    for d in range(A):
        at = gq.at[pl.ds(d * QR, QR)]
        if d > 0:
            slot = jnp.where(a + 1 == d, A, d)
            up_gq[d] = links.copy(at, cqu.at[slot], above, a < d, jnp.logical_and(a > 0, a <= d))
        if d < A - 1:
            down_gq[d] = links.copy(
                at, cqu.at[d], below, a > d, jnp.logical_and(a < A - 1, a >= d)
            )

    def line_sum_q(d):
        at = gq.at[pl.ds(d * QR, QR)]

        def from_below():
            up_gq[d].make().wait_recv()
            add_into(at, cqu.at[jnp.where(a == d, A, d)])

        def from_above():
            down_gq[d].make().wait_recv()
            add_into(at, cqu.at[d])

        if d > 0:
            pl.when(jnp.logical_and(a > 0, a <= d))(from_below)
            up_gq[d].start()
        if d < A - 1:
            pl.when(jnp.logical_and(a < A - 1, a >= d))(from_above)
            down_gq[d].start()

    for d in line_order:
        line_sum_q(d)

    for db in range(1, q):
        for u2 in range(U):
            afb[db, u2].arrived()
            add_rows(arc.at[u2, b, HA], landing["fb", db, u2], HALF)
    for du in range(1, U):
        for b2 in range(q):
            afu[du, b2].arrived()
            add_rows(arc.at[u, b2, HB], landing["fu", du, b2], HALF)
    for moved in list(asb.values()) + list(asu.values()):
        moved.start()

    for d in line_order:
        line_sum(d)

    ones = jnp.ones((8, T), BF16)
    head_sums = dot_nt(ones, dqkvt[...])
    small[pl.ds(8 + g, 1), 0:CW] = head_sums[0:1]
    small[5:6, 0:E] = jnp.transpose(jnp.broadcast_to(scale_terms, (E, 128)))[0:1, :]

    for db in range(1, q):
        asb[db].arrived()
        add_rows(arc.at[u, b, HB], landing["sb", db], HALF)
    for du in range(1, U):
        asu[du].arrived()
        add_rows(arc.at[u, b, HA], landing["su", du], HALF)

    def tok_back(i, carried):
        x, grad = tok[strip(i), :].astype(F32), arc[u, b, strip(i)].astype(F32)
        inverse = unit(x)
        normed = x * inverse
        small[0:1, :] += jnp.sum(grad * normed, axis=0, keepdims=True)
        scaled = grad * gain_attn
        mean = jnp.mean(scaled * normed, axis=-1, keepdims=True)
        ref["gtb"][strip(i), :] = (mg[strip(i), :] + inverse * (scaled - normed * mean)).astype(BF16)
        return carried

    lax.fori_loop(0, L // STEP, tok_back, 0)
    back_tok = links.copy(ref["gtb"], ref["gtok"], home, moves, moves)
    back_tok.start()

    def keep_tok():
        ref["gtok"][...] = ref["gtb"][...]

    pl.when(stays)(keep_tok)

    stages = [
        [sibling],
        [peer(u, c, b_off[db]) for db in range(1, q)],
        [peer(u_off[du], c, b) for du in range(1, U)],
        [device(r, (a + k) % A, b) for k in range(1, A)],
    ]
    stages = [stage for stage in stages if stage]
    sums, landed = ref["sums"], ref["landed"]
    count, moved_small = 0, []
    for n, stage in enumerate(stages):
        moved_small.append(
            [links.copy(sums.at[n], landed.at[count + k], to) for k, to in enumerate(stage)]
        )
        count += len(stage)

    def small_stage(n):
        for moved in moved_small[n]:
            moved.arrived()
        total = sums[n]
        first = sum(len(stage) for stage in stages[:n])
        for k in range(len(stages[n])):
            total = total + landed[first + k]
        return total

    sums[0] = small[...]
    for moved in moved_small[0]:
        moved.start()

    wide = {}
    for db in range(1, q):
        at = gq.at[pl.ds(pl.multiple_of(a * QR + b_off[db] * SR, 16), SR)]
        wide[db] = links.copy(at, gall.at[g], device(r, a, b_off[db]))
        wide[db].start()
    gall[g] = gq[pl.ds(pl.multiple_of(a * QR + b * SR, 16), SR), :]
    go = ref["go"]
    piece = rc.at[:, a, b, my_rows]
    spread = []
    if H > 1:
        at = go.at[:, my_rows, own_half]
        for du in range(U):
            for dc in range(2):
                if du or dc:
                    spread.append(links.copy(piece, at, peer(u_off[du], (c + dc) % 2, b)))
    else:
        partials = [
            links.copy(piece, ref["ru"].at[du - 1], peer(u_off[du], c, b)) for du in range(1, U)
        ]
        for moved in partials:
            moved.start()
        for moved in partials:
            moved.arrived()
        for moved in partials:
            moved.sent()
            links.copies.remove(moved)
        for k in range(U - 1):
            other = near(ref["ru"].at[k], "c_rows", 7)
            for w in range(3):
                add_into(rc.at[w, a, b, my_rows], other.at[w])
        spread.append(links.copy(piece, go.at[:, :, own_half], sibling))
    for moved in spread:
        moved.start()
    go[:, my_rows, own_half] = piece[...]

    if len(stages) > 1:
        sums[1] = small_stage(0)
        for moved in moved_small[1]:
            moved.start()
    q_across, q_core = [], []
    for db in range(1, q):
        wide[db].arrived()
    here = pl.ds(r * q, q)
    for du in range(1, U):
        q_across.append(links.copy(gall.at[here], gall.at[here], peer(u_off[du], c, b)))
        q_across[-1].start()
    for du in range(U):
        here = pl.ds((u_from[du] * 2 + c) * q, q)
        q_core.append(links.copy(gall.at[here], gall.at[here], sibling))
    q_core[0].start()
    for n in range(1, len(stages) - 1):
        sums[n + 1] = small_stage(n)
        for moved in moved_small[n + 1]:
            moved.start()
    for moved in spread:
        moved.arrived()
    for du in range(1, U):
        q_across[du - 1].arrived()
        q_core[du].start()
    ref["g_small"][...] = small_stage(len(stages) - 1)
    for moved in q_core:
        moved.arrived()
    for g2 in range(S):
        mine = gall[g2]
        for n, name in enumerate(("g_query", "g_key", "g_value")):
            ref[name][:, g2 * E : (g2 + 1) * E] = mine[:, n * E : (n + 1) * E].astype(F32)
    back_out.arrived()
    back_tok.arrived()

    lax.fori_loop(0, S, o_sent, 0)

    def m_sent(k, carried):
        m_copy(k).sent()
        return carried

    lax.fori_loop(1, S, m_sent, 0)
    for moved in links.copies:
        moved.sent()


def shards(
    R,
    S,
    tokens,
    lengths,
    parents,
    w_query,
    w_key,
    w_value,
    w_out,
    w_up,
    w_down,
    gain_attn,
    gain_ff,
    query_scale,
    bias_query,
    bias_value,
    bias_out,
    bias_up,
    bias_down,
    cotangent,
):
    L, D = tokens.shape
    SR = w_query.shape[0]
    HG = HEADS // S
    E = HG * HEAD_DIM
    CW = -(-3 * E // 128) * 128
    q, U, A, T = S // R, R // 2, R, S * L
    H = U if SR % (16 * U) == 0 else 1
    SRH = SR // H
    DH = D // 2
    NS = 8 + S
    segments = lengths.shape[1]
    dims = dict(R=R, S=S, L=L, D=D, HG=HG, E=E, CW=CW, SR=SR, H=H, SRH=SRH, segments=segments)

    tab = jnp.pad(
        jnp.concatenate([lengths, parents], axis=0).astype(F32), ((0, 6), (0, 128 - segments))
    )
    by_group = [w.reshape(SR, S, E) for w in (w_query, w_key, w_value)]
    wcat = jnp.pad(jnp.concatenate(by_group, axis=2), ((0, 0), (0, 0), (0, CW - 3 * E)))
    wcat = wcat.transpose(1, 0, 2)
    bias_rows = [bias_query.reshape(S, E), jnp.zeros((S, E), F32), bias_value.reshape(S, E)]
    biascat = jnp.pad(jnp.concatenate(bias_rows, axis=1), ((0, 0), (0, CW - 3 * E)))
    biascat = jnp.broadcast_to(biascat[:, None, :], (S, 8, CW))
    query_gain = query_base * jax.nn.softplus(query_scale) / math.sqrt(HEAD_DIM)
    qgain = jnp.pad(jnp.tile(query_gain, HG), (0, CW - E), constant_values=1.0)
    qgain = jnp.broadcast_to(qgain[None, :], (8, CW))
    zero_row = jnp.zeros_like(gain_attn)
    gains = jnp.stack(
        [gain_attn, gain_ff, bias_out, bias_up, bias_down, zero_row, zero_row, zero_row]
    )

    operands = dict(
        tokens=tokens, cotangent=cotangent, tab=tab, wcat=wcat, w_out=w_out, w_up=w_up,
        w_down=w_down, biascat=biascat, qgain=qgain, gains=gains,
    )
    outputs = dict(
        out=((L, D), BF16), gtok=((L, D), BF16), g_query=((SR, D), F32), g_key=((SR, D), F32),
        g_value=((SR, D), F32), go=((3, SR, D), BF16),
        g_small=((NS, D), F32),
    )
    um = max(U - 1, 1)
    peers = 1 + (q - 1) + (U - 1) + (A - 1)
    scratch = dict(
        tok=((L, D), BF16), cot=((L, D), BF16), tabs=((8, 128), F32),
        wq=((D, CW), BF16), w3=((3, D, D), BF16), xa=((T, D), BF16),
        qkvf=((CW, L), F32), qpre=((E, T), F32), qt=((HG, 128, T), BF16),
        keys=((HG, T, 128), BF16), kt=((HG, HEAD_DIM, T), BF16),
        vals=((HG, T, 128), BF16), vt=((HG, HEAD_DIM, T), BF16),
        ot=((E, T), F32), otb=((E, T), BF16), lse=((HG, 8, T), F32), oa=((D, L), BF16),
        otok=((L, D), BF16), mid=((L, D), F32), ffin=((L, D), BF16), up=((L, D), F32),
        hid=((L, D), BF16), outb=((L, D), BF16),
        mg=((L, D), F32), og=((L, D), BF16), mgt=((D, L), BF16), dot_t=((E, T), BF16),
        small=((NS, D), F32), gp=((3, D, DH), BF16),
        rc=((3, A, q, SR, DH), BF16),
        cu=((A + 1, 3, SRH, DH), BF16), delta=((HG, 8, T), F32), dqkvt=((CW, T), BF16),
        ags=((U, q, L, D), BF16), arc=((U, q, L, D), BF16),
        dtok=((L, CW), BF16),
        gq=((D, CW), BF16), cqu=((A + 1, q * SR, CW), BF16),
        gall=((S, SR, CW), BF16),
        sums=((5, NS, D), F32), landed=((peers, NS, D), F32),
    )
    if H == 1:
        scratch["ru"] = ((um, 3, SR, DH), BF16)
    held = [jax.ShapeDtypeStruct(*v) for v in (outputs | scratch).values()]
    dims["fits"] = sum(v.size * v.dtype.itemsize for v in held) <= VMEM_BYTES - (2 << 20)
    results = len(outputs)
    distant = () if dims["fits"] else ("xa", "cu", "ru")
    for name in distant:
        outputs[name] = scratch.pop(name)
    if distant:
        scratch["x_rows"] = ((L, D), BF16)
        scratch["x_cols"] = ((T, 256), BF16)
        scratch["c_rows"] = ((3, SRH, DH), BF16)
    names = list(operands) + list(outputs) + list(scratch)
    names += ["send_sems", "recv_sems", "local_sems", "freed", "freed_again"]

    def kernel(*refs):
        named = dict(zip(names, refs))
        for later, earlier in (("fg", "up"), ("dqt", "ot"), ("ug", "otok"), ("gtb", "ffin")):
            named[later] = named[earlier]
        named["wqt"] = named["dqkvt"].at[:, 0:D]
        layer_kernel(dims, named)

    whole = pl.BlockSpec(memory_space=pltpu.VMEM)
    far = ("tokens", "cotangent", "wcat", "w_out", "w_up", "w_down")
    made = pl.pallas_call(
        kernel,
        out_shape=[jax.ShapeDtypeStruct(*shape) for shape in outputs.values()],
        in_specs=[pl.BlockSpec(memory_space=pl.ANY) if k in far else whole for k in operands],
        out_specs=[pl.BlockSpec(memory_space=pl.ANY) if k in distant else whole for k in outputs],
        scratch_shapes=[pltpu.VMEM(*shape) for shape in scratch.values()]
        + [pltpu.SemaphoreType.DMA((COPIES,))] * 2
        + [pltpu.SemaphoreType.DMA((8,))]
        + [pltpu.SemaphoreType.REGULAR] * 2,
        compiler_params=pltpu.CompilerParams(
            collective_id=0, has_side_effects=True, vmem_limit_bytes=VMEM_BYTES
        ),
    )(*operands.values())
    out, gtok, g_query, g_key, g_value, go, g_small = made[:results]
    g_out, g_up, g_down = (go[w].astype(F32) for w in range(3))
    scale = jnp.sum(g_small[5, :E].reshape(HG, HEAD_DIM), axis=0)
    scale = scale * query_base * jax.nn.sigmoid(query_scale) / math.sqrt(HEAD_DIM)
    by_head = g_small[8:, : 3 * E]
    return (
        out,
        gtok,
        g_query,
        g_key,
        g_value,
        g_out,
        g_up,
        g_down,
        g_small[0],
        g_small[1],
        scale,
        by_head[:, :E].reshape(D),
        by_head[:, 2 * E :].reshape(D),
        g_small[2],
        g_small[3],
        g_small[4],
    )


def solution(mesh):
    rows, line, copied = P(("rep", "shard"), None), P("shard", None), P()
    in_specs = (rows, P("rep", None), P("rep", None)) + (line,) * 6 + (copied,) * 8 + (rows,)
    out_specs = (rows, rows) + (line,) * 6 + (copied,) * 8
    body = functools.partial(shards, mesh.shape["rep"], mesh.shape["shard"])
    return jax.shard_map(
        body, mesh=mesh, in_specs=in_specs, out_specs=out_specs, check_vma=False
    )
```

time: 1310 us -> 430 us (0.33)
  waiting for transfers between devices: 920 us -> 0 us
  Pallas kernels: 0 us -> 392 us
  matrix products: 178 us -> 0 us
  local copies, waits for them, and re-layouts: 94.8 us -> 21.1 us
  blocking collectives: 41.4 us -> 0 us
  other arithmetic: 43.2 us -> 7.31 us
  between operations: 15.1 us -> 0.76 us
    reduce_scatter x3 -> x0, waiting for transfers between devices: 502 us -> none  [the longest x1 315 us: shards(): lax.psum_scatter(jnp.concatenate(pieces, axis=1).astype(jnp.bfloat16), 's...]
    all_gather x8 -> x0, waiting for transfers between devices: 401 us -> none  [the longest x1 81.5 us: shards(): piece_keys = lax.all_gather(key_rows, 'shard', axis=0, tiled=True)]
    pallas_call x0 -> x1, Pallas kernels: none -> 392 us  [shards(): pl.pallas_call(kernel, out_shape=[jax.ShapeDtypeStruct(*shape) for shape...]
    dot_general x59 -> x0, matrix products: 178 us -> none  [the longest x4 27.1 us: block_grads(): jnp.einsum('qhd,khd->hqk', out_grad, value_rows, preferred_element_type=j...]
    psum x1 -> x0, blocking collectives: 41.4 us -> none  [shards(): lax.psum((grad_gain_attn, grad_gain_ff, grad_query_scale, jnp.sum(qpre_gr...]
    unnamed x88 -> x19, local copies, waits for them, and re-layouts: 41.1 us -> 4.87 us
    reduce_sum x18 -> x1, other arithmetic: 25.5 us -> 0.02 us  [shards(): scale = jnp.sum(g_small[5, :E].reshape(HG, HEAD_DIM), axis=0)]
    reshape x2 -> x10, local copies, waits for them, and re-layouts: 31.6 us -> 6.74 us  [the longest x6 3.86 us: shards(): by_group = [w.reshape(SR, S, E) for w in (w_query, w_key, w_value)]]
  transfers between devices with their start and end apart: 12 -> 0, of which waited for: 11 -> 0; matrix products, arithmetic and copies ran while one was open for 14% -> 0% of each run, Pallas kernels for 0% -> 0%
where the time goes in v1:
time: 430 us; the launch traced here: 421 us
  Pallas kernels  392 us (91%)
  local copies, waits for them, and re-layouts  21.1 us (5%)
  other arithmetic  7.31 us (2%)
    pallas_call x1, Pallas kernels, shards(): pl.pallas_call(kernel, out_shape=[jax.ShapeDtypeStruct(*shape) for shape...  392 us

profile of v1, /device:TPU:1, one launch (start us, length us, event | category | flops | bytes accessed | tf_op | source)
XLA Modules:
  0.0 421.2 jit_solution(10224511371543250800)
XLA Ops:
  0.6 0.7 fusion.6
  1.3 0.1 tile.10
  1.4 0.7 add_convert_fusion
  2.1 0.1 pad.21.clone
  2.2 0.6 pad.16.refs_2_
  2.8 0.7 stack.21
  3.5 0.7 stack.22
  4.2 0.7 stack.23
  4.9 0.7 stack.24
  5.6 0.7 stack.25
  6.3 0.8 reshape.65
  7.1 0.8 reshape.66
  7.8 0.1 pad_maximum_fusion
  7.9 0.0 copy-start.5
  7.9 0.7 stack.27.refs_9_
  8.6 0.6 broadcast_in_dim.8.refs_8_
  9.2 0.7 broadcast_in_dim.7.refs_7_
  9.9 1.8 reshape.62
  11.7 0.1 copy.34
  11.8 0.0 copy-done.5
  11.9 0.0 copy-start.6
  11.9 0.8 reshape.63
  12.7 0.1 copy.35
  12.8 0.0 copy-done.6
  12.9 0.8 reshape.64
  13.7 0.1 copy.36
  13.8 1.9 fusion.5.refs_3_
  15.7 392.0 %shard_map.297 = (bf16[256,1280]{1,0:T(8,128)(2,1)}, bf16[256,1280]{1,0:T(8,128)(2,1)}, f32[160,1280]{1,0:T(8,128)}, f32[160,1280]{1,0:T(8,128)}, f32[160,1280]{...) custom-call(bf16[256,1280]{1,0:T(8,128)(2,1)} %refs_0_.1, bf16[256,1280]{1,0:T(8,128)(2,1)} %refs_1_.1, ...), custom_call_target="tpu_custom_call" | custom-call | tf_op jit(solution)/shard_map/pallas_call | solution.py:1279
  407.7 0.7 slice_reduce_fusion.5
  408.4 0.1 reshape_squeeze.3
  408.5 1.2 fusion.7
  409.7 0.8 fusion.8
  410.5 1.7 slice_reduce_fusion
  412.2 0.7 reshape.68
  412.8 0.7 reshape.67
  413.5 0.0 copy-start.4
  413.5 2.8 bitcast_convert_fusion
  416.3 0.0 copy-done.4
  416.3 0.0 copy-start.2
  416.3 0.8 copy.42
  417.2 0.5 copy-done.3
  417.6 0.8 copy.43
  418.5 0.0 copy-done.2
  418.5 0.9 copy.44
  419.4 0.0 copy-done.1
  419.4 0.9 copy.45
  420.3 0.0 copy-done
  420.3 0.9 copy.46
  (10 shorter events, 0.1 us)
Async XLA Ops:
  7.9 3.9 copy-start.5
  11.9 1.0 copy-start.6
  413.5 2.8 copy-start.4
  416.3 1.3 copy-start.3
  416.3 2.2 copy-start.2
  417.6 1.7 copy-start.1
  418.5 1.8 copy-start

commit v2 on v1

--- a/solution.py
+++ b/solution.py
@@ -18,7 +18,6 @@
 query_base = 1.442695
 masked_score = -1e30
 LABELS = 16
-COPIES = 700
 VMEM_BYTES = 64 << 20
 
 
@@ -58,7 +57,6 @@
     def block(self, count):
         first = self.used
         self.used += count
-        assert self.used <= COPIES
         return first
 
     def copy(self, src, dst, device, sends=True, receives=True, index=None, keep=True):
@@ -171,7 +169,7 @@
         return pl.ds(pl.multiple_of((a2 * q + b2) * SR, 16), SR)
 
     def near(src, name, n):
-        if dims["fits"]:
+        if dims["fits"] or name == "q_rows":
             return src
         copy = local(src, ref[name], n)
         copy.start()
@@ -252,10 +250,13 @@
                 for du in range(1, U):
                     side_w[w, slot, du, 0] = links.copy(at, at, peer(u_off[du], c, b), valid, valid)
                     for db in range(1, q):
-                        passed = w3.at[w, piece_rows(a0, b_from[db], u), own_half]
-                        side_w[w, slot, du, db] = links.copy(
-                            passed, passed, peer(u_off[du], c, b), valid, valid
-                        )
+                        if (slot + w) % 2:
+                            passed = w3.at[w, piece_rows(a0, b_from[db], u), own_half]
+                            to = peer(u_off[du], c, b)
+                        else:
+                            passed = w3.at[w, piece_rows(a0, b, u_from[du]), own_half]
+                            to = peer(u, c, b_off[db])
+                        side_w[w, slot, du, db] = links.copy(passed, passed, to, valid, valid)
             at = w3.at[w, pl.ds(pl.multiple_of(a0 * q * SR, 16), q * SR), own_half]
             core_w[w, slot] = links.copy(at, at, sibling, valid, valid)
         for db in range(1, q):
@@ -264,12 +265,13 @@
             at = w3.at[w, shard_rows(a, b_from[db]), own_half]
             core_own[w, db] = links.copy(at, at, sibling)
 
+    for moved in own_w.values():
+        moved.start()
+
     def w3_line(w, k):
         if k < 0:
             up_w[w, 0].start()
             down_w[w, 0].start()
-            for db in range(1, q):
-                own_w[w, db].start()
             return
         up_w[w, k].arrived()
         down_w[w, k].arrived()
@@ -290,15 +292,16 @@
         for slot in (-(k + 1), k + 1):
             for db in range(1, q):
                 side_w[w, slot, 0, db].arrived()
-                if H > 1:
-                    for du in range(1, U):
+            if H > 1:
+                for du in range(1, U):
+                    side_w[w, slot, du, 0].arrived()
+                    for db in range(1, q):
                         side_w[w, slot, du, db].start()
 
     def w3_core(w, k):
         for slot in (-(k + 1), k + 1):
             if H > 1:
                 for du in range(1, U):
-                    side_w[w, slot, du, 0].arrived()
                     for db in range(1, q):
                         side_w[w, slot, du, db].arrived()
             core_w[w, slot].start()
@@ -368,9 +371,6 @@
         wcat_b[db].arrived()
         up_q[0, db].start()
         down_q[0, db].start()
-    swaps[2].start()
-    for w in range(3):
-        w3_line(w, -1)
 
     swaps[1].arrived()
     lane = lax.broadcasted_iota(jnp.int32, (LABELS, 128), 1)
@@ -405,18 +405,18 @@
     for du in range(1, U):
         own_x[0, du, 0].arrived()
         sib_x[0, du, 0].start()
-    for k in range(1, A - 1):
+    for w in range(3):
+        w3_side(w, -1)
+    for k in range(1, A - 2):
         wq_pass(k)
     for w in range(3):
-        w3_side(w, -1)
-    w3_line(0, 0)
+        w3_line(w, -1)
     for h in range(2):
         for du in range(1, U):
             for db in range(1, q):
                 pass_x[h, du, db].arrived()
                 sib_x[h, du, db].start()
-    w3_line(1, 0)
-    w3_line(2, 0)
+    wq_pass(A - 2)
 
     def turn_wq(i, carried):
         here = pl.ds(pl.multiple_of(i * W, W), W)
@@ -470,9 +470,6 @@
 
     ot, otb, lse, oa = ref["ot"], ref["otb"], ref["lse"], ref["oa"]
     first_o = links.block(S)
-    diagonal = lax.broadcasted_iota(jnp.int32, (L, L), 0) <= lax.broadcasted_iota(
-        jnp.int32, (L, L), 1
-    )
     o_slot = pl.ds(pl.multiple_of(g * E, 16), E)
 
     def o_copy(block):
@@ -482,25 +479,33 @@
             otb.at[:, rows_of(block)], oa.at[o_slot], device(r2, a, b2), index=index, keep=False
         )
 
-    services = {}
-
-    def serve(at, job):
-        services.setdefault(at, []).append(job)
-
-    for k in range(A - 1):
+    PAIR = 2
+    SQ = PAIR * L
+    diagonal = lax.broadcasted_iota(jnp.int32, (SQ, SQ), 0) <= lax.broadcasted_iota(
+        jnp.int32, (SQ, SQ), 1
+    )
+    for w in range(3):
+        w3_line(w, 0)
+
+    def after_block(i):
         for w in range(3):
-            at = min(S - 1, 2 * k + (w + 1) // 2)
-            serve(at, functools.partial(w3_side, w, k))
-            if k + 1 < A - 1:
-                serve(at, functools.partial(w3_line, w, k + 1))
-            serve(min(S - 1, at + 1), functools.partial(w3_core, w, k))
+            if i == 1:
+                w3_side(w, 0)
+            elif i == 2 and A > 2:
+                w3_line(w, 1)
+            elif i == 3 and A > 2:
+                w3_side(w, 1)
+                w3_core(w, 0)
+
+    def wide_rows(i):
+        return pl.ds(pl.multiple_of(i * SQ, SQ), SQ)
 
     def attend(i, carried):
-        cols = rows_of(i)
+        cols = wide_rows(i)
         query = [qt[hd, :, cols] for hd in range(HG)]
 
         def key_block(j, state, on_diagonal):
-            here = rows_of(j)
+            here = wide_rows(j)
             result = []
             for hd in range(HG):
                 top, total, acc = state[hd]
@@ -517,9 +522,9 @@
 
         start = tuple(
             (
-                jnp.full((1, L), masked_score, F32),
-                jnp.zeros((1, L), F32),
-                jnp.zeros((HD, L), F32),
+                jnp.full((1, SQ), masked_score, F32),
+                jnp.zeros((1, SQ), F32),
+                jnp.zeros((HD, SQ), F32),
             )
             for _ in range(HG)
         )
@@ -531,23 +536,24 @@
             head = pl.ds(hd * HD, HD)
             ot[head, cols] = mixed
             otb[head, cols] = mixed.astype(BF16)
-            lse[hd, :, cols] = jnp.broadcast_to(top + jnp.log(total), (8, L))
-
-        def keep_block():
-            oa[o_slot, :] = otb[:, cols]
-
-        pl.when(i == blk)(keep_block)
-        pl.when(i != blk)(lambda: o_copy(i).start())
-        for j in sorted(services):
-
-            def run(j=j):
-                for job in services[j]:
-                    job()
-
-            pl.when(i == j)(run)
-        return carried
-
-    lax.fori_loop(0, S, attend, 0)
+            lse[hd, :, cols] = jnp.broadcast_to(top + jnp.log(total), (8, SQ))
+        for k in range(PAIR):
+            block = i * PAIR + k
+
+            def keep_block(block=block):
+                oa[o_slot, :] = otb[:, rows_of(block)]
+
+            pl.when(block == blk)(keep_block)
+            pl.when(block != blk)(lambda block=block: o_copy(block).start())
+        for j in range(1, 4):
+            pl.when(i == j)(functools.partial(after_block, j))
+        return carried
+
+    lax.fori_loop(0, S // PAIR, attend, 0)
+    if A > 2:
+        for w in range(3):
+            w3_line(w, 2)
+    swaps[2].start()
 
     def o_arrived(k, carried):
         links.copy(
@@ -556,6 +562,13 @@
         return carried
 
     lax.fori_loop(1, S, o_arrived, 0)
+    for w in range(3):
+        if A > 2:
+            w3_core(w, 1)
+            w3_side(w, 2)
+        else:
+            w3_side(w, 0)
+            w3_core(w, 0)
 
     def o_sent(i, carried):
         pl.when(i != blk)(lambda: o_copy(i).sent())
@@ -573,6 +586,13 @@
         return carried
 
     lax.fori_loop(0, NW, turn_o, 0)
+    for w in range(3):
+        if A > 2:
+            w3_core(w, 2)
+        for k in range(3, A - 1):
+            w3_line(w, k)
+            w3_side(w, k)
+            w3_core(w, k)
     w3_whole(0)
 
     def out_step(n, carried):
@@ -612,7 +632,9 @@
     back_out.start()
 
     def keep_out():
-        ref["out"][...] = outb[...]
+        kept = local(outb, ref["out"], 0)
+        kept.start()
+        kept.wait()
 
     pl.when(stays)(keep_out)
     swaps[2].arrived()
@@ -811,40 +833,62 @@
                     second_u[w, du, a2].arrived()
                     add_into(rc.at[w, a2, b, my_rows], t2u(w, du, a2))
 
+    class Line:
+        def __init__(self, part, landed):
+            self.part, self.landed = part, landed
+            self.first_up, self.first_down = links.block(A), links.block(A)
+
+        def copy(self, d, upward):
+            slot = jnp.where(d == a + 1, A, d) if upward else d
+            return links.copy(
+                self.part(d),
+                self.landed(slot),
+                above if upward else below,
+                index=(self.first_up if upward else self.first_down) + d,
+                keep=False,
+            )
+
+        def begin(self):
+            for k in range(1, A):
+                pl.when(a == 0)(lambda k=k: self.copy(A - k, True).make().start())
+                pl.when(a == A - 1)(lambda k=k: self.copy(k - 1, False).make().start())
+
+        def step(self, t):
+            for upward in (True, False):
+                d = A - 1 + a - t if upward else a + t - (A - 1)
+                if upward:
+                    takes = (a > 0) & (d >= a) & (d <= A - 1)
+                    passes = takes & (d > a)
+                    slot = jnp.where(d == a, A, d)
+                else:
+                    takes = (a < A - 1) & (d <= a) & (d >= 0)
+                    passes = takes & (d < a)
+                    slot = d
+                d = jnp.clip(d, 0, A - 1)
+                slot = jnp.clip(slot, 0, A)
+
+                def take(d=d, upward=upward, slot=slot):
+                    self.copy(d, upward).make().wait_recv()
+                    add_into(self.part(d), near(self.landed(slot), self.near_name, 7))
+
+                pl.when(takes)(take)
+                pl.when(passes)(lambda d=d, upward=upward: self.copy(d, upward).make().start())
+
+        def finish(self):
+            for d in range(A):
+                pl.when(a < d)(lambda d=d: self.copy(d, True).make().wait_send())
+                pl.when(a > d)(lambda d=d: self.copy(d, False).make().wait_send())
+
     cu = ref["cu"]
-    up_g, down_g = {}, {}
-    for d in range(A):
-        at = rc.at[:, d, b, my_rows]
-        if d > 0:
-            slot = jnp.where(a + 1 == d, A, d)
-            up_g[d] = links.copy(at, cu.at[slot], above, a < d, jnp.logical_and(a > 0, a <= d))
-        if d < A - 1:
-            down_g[d] = links.copy(
-                at, cu.at[d], below, a > d, jnp.logical_and(a < A - 1, a >= d)
+    lines = []
+    for w in range(3):
+        lines.append(
+            Line(
+                lambda d, w=w: rc.at[w, d, b, my_rows],
+                lambda slot, w=w: cu.at[slot, w],
             )
-
-    def line_sum(d):
-        def from_below():
-            up_g[d].make().wait_recv()
-            slot = jnp.where(a == d, A, d)
-            other = near(cu.at[slot], "c_rows", 7)
-            for w in range(3):
-                add_into(rc.at[w, d, b, my_rows], other.at[w])
-
-        def from_above():
-            down_g[d].make().wait_recv()
-            other = near(cu.at[d], "c_rows", 7)
-            for w in range(3):
-                add_into(rc.at[w, d, b, my_rows], other.at[w])
-
-        if d > 0:
-            pl.when(jnp.logical_and(a > 0, a <= d))(from_below)
-            up_g[d].start()
-        if d < A - 1:
-            pl.when(jnp.logical_and(a < A - 1, a >= d))(from_above)
-            down_g[d].start()
-
-    line_order = sorted(range(A), key=lambda d: -abs(2 * d - (A - 1)))
+        )
+        lines[-1].near_name = "c_rows"
 
     delta, dqt, dqkvt = ref["delta"], ref["dqt"], ref["dqkvt"]
     for hd in range(HG):
@@ -852,19 +896,28 @@
         total = jnp.sum(dot_t[head, :].astype(F32) * ot[head, :], axis=0, keepdims=True)
         delta[hd, :, :] = jnp.broadcast_to(total, (8, T))
     dqt[...] = jnp.zeros_like(dqt)
-    back_services = {}
-    for w, at in ((2, 0), (1, 1), (0, 1)):
-        back_services.setdefault(at, []).append(functools.partial(core_sum, w))
-    for w, at in ((2, 2), (1, 3), (0, 4)):
-        back_services.setdefault(min(at, S - 1), []).append(functools.partial(side_sum_1, w))
-    for w, at in ((2, 4), (1, 5), (0, 6)):
-        back_services.setdefault(min(at, S - 1), []).append(functools.partial(side_sum_2, w))
+    core_sum(0)
+
+    def after_back(j):
+        if j == 0:
+            core_sum(1)
+            core_sum(2)
+        elif j == 1:
+            side_sum_1(0)
+        elif j == 2:
+            side_sum_1(1)
+            side_sum_2(0)
+            lines[0].begin()
+        elif j == 3:
+            side_sum_1(2)
+            side_sum_2(1)
+            lines[1].begin()
 
     def attend_back(j, carried):
-        here = rows_of(j)
+        here = wide_rows(j)
 
         def query_block(i, state, on_diagonal):
-            cols = rows_of(i)
+            cols = wide_rows(i)
             result = []
             for hd in range(HG):
                 dk, dv = state[hd]
@@ -882,23 +935,18 @@
                 result.append((dk, dv))
             return tuple(result)
 
-        zero = jnp.zeros((HD, L), F32)
+        zero = jnp.zeros((HD, SQ), F32)
         state = query_block(j, tuple((zero, zero) for _ in range(HG)), True)
-        state = lax.fori_loop(j + 1, S, functools.partial(query_block, on_diagonal=False), state)
+        state = lax.fori_loop(j + 1, S // PAIR, functools.partial(query_block, on_diagonal=False), state)
         for hd in range(HG):
             dk, dv = state[hd]
             dqkvt[pl.ds(E + hd * HD, HD), here] = dk.astype(BF16)
             dqkvt[pl.ds(2 * E + hd * HD, HD), here] = dv.astype(BF16)
-        for n in sorted(back_services):
-
-            def run(n=n):
-                for job in back_services[n]:
-                    job()
-
-            pl.when(j == n)(run)
-        return carried
-
-    lax.fori_loop(0, S, attend_back, 0)
+        for n in range(4):
+            pl.when(j == n)(functools.partial(after_back, n))
+        return carried
+
+    lax.fori_loop(0, S // PAIR, attend_back, 0)
     if CW > 3 * E:
         dqkvt[3 * E :, :] = jnp.zeros((CW - 3 * E, T), BF16)
 
@@ -909,6 +957,25 @@
 
     scale_terms = lax.fori_loop(0, S, query_part, jnp.zeros((E, 1), F32))
 
+    gq, cqu, gall = ref["gq"], ref["cqu"], ref["gall"]
+
+    def qkv_grad(n, carried):
+        gq[tile(n), :] = dot(dqkvt[...], near(xa.at[:, tile(n)], "x_cols", 7)[...]).T.astype(BF16)
+        return carried
+
+    lax.fori_loop(0, NW, qkv_grad, 0)
+    QR = q * SR
+    line_q = Line(
+        lambda d: gq.at[pl.ds(pl.multiple_of(d * QR, 16), QR)], lambda slot: cqu.at[slot]
+    )
+    line_q.near_name = "q_rows"
+    line_q.begin()
+
+    for group in (own_x, pass_x, sib_x):
+        for moved in group.values():
+            moved.sent()
+            links.copies.remove(moved)
+
     ags, arc = ref["ags"], ref["arc"]
 
     def slot_of(n, rows):
@@ -919,8 +986,10 @@
     slots_used = 2 * U * q
     core_a = {}
     for n, (u2, b2) in enumerate(order):
-        core_a[u2, b2] = links.copy(ags.at[u2, b2], slot_of(2 * n, L), sibling)
+        core_a[u2, b2] = links.copy(ags.at[pl.ds(n * L, L)], slot_of(2 * n, L), sibling)
     dtok = ref["dtok"]
+    side_sum_2(2)
+    lines[2].begin()
     release(freed_again)
     pl.semaphore_wait(freed_again, len(writers))
 
@@ -930,10 +999,8 @@
         for k in range(NW):
             at = slice(k * W, (k + 1) * W)
             part = dot_nt(dtok[...], wq[at, :]).astype(BF16)
-            if others:
-                ags[m // q, m % q, :, at] = part
-            else:
-                arc[m // q, m % q, :, at] = part
+            target = ags if others else arc
+            target[rows_of(m), at] = part
         if others:
             for j, key in enumerate(order):
                 pl.when(m == j)(core_a[key].start)
@@ -942,7 +1009,10 @@
     lax.fori_loop(0, U * q, functools.partial(partial_rows, others=True), 0)
     lax.fori_loop(0, U * q, functools.partial(partial_rows, others=False), 0)
 
-    HA, HB = pl.ds(0, HALF), pl.ds(HALF, HALF)
+
+    def part(u2, b2, h):
+        return arc.at[half_rows(u2 * q + b2, h)]
+
     afb, afu, asb, asu, landing = {}, {}, {}, {}, {}
 
     def land(key):
@@ -955,13 +1025,13 @@
     for db in range(1, q):
         to = peer(u, c, b_off[db])
         for u2 in range(U):
-            afb[db, u2] = links.copy(arc.at[u2, b_off[db], HA], land(("fb", db, u2)), to)
-        asb[db] = links.copy(arc.at[u, b_off[db], HB], land(("sb", db)), to)
+            afb[db, u2] = links.copy(part(u2, b_off[db], 0), land(("fb", db, u2)), to)
+        asb[db] = links.copy(part(u, b_off[db], 1), land(("sb", db)), to)
     for du in range(1, U):
         to = peer(u_off[du], c, b)
         for b2 in range(q):
-            afu[du, b2] = links.copy(arc.at[u_off[du], b2, HB], land(("fu", du, b2)), to)
-        asu[du] = links.copy(arc.at[u_off[du], b, HA], land(("su", du)), to)
+            afu[du, b2] = links.copy(part(u_off[du], b2, 1), land(("fu", du, b2)), to)
+        asu[du] = links.copy(part(u_off[du], b, 0), land(("su", du)), to)
 
     def add_rows(target, other, count):
         def step(i, carried):
@@ -973,63 +1043,26 @@
     for u2, b2 in order:
         core_a[u2, b2].arrived()
 
-        add_rows(arc.at[u2, b2], slot_of(2 * order.index((u2, b2)), L), L)
+        add_rows(arc.at[rows_of(u2 * q + b2)], slot_of(2 * order.index((u2, b2)), L), L)
     for moved in list(afb.values()) + list(afu.values()):
         moved.start()
-
-    gq, cqu, gall = ref["gq"], ref["cqu"], ref["gall"]
-
-    def qkv_grad(n, carried):
-        gq[tile(n), :] = dot(dqkvt[...], near(xa.at[:, tile(n)], "x_cols", 7)[...]).T.astype(BF16)
-        return carried
-
-    lax.fori_loop(0, NW, qkv_grad, 0)
-    QR = q * SR
-    up_gq, down_gq = {}, {}
-    for d in range(A):
-        at = gq.at[pl.ds(d * QR, QR)]
-        if d > 0:
-            slot = jnp.where(a + 1 == d, A, d)
-            up_gq[d] = links.copy(at, cqu.at[slot], above, a < d, jnp.logical_and(a > 0, a <= d))
-        if d < A - 1:
-            down_gq[d] = links.copy(
-                at, cqu.at[d], below, a > d, jnp.logical_and(a < A - 1, a >= d)
-            )
-
-    def line_sum_q(d):
-        at = gq.at[pl.ds(d * QR, QR)]
-
-        def from_below():
-            up_gq[d].make().wait_recv()
-            add_into(at, cqu.at[jnp.where(a == d, A, d)])
-
-        def from_above():
-            down_gq[d].make().wait_recv()
-            add_into(at, cqu.at[d])
-
-        if d > 0:
-            pl.when(jnp.logical_and(a > 0, a <= d))(from_below)
-            up_gq[d].start()
-        if d < A - 1:
-            pl.when(jnp.logical_and(a < A - 1, a >= d))(from_above)
-            down_gq[d].start()
-
-    for d in line_order:
-        line_sum_q(d)
 
     for db in range(1, q):
         for u2 in range(U):
             afb[db, u2].arrived()
-            add_rows(arc.at[u2, b, HA], landing["fb", db, u2], HALF)
+            add_rows(part(u2, b, 0), landing["fb", db, u2], HALF)
     for du in range(1, U):
         for b2 in range(q):
             afu[du, b2].arrived()
-            add_rows(arc.at[u, b2, HB], landing["fu", du, b2], HALF)
+            add_rows(part(u, b2, 1), landing["fu", du, b2], HALF)
     for moved in list(asb.values()) + list(asu.values()):
         moved.start()
-
-    for d in line_order:
-        line_sum(d)
+    line_q.step(1)
+    for t in range(1, A):
+        for line in lines:
+            line.step(t)
+        if t > 1:
+            line_q.step(t)
 
     ones = jnp.ones((8, T), BF16)
     head_sums = dot_nt(ones, dqkvt[...])
@@ -1038,13 +1071,14 @@
 
     for db in range(1, q):
         asb[db].arrived()
-        add_rows(arc.at[u, b, HB], landing["sb", db], HALF)
+        add_rows(part(u, b, 1), landing["sb", db], HALF)
     for du in range(1, U):
         asu[du].arrived()
-        add_rows(arc.at[u, b, HA], landing["su", du], HALF)
+        add_rows(part(u, b, 0), landing["su", du], HALF)
 
     def tok_back(i, carried):
-        x, grad = tok[strip(i), :].astype(F32), arc[u, b, strip(i)].astype(F32)
+        x = tok[strip(i), :].astype(F32)
+        grad = arc[pl.ds(pl.multiple_of((u * q + b) * L + i * STEP, STEP), STEP), :].astype(F32)
         inverse = unit(x)
         normed = x * inverse
         small[0:1, :] += jnp.sum(grad * normed, axis=0, keepdims=True)
@@ -1058,7 +1092,9 @@
     back_tok.start()
 
     def keep_tok():
-        ref["gtok"][...] = ref["gtb"][...]
+        kept = local(ref["gtb"], ref["gtok"], 0)
+        kept.start()
+        kept.wait()
 
     pl.when(stays)(keep_tok)
 
@@ -1117,9 +1153,8 @@
             moved.sent()
             links.copies.remove(moved)
         for k in range(U - 1):
-            other = near(ref["ru"].at[k], "c_rows", 7)
             for w in range(3):
-                add_into(rc.at[w, a, b, my_rows], other.at[w])
+                add_into(rc.at[w, a, b, my_rows], near(ref["ru"].at[k, w], "c_rows", 7))
         spread.append(links.copy(piece, go.at[:, :, own_half], sibling))
     for moved in spread:
         moved.start()
@@ -1152,10 +1187,18 @@
     ref["g_small"][...] = small_stage(len(stages) - 1)
     for moved in q_core:
         moved.arrived()
+    unpacked = [ref[name].at[pl.ds(0, SR)] for name in ("mid", "up", "mg")]
     for g2 in range(S):
         mine = gall[g2]
-        for n, name in enumerate(("g_query", "g_key", "g_value")):
-            ref[name][:, g2 * E : (g2 + 1) * E] = mine[:, n * E : (n + 1) * E].astype(F32)
+        for n in range(3):
+            unpacked[n][:, g2 * E : (g2 + 1) * E] = mine[:, n * E : (n + 1) * E].astype(F32)
+    written = [
+        local(unpacked[n], ref[name], n) for n, name in enumerate(("g_query", "g_key", "g_value"))
+    ]
+    for copy in written:
+        copy.start()
+    for copy in written:
+        copy.wait()
     back_out.arrived()
     back_tok.arrived()
 
@@ -1166,8 +1209,11 @@
         return carried
 
     lax.fori_loop(1, S, m_sent, 0)
+    for line in lines + [line_q]:
+        line.finish()
     for moved in links.copies:
         moved.sent()
+    return links.used
 
 
 def shards(
@@ -1246,7 +1292,7 @@
         small=((NS, D), F32), gp=((3, D, DH), BF16),
         rc=((3, A, q, SR, DH), BF16),
         cu=((A + 1, 3, SRH, DH), BF16), delta=((HG, 8, T), F32), dqkvt=((CW, T), BF16),
-        ags=((U, q, L, D), BF16), arc=((U, q, L, D), BF16),
+        ags=((T // 2, D), BF16), arc=((T // 2, D), BF16),
         dtok=((L, CW), BF16),
         gq=((D, CW), BF16), cqu=((A + 1, q * SR, CW), BF16),
         gall=((S, SR, CW), BF16),
@@ -1254,41 +1300,54 @@
     )
     if H == 1:
         scratch["ru"] = ((um, 3, SR, DH), BF16)
-    held = [jax.ShapeDtypeStruct(*v) for v in (outputs | scratch).values()]
-    dims["fits"] = sum(v.size * v.dtype.itemsize for v in held) <= VMEM_BYTES - (2 << 20)
+    held = [jax.ShapeDtypeStruct(*v) for v in scratch.values()]
+    dims["fits"] = sum(v.size * v.dtype.itemsize for v in held) <= VMEM_BYTES - (6 << 20)
     results = len(outputs)
-    distant = () if dims["fits"] else ("xa", "cu", "ru")
-    for name in distant:
-        outputs[name] = scratch.pop(name)
-    if distant:
+    distant = ["out", "gtok", "g_query", "g_key", "g_value"]
+    if dims["fits"]:
+        scratch.pop("ags")
+        scratch.pop("arc")
+    else:
+        for name in ("xa", "cu", "ru"):
+            outputs[name] = scratch.pop(name)
+            distant.append(name)
         scratch["x_rows"] = ((L, D), BF16)
         scratch["x_cols"] = ((T, 256), BF16)
-        scratch["c_rows"] = ((3, SRH, DH), BF16)
+        scratch["c_rows"] = ((SRH, DH), BF16)
     names = list(operands) + list(outputs) + list(scratch)
     names += ["send_sems", "recv_sems", "local_sems", "freed", "freed_again"]
+
+    counted = [1024]
 
     def kernel(*refs):
         named = dict(zip(names, refs))
         for later, earlier in (("fg", "up"), ("dqt", "ot"), ("ug", "otok"), ("gtb", "ffin")):
             named[later] = named[earlier]
         named["wqt"] = named["dqkvt"].at[:, 0:D]
-        layer_kernel(dims, named)
+        if dims["fits"]:
+            named["ags"] = named["xa"].at[pl.ds(0, T // 2)]
+            named["arc"] = named["xa"].at[pl.ds(T // 2, T // 2)]
+        counted[0] = layer_kernel(dims, named)
 
     whole = pl.BlockSpec(memory_space=pltpu.VMEM)
     far = ("tokens", "cotangent", "wcat", "w_out", "w_up", "w_down")
-    made = pl.pallas_call(
+    def call(*operands):
+        return pl.pallas_call(
         kernel,
         out_shape=[jax.ShapeDtypeStruct(*shape) for shape in outputs.values()],
         in_specs=[pl.BlockSpec(memory_space=pl.ANY) if k in far else whole for k in operands],
         out_specs=[pl.BlockSpec(memory_space=pl.ANY) if k in distant else whole for k in outputs],
         scratch_shapes=[pltpu.VMEM(*shape) for shape in scratch.values()]
-        + [pltpu.SemaphoreType.DMA((COPIES,))] * 2
+        + [pltpu.SemaphoreType.DMA((counted[0],))] * 2
         + [pltpu.SemaphoreType.DMA((8,))]
         + [pltpu.SemaphoreType.REGULAR] * 2,
         compiler_params=pltpu.CompilerParams(
             collective_id=0, has_side_effects=True, vmem_limit_bytes=VMEM_BYTES
         ),
-    )(*operands.values())
+    )(*operands)
+
+    jax.eval_shape(call, *operands.values())
+    made = call(*operands.values())
     out, gtok, g_query, g_key, g_value, go, g_small = made[:results]
     g_out, g_up, g_down = (go[w].astype(F32) for w in range(3))
     scale = jnp.sum(g_small[5, :E].reshape(HG, HEAD_DIM), axis=0)

time: 430 us -> 325 us (0.76); the launches traced: 421 us -> 321 us
  Pallas kernels: 392 us -> 292 us
    pallas_call x1, Pallas kernels: 392 us -> 292 us  [call(): pl.pallas_call(kernel, out_shape=[jax.ShapeDtypeStruct(*shape) for shape...]
where the time goes in v2:
time: 325 us; the launch traced here: 321 us
  Pallas kernels  292 us (90%)
  local copies, waits for them, and re-layouts  21.1 us (6%)
  other arithmetic  7.31 us (2%)
    pallas_call x1, Pallas kernels, call(): pl.pallas_call(kernel, out_shape=[jax.ShapeDtypeStruct(*shape) for shape...  292 us

profile of v2, /device:TPU:1, one launch (start us, length us, event | category | flops | bytes accessed | tf_op | source)
XLA Modules:
  0.0 320.8 jit_solution(12889832853958431205)
XLA Ops:
  0.6 0.7 fusion.6
  1.3 0.1 tile.10
  1.4 0.7 add_convert_fusion
  2.1 0.1 pad.21.clone
  2.2 0.6 pad.16.refs_2_
  2.8 0.7 stack.21
  3.5 0.7 stack.22
  4.2 0.7 stack.23
  4.9 0.7 stack.24
  5.6 0.7 stack.25
  6.3 0.8 reshape.65
  7.1 0.8 reshape.66
  7.8 0.1 pad_maximum_fusion
  7.9 0.0 copy-start.5
  7.9 0.7 stack.27.refs_9_
  8.6 0.6 broadcast_in_dim.8.refs_8_
  9.2 0.7 broadcast_in_dim.7.refs_7_
  9.9 1.8 reshape.62
  11.7 0.1 copy.34
  11.8 0.0 copy-done.5
  11.9 0.0 copy-start.6
  11.9 0.8 reshape.63
  12.7 0.1 copy.35
  12.8 0.0 copy-done.6
  12.9 0.8 reshape.64
  13.7 0.1 copy.36
  13.8 1.9 fusion.5.refs_3_
  15.7 291.6 %shard_map.297 = (bf16[256,1280]{1,0:T(8,128)(2,1)}, bf16[256,1280]{1,0:T(8,128)(2,1)}, f32[160,1280]{1,0:T(8,128)}, f32[160,1280]{1,0:T(8,128)}, f32[160,1280]{...) custom-call(bf16[256,1280]{1,0:T(8,128)(2,1)} %refs_0_.1, bf16[256,1280]{1,0:T(8,128)(2,1)} %refs_1_.1, ...), custom_call_target="tpu_custom_call" | custom-call | tf_op jit(solution)/shard_map/pallas_call | solution.py:1335
  307.3 0.7 slice_reduce_fusion.5
  308.0 0.1 reshape_squeeze.3
  308.1 1.2 fusion.7
  309.3 0.8 fusion.8
  310.1 1.7 slice_reduce_fusion
  311.8 0.7 reshape.68
  312.5 0.7 reshape.67
  313.1 0.0 copy-start.4
  313.1 2.8 bitcast_convert_fusion
  315.9 0.0 copy-start.3
  315.9 0.0 copy-done.4
  315.9 0.8 copy.42
  316.8 0.5 copy-done.3
  317.3 0.8 copy.43
  318.1 0.0 copy-done.2
  318.1 0.9 copy.44
  319.0 0.0 copy-done.1
  319.0 0.9 copy.45
  319.9 0.0 copy-done
  319.9 0.9 copy.46
  (10 shorter events, 0.1 us)
Async XLA Ops:
  7.9 3.9 %copy-start.5 = (bf16[160,1280]{1,0:T(8,128)(2,1)S(1)}, bf16[160,1280]{1,0:T(8,128)(2,1)}, u32[]{:S(2)}) copy-start(bf16[160,1280]{1,0:T(8,128)(2,1)} %param.22) | copy-start | bytes 1228804
  11.9 1.0 copy-start.6
  313.1 2.8 copy-start.4
  315.9 1.3 copy-start.3
  315.9 2.2 copy-start.2
  317.3 1.7 copy-start.1
  318.1 1.8 copy-start

commit v3 on v2

--- a/solution.py
+++ b/solution.py
@@ -97,6 +97,12 @@
     def rho_back(j):
         return (j % (R // 2)) * 2 + j // (R // 2)
 
+    def turned(i, layer):
+        return (i + (R // 2) * (layer // (R // 2))) % R
+
+    def place_of(line_block, layer):
+        return turned(rho_back(line_block), layer)
+
     def device(r2, a2, b2):
         return (r2, a2 * q + b2)
 
@@ -104,7 +110,7 @@
         return device(u2 * 2 + c2, a, b2)
 
     def block_of(u2, c2, b2):
-        return rho(u2 * 2 + c2) * q + b2
+        return rho(turned(u2 * 2 + c2, a)) * q + b2
 
     def rows_of(blk):
         return pl.ds(pl.multiple_of(blk * L, L), L)
@@ -115,10 +121,13 @@
     b_off = [(b + d) % q for d in range(q)]
     u_from = [(u + U - d) % U for d in range(U)]
     b_from = [(b + q - d) % q for d in range(q)]
-    home_r, home_a = rho_back(a), rho(r)
+    home_r, home_a = place_of(a, rho(r)), rho(r)
     home = device(home_r, home_a, b)
+    origin_r, origin_a = rho_back(a), rho(turned(r, a))
+    origin = device(origin_r, origin_a, b)
     stays = jnp.logical_and(home_r == r, home_a == a)
     moves = jnp.logical_not(stays)
+    apart = jnp.logical_or(home_r != origin_r, home_a != origin_a)
     sibling = peer(u, 1 - c, b)
     above = device(r, jnp.minimum(a + 1, A - 1), b)
     below = device(r, jnp.maximum(a - 1, 0), b)
@@ -127,46 +136,10 @@
 
     links = Links(ref["send_sems"], ref["recv_sems"])
 
-    barrier = pltpu.get_barrier_semaphore()
-
-    def greet(where):
-        pl.semaphore_signal(barrier, inc=1, device_id=where, device_id_type=MESH)
-
-    for k in range(1, S):
-        g2 = (g + k) % S
-        greet(device(g2 // q, a, g2 % q))
-    for k in range(1, A):
-        greet(device(r, (a + k) % A, b))
-    pl.when(moves)(lambda: greet(home))
-    pl.semaphore_wait(barrier, S - 1 + A - 1 + jnp.where(moves, 1, 0))
-
-    swaps = []
-    for name, there in (("tokens", "tok"), ("tab", "tabs"), ("cotangent", "cot")):
-        swaps.append(links.copy(ref[name], ref[there], home, moves, moves))
-
     local_sems = ref["local_sems"]
 
     def local(src, dst, n):
         return pltpu.make_async_copy(src, dst, local_sems.at[n])
-
-    def keep_rows():
-        kept = [
-            local(ref["tokens"], ref["tok"], 0),
-            local(ref["tab"], ref["tabs"], 1),
-            local(ref["cotangent"], ref["cot"], 2),
-        ]
-        for copy in kept:
-            copy.start()
-        for copy in kept:
-            copy.wait()
-
-    swaps[0].start()
-    swaps[1].start()
-
-    wq, wqt, wcat = ref["wq"], ref["wqt"], ref["wcat"]
-
-    def wq_rows(a2, b2):
-        return pl.ds(pl.multiple_of((a2 * q + b2) * SR, 16), SR)
 
     def near(src, name, n):
         if dims["fits"] or name == "q_rows":
@@ -176,12 +149,93 @@
         copy.wait()
         return ref[name]
 
-    own_wq = local(wcat.at[g], wq.at[wq_rows(a, b)], 3)
-    own_wq.start()
+    def shard_rows(a2, b2):
+        return pl.ds(pl.multiple_of((a2 * q + b2) * SR, 16), SR)
+
+    w3 = ref["w3"]
+    names = ("w_query", "w_key", "w_value")
+    parts = [ref[name].at[pl.ds(0, SR)] for name in ("hid", "ffin", "outb")]
+    near_parts = [local(ref[names[n]], parts[n], n) for n in range(3)]
+    names = ("w_out", "w_up", "w_down")
+    own_shards = [local(ref[names[w]], w3.at[w, shard_rows(a, b)], 4 + w) for w in range(3)]
+    near_rows = [local(ref["tokens"], ref["otok"], 3), local(ref["cotangent"], ref["og"], 7)]
+    for copy in near_rows[:1] + near_parts + own_shards + near_rows[1:]:
+        copy.start()
+
+    barrier = pltpu.get_barrier_semaphore()
+
+    def greet(where):
+        pl.semaphore_signal(barrier, inc=1, device_id=where, device_id_type=MESH)
+
+    for k in range(1, S):
+        g2 = (g + k) % S
+        greet(device(g2 // q, a, g2 % q))
+    for k in range(1, A):
+        greet(device(r, (a + k) % A, b))
+    spread_out = [(u2, k) for u2 in u_off[1:] for k in range(1, A)] if U * A <= 16 else []
+    for u2, k in spread_out:
+        greet(device(u2 * 2 + c, (a + k) % A, b))
+    pl.when(moves)(lambda: greet(home))
+    pl.when(apart)(lambda: greet(origin))
+
+    gains, biascat, qgain, tab = ref["gains"], ref["biascat"], ref["qgain"], ref["tab"]
+    rows = ("gain_attn", "gain_ff", "bias_out", "bias_up", "bias_down", "bias_query", "bias_value")
+    for n, name in enumerate(rows):
+        gains[n : n + 1, :] = ref[name][...].reshape(1, D)
+    segments = dims["segments"]
+    tab[...] = jnp.zeros((8, 128), F32)
+    tab[0:1, 0:segments] = ref["lengths"][...].astype(F32)
+    tab[1:2, 0:segments] = ref["parents"][...].astype(F32)
+    biascat[...] = jnp.zeros((8, CW), F32)
+
+    def bias_slice(k):
+        biascat[0:1, 0:E] = gains[5:6, k * E : (k + 1) * E]
+        biascat[0:1, 2 * E : 3 * E] = gains[6:7, k * E : (k + 1) * E]
+
+    for k in range(S):
+        pl.when(g == k)(functools.partial(bias_slice, k))
+    scale = ref["query_scale"][...].reshape(1, HD)
+    soft = jnp.maximum(scale, 0.0) + jnp.log(1.0 + jnp.exp(-jnp.abs(scale)))
+    qgain[...] = jnp.ones((8, CW), F32)
+    for hd in range(HG):
+        qgain[0:1, hd * HD : (hd + 1) * HD] = soft * (query_base / math.sqrt(HD))
+
+    wq, wqt, wcat = ref["wq"], ref["wqt"], ref["gall"]
+    for copy in near_parts:
+        copy.wait()
+
+    def cut_columns(r2):
+        for b2 in range(q):
+            first = (r2 * q + b2) * E
+            for n in range(3):
+                wcat[b2, :, n * E : (n + 1) * E] = parts[n][:, first : first + E]
+            if CW > 3 * E:
+                wcat[b2, :, 3 * E : CW] = jnp.zeros((SR, CW - 3 * E), BF16)
+
+    for r2 in range(R):
+        pl.when(r == r2)(functools.partial(cut_columns, r2))
+    wq[shard_rows(a, b), :] = wcat[b]
+    others = S - 1 + A - 1 + len(spread_out) + jnp.where(moves, 1, 0) + jnp.where(apart, 1, 0)
+    pl.semaphore_wait(barrier, others)
+
+    swaps = []
+    for copy in near_rows:
+        copy.wait()
+    for name, there in (("otok", "tok"), ("tab", "tabs"), ("og", "cot")):
+        swaps.append(links.copy(ref[name], ref[there], home, moves, moves))
+
+    def keep_rows():
+        for name, there in (("otok", "tok"), ("tab", "tabs"), ("og", "cot")):
+            ref[there][...] = ref[name][...]
+
+    swaps[1].start()
+    swaps[0].start()
+
+    wq_rows = shard_rows
     wcat_b = {}
     for db in range(1, q):
         wcat_b[db] = links.copy(
-            wcat.at[r * q + b_off[db]], wq.at[wq_rows(a, b)], device(r, a, b_off[db])
+            wcat.at[b_off[db]], wq.at[wq_rows(a, b)], device(r, a, b_off[db])
         )
         wcat_b[db].start()
     up_q, down_q = {}, {}
@@ -198,7 +252,6 @@
                 wq.at[slot], wq.at[slot], below,
                 jnp.logical_and(a + k <= A - 1, a > 0), a + 1 + k <= A - 1,
             )
-    own_wq.wait()
     up_q[0, 0].start()
     down_q[0, 0].start()
 
@@ -210,23 +263,18 @@
                 up_q[k + 1, db].start()
                 down_q[k + 1, db].start()
 
-    w3 = ref["w3"]
-    shards = (ref["w_out"], ref["w_up"], ref["w_down"])
-
-    def shard_rows(a2, b2):
-        return pl.ds(pl.multiple_of((a2 * q + b2) * SR, 16), SR)
-
     def piece_rows(a2, b2, u2):
         if H == 1:
             return shard_rows(a2, b2)
         return pl.ds(pl.multiple_of((a2 * q + b2) * SR + u2 * SRH, 16), SRH)
 
-    own_shards = [local(shards[w], w3.at[w, shard_rows(a, b)], 4 + w) for w in range(3)]
-    for copy in own_shards:
-        copy.start()
     for copy in own_shards:
         copy.wait()
     pl.when(stays)(keep_rows)
+
+    def b_then_u(u2, w):
+        return u2 % 2 != a % 2 if w < 2 else False
+
     up_w, down_w, side_w, own_w, core_w, core_own = {}, {}, {}, {}, {}, {}
     slots = [sign * k for k in range(1, A) for sign in (1, -1)]
     for w in range(3):
@@ -250,13 +298,17 @@
                 for du in range(1, U):
                     side_w[w, slot, du, 0] = links.copy(at, at, peer(u_off[du], c, b), valid, valid)
                     for db in range(1, q):
-                        if (slot + w) % 2:
-                            passed = w3.at[w, piece_rows(a0, b_from[db], u), own_half]
-                            to = peer(u_off[du], c, b)
-                        else:
-                            passed = w3.at[w, piece_rows(a0, b, u_from[du]), own_half]
-                            to = peer(u, c, b_off[db])
-                        side_w[w, slot, du, db] = links.copy(passed, passed, to, valid, valid)
+                        sent, came = b_then_u(u, w), b_then_u(u_from[du], w)
+                        at = w3.at[w, piece_rows(a0, b_from[db], u), own_half]
+                        side_w[w, slot, du, db] = links.copy(
+                            at, at, peer(u_off[du], c, b),
+                            jnp.logical_and(valid, sent), jnp.logical_and(valid, came),
+                        )
+                        at = w3.at[w, piece_rows(a0, b, u_from[du]), own_half]
+                        other = jnp.logical_and(valid, jnp.logical_not(came))
+                        side_w[w, slot, du, -db] = links.copy(
+                            at, at, peer(u, c, b_off[db]), other, other
+                        )
             at = w3.at[w, pl.ds(pl.multiple_of(a0 * q * SR, 16), q * SR), own_half]
             core_w[w, slot] = links.copy(at, at, sibling, valid, valid)
         for db in range(1, q):
@@ -297,6 +349,7 @@
                     side_w[w, slot, du, 0].arrived()
                     for db in range(1, q):
                         side_w[w, slot, du, db].start()
+                        side_w[w, slot, du, -db].start()
 
     def w3_core(w, k):
         for slot in (-(k + 1), k + 1):
@@ -304,6 +357,7 @@
                 for du in range(1, U):
                     for db in range(1, q):
                         side_w[w, slot, du, db].arrived()
+                        side_w[w, slot, du, -db].arrived()
             core_w[w, slot].start()
 
     def w3_whole(w):
@@ -313,7 +367,6 @@
             core_w[w, slot].arrived()
 
     tok, cot, xa = ref["tok"], ref["cot"], ref["xa"]
-    gains = ref["gains"]
     gain_attn, gain_ff = gains[0:1, :], gains[1:2, :]
     STEP = 32
 
@@ -343,6 +396,12 @@
                 at = xa.at[half_rows(block_of(u_from[du], c, b_from[db]), h)]
                 sib_x[h, du, db] = links.copy(at, at, sibling)
 
+    for db in range(1, q):
+        wcat_b[db].arrived()
+        up_q[0, db].start()
+        down_q[0, db].start()
+    for w in range(3):
+        w3_line(w, -1)
     swaps[0].arrived()
     for h in range(2):
 
@@ -366,11 +425,7 @@
         for moved in [m for (h2, *_), m in own_x.items() if h2 == h]:
             moved.start()
         sib_x[h, 0, 0].start()
-
-    for db in range(1, q):
-        wcat_b[db].arrived()
-        up_q[0, db].start()
-        down_q[0, db].start()
+    wq_pass(0)
 
     swaps[1].arrived()
     lane = lax.broadcasted_iota(jnp.int32, (LABELS, 128), 1)
@@ -381,7 +436,6 @@
     lane = lax.broadcasted_iota(jnp.int32, (128, 128), 1)
     row = lax.broadcasted_iota(jnp.int32, (128, 128), 0)
     parents = jnp.broadcast_to(ref["tabs"][1:2, :], (128, 128))
-    segments = dims["segments"]
     is_parent = (parents == row.astype(F32)) & (lane > 0) & (lane < segments)
     reach = jnp.where((lane == row) | is_parent, 1.0, 0.0)
     for _ in range(max(1, (segments - 1).bit_length())):
@@ -398,7 +452,10 @@
         for db in range(1, q):
             pass_x[1, du, db].start()
         sib_x[1, du, 0].start()
-    wq_pass(0)
+    for k in range(1, A - 2):
+        wq_pass(k)
+    for w in range(3):
+        w3_line(w, 0)
     for db in range(1, q):
         own_x[1, 0, db].arrived()
         sib_x[1, 0, db].start()
@@ -407,10 +464,9 @@
         sib_x[0, du, 0].start()
     for w in range(3):
         w3_side(w, -1)
-    for k in range(1, A - 2):
-        wq_pass(k)
-    for w in range(3):
-        w3_line(w, -1)
+    if A > 2:
+        for w in range(3):
+            w3_line(w, 1)
     for h in range(2):
         for du in range(1, U):
             for db in range(1, q):
@@ -424,8 +480,8 @@
         return carried
 
     lax.fori_loop(0, NW, turn_wq, 0)
-    bias_col = jnp.transpose(ref["biascat"][g])[:, 0:1]
-    qgain_col = jnp.transpose(ref["qgain"][...])[:, 0:1]
+    bias_col = jnp.transpose(biascat[...])[:, 0:1]
+    qgain_col = jnp.transpose(qgain[...])[:, 0:1]
     qkvf, qpre, qt, keys, kt, vals, vt = (
         ref[k] for k in ("qkvf", "qpre", "qt", "keys", "kt", "vals", "vt")
     )
@@ -473,7 +529,7 @@
     o_slot = pl.ds(pl.multiple_of(g * E, 16), E)
 
     def o_copy(block):
-        r2, b2 = rho_back(block // q), block % q
+        r2, b2 = place_of(block // q, a), block % q
         index = first_o + (r2 * q + b2 + S - g) % S
         return links.copy(
             otb.at[:, rows_of(block)], oa.at[o_slot], device(r2, a, b2), index=index, keep=False
@@ -485,17 +541,27 @@
         jnp.int32, (SQ, SQ), 1
     )
     for w in range(3):
-        w3_line(w, 0)
+        w3_side(w, 0)
 
     def after_block(i):
-        for w in range(3):
-            if i == 1:
-                w3_side(w, 0)
-            elif i == 2 and A > 2:
-                w3_line(w, 1)
-            elif i == 3 and A > 2:
-                w3_side(w, 1)
-                w3_core(w, 0)
+        if A <= 2:
+            return
+        if i == 0:
+            for w in range(3):
+                w3_line(w, 2)
+        elif i == 1:
+            w3_core(0, 0)
+            w3_side(0, 1)
+            w3_core(1, 0)
+        elif i == 2:
+            w3_side(1, 1)
+            w3_core(2, 0)
+            w3_core(0, 1)
+            w3_side(2, 1)
+        elif i == 3:
+            w3_side(0, 2)
+            w3_core(1, 1)
+            w3_side(1, 2)
 
     def wide_rows(i):
         return pl.ds(pl.multiple_of(i * SQ, SQ), SQ)
@@ -545,16 +611,12 @@
 
             pl.when(block == blk)(keep_block)
             pl.when(block != blk)(lambda block=block: o_copy(block).start())
-        for j in range(1, 4):
+        for j in range(4):
             pl.when(i == j)(functools.partial(after_block, j))
         return carried
 
     lax.fori_loop(0, S // PAIR, attend, 0)
-    if A > 2:
-        for w in range(3):
-            w3_line(w, 2)
     swaps[2].start()
-
     def o_arrived(k, carried):
         links.copy(
             otb.at[:, rows_of(0)], oa.at[o_slot], sibling, index=first_o + k, keep=False
@@ -562,38 +624,39 @@
         return carried
 
     lax.fori_loop(1, S, o_arrived, 0)
-    for w in range(3):
+    def w3_rest(w):
         if A > 2:
-            w3_core(w, 1)
-            w3_side(w, 2)
+            if w == 2:
+                w3_core(w, 1)
+                w3_side(w, 2)
+            w3_core(w, 2)
         else:
-            w3_side(w, 0)
             w3_core(w, 0)
-
-    def o_sent(i, carried):
-        pl.when(i != blk)(lambda: o_copy(i).sent())
-        return carried
-
-    otok, mid, ffin, up, hid, outb = (ref[k] for k in ("otok", "mid", "ffin", "up", "hid", "outb"))
-    ug, fg, mg, og, mgt = (ref[k] for k in ("ug", "fg", "mg", "og", "mgt"))
-    small = ref["small"]
-
-    def tile(n):
-        return pl.ds(pl.multiple_of(n * W, W), W)
-
-    def turn_o(n, carried):
-        otok[:, tile(n)] = oa[tile(n), :].T
-        return carried
-
-    lax.fori_loop(0, NW, turn_o, 0)
-    for w in range(3):
-        if A > 2:
-            w3_core(w, 2)
         for k in range(3, A - 1):
             w3_line(w, k)
             w3_side(w, k)
             w3_core(w, k)
-    w3_whole(0)
+        w3_whole(w)
+
+    def o_sent(i, carried):
+        pl.when(i != blk)(lambda: o_copy(i).sent())
+        return carried
+
+    otok, mid, ffin, up, hid, outb = (ref[k] for k in ("otok", "mid", "ffin", "up", "hid", "outb"))
+    ug, fg, mg, og, mgt = (ref[k] for k in ("ug", "fg", "mg", "og", "mgt"))
+    small = ref["small"]
+
+    def tile(n):
+        return pl.ds(pl.multiple_of(n * W, W), W)
+
+    def turn_o(n, carried):
+        otok[:, tile(n)] = oa[tile(n), :].T
+        return carried
+
+    swaps[0].sent()
+    links.copies.remove(swaps[0])
+    lax.fori_loop(0, NW, turn_o, 0)
+    w3_rest(0)
 
     def out_step(n, carried):
         added = dot(otok[...], w3[0, :, tile(n)]) + gains[2:3, tile(n)]
@@ -611,7 +674,7 @@
         return carried
 
     lax.fori_loop(0, L // STEP, ff_norm, 0)
-    w3_whole(1)
+    w3_rest(1)
 
     def up_step(n, carried):
         pre = dot(ffin[...], w3[1, :, tile(n)]) + gains[3:4, tile(n)]
@@ -620,7 +683,7 @@
         return carried
 
     lax.fori_loop(0, NW, up_step, 0)
-    w3_whole(2)
+    w3_rest(2)
 
     def down_step(n, carried):
         added = dot(hid[...], w3[2, :, tile(n)]) + gains[4:5, tile(n)]
@@ -628,7 +691,7 @@
         return carried
 
     lax.fori_loop(0, NW, down_step, 0)
-    back_out = links.copy(outb, ref["out"], home, moves, moves)
+    back_out = links.copy(outb, ref["out"], origin, moves, moves)
     back_out.start()
 
     def keep_out():
@@ -638,6 +701,8 @@
 
     pl.when(stays)(keep_out)
     swaps[2].arrived()
+    swaps[2].sent()
+    links.copies.remove(swaps[2])
     small[...] = jnp.zeros_like(small)
 
     def up_back(n, carried):
@@ -701,7 +766,7 @@
         for where in writers:
             pl.semaphore_signal(sem, inc=1, device_id=where, device_id_type=MESH)
 
-    for group in (up_w, down_w, side_w, own_w, core_w, core_own):
+    for group in (wcat_b, up_w, down_w, side_w, own_w, core_w, core_own):
         for moved in group.values():
             moved.sent()
             links.copies.remove(moved)
@@ -729,19 +794,9 @@
 
         lax.fori_loop(0, S, step, 0)
 
-    weight_grad(0, None, og)
-    pl.semaphore_wait(freed, len(writers))
-    core_g[0].start()
-    weight_grad(2, hid, cot)
-    core_g[2].start()
-    weight_grad(1, ffin, ug)
-    core_g[1].start()
-
     def m_arrived(k, carried):
         m_copy(k).arrived()
         return carried
-
-    lax.fori_loop(1, S, m_arrived, 0)
 
     A2 = A // 2
     u_rows = [pl.ds(pl.multiple_of(v * SRH, 16), SRH) for v in u_off]
@@ -749,8 +804,8 @@
     qm, um = q - 1, U - 1
 
     def t1b(w, db, a2):
-        at = ((w * qm + db - 1) * A2 + a2) * SR
-        assert at + SR <= D
+        at = D - 3 * qm * A2 * SR + ((w * qm + db - 1) * A2 + a2) * SR
+        assert at >= 0
         return w3.at[1, at : at + SR, DH:D]
 
     def t1u(w, du, a2, b2):
@@ -833,51 +888,47 @@
                     second_u[w, du, a2].arrived()
                     add_into(rc.at[w, a2, b, my_rows], t2u(w, du, a2))
 
+    weight_grad(0, None, og)
+    pl.semaphore_wait(freed, len(writers))
+    core_g[0].start()
+    weight_grad(2, hid, cot)
+    core_g[2].start()
+    core_sum(0)
+    weight_grad(1, ffin, ug)
+    core_g[1].start()
+    core_sum(2)
+    lax.fori_loop(1, S, m_arrived, 0)
+
+    assert A & (A - 1) == 0
+    strides = [1 << n for n in range(A.bit_length() - 1)]
+
+    def across(k):
+        return a + k - 2 * k * (a // k % 2)
+
     class Line:
-        def __init__(self, part, landed):
-            self.part, self.landed = part, landed
-            self.first_up, self.first_down = links.block(A), links.block(A)
-
-        def copy(self, d, upward):
-            slot = jnp.where(d == a + 1, A, d) if upward else d
-            return links.copy(
-                self.part(d),
-                self.landed(slot),
-                above if upward else below,
-                index=(self.first_up if upward else self.first_down) + d,
-                keep=False,
-            )
-
-        def begin(self):
-            for k in range(1, A):
-                pl.when(a == 0)(lambda k=k: self.copy(A - k, True).make().start())
-                pl.when(a == A - 1)(lambda k=k: self.copy(k - 1, False).make().start())
-
-        def step(self, t):
-            for upward in (True, False):
-                d = A - 1 + a - t if upward else a + t - (A - 1)
-                if upward:
-                    takes = (a > 0) & (d >= a) & (d <= A - 1)
-                    passes = takes & (d > a)
-                    slot = jnp.where(d == a, A, d)
-                else:
-                    takes = (a < A - 1) & (d <= a) & (d >= 0)
-                    passes = takes & (d < a)
-                    slot = d
-                d = jnp.clip(d, 0, A - 1)
-                slot = jnp.clip(slot, 0, A)
-
-                def take(d=d, upward=upward, slot=slot):
-                    self.copy(d, upward).make().wait_recv()
-                    add_into(self.part(d), near(self.landed(slot), self.near_name, 7))
-
-                pl.when(takes)(take)
-                pl.when(passes)(lambda d=d, upward=upward: self.copy(d, upward).make().start())
-
-        def finish(self):
-            for d in range(A):
-                pl.when(a < d)(lambda d=d: self.copy(d, True).make().wait_send())
-                pl.when(a > d)(lambda d=d: self.copy(d, False).make().wait_send())
+        def __init__(self, part, landed, near_name):
+            self.part, self.landed, self.near_name, self.steps = part, landed, near_name, []
+            slot = 0
+            for k in strides:
+                step = []
+                for m in range(A // (2 * k)):
+                    mine = a % (2 * k) + 2 * k * m
+                    theirs = across(k) % (2 * k) + 2 * k * m
+                    copy = links.copy(part(theirs), landed(slot), device(r, across(k), b))
+                    step.append((copy, mine, slot))
+                    slot += 1
+                self.steps.append(step)
+
+        def begin(self, n=0):
+            for copy, _, _ in self.steps[n]:
+                copy.start()
+
+        def step(self, n):
+            for copy, mine, slot in self.steps[n]:
+                copy.arrived()
+                add_into(self.part(mine), near(self.landed(slot), self.near_name, 7))
+            if n + 1 < len(self.steps):
+                self.begin(n + 1)
 
     cu = ref["cu"]
     lines = []
@@ -886,9 +937,9 @@
             Line(
                 lambda d, w=w: rc.at[w, d, b, my_rows],
                 lambda slot, w=w: cu.at[slot, w],
+                "c_rows",
             )
         )
-        lines[-1].near_name = "c_rows"
 
     delta, dqt, dqkvt = ref["delta"], ref["dqt"], ref["dqkvt"]
     for hd in range(HG):
@@ -896,31 +947,24 @@
         total = jnp.sum(dot_t[head, :].astype(F32) * ot[head, :], axis=0, keepdims=True)
         delta[hd, :, :] = jnp.broadcast_to(total, (8, T))
     dqt[...] = jnp.zeros_like(dqt)
-    core_sum(0)
-
-    def after_back(j):
-        if j == 0:
-            core_sum(1)
-            core_sum(2)
-        elif j == 1:
-            side_sum_1(0)
-        elif j == 2:
-            side_sum_1(1)
-            side_sum_2(0)
-            lines[0].begin()
-        elif j == 3:
-            side_sum_1(2)
-            side_sum_2(1)
-            lines[1].begin()
-
-    def attend_back(j, carried):
-        here = wide_rows(j)
-
-        def query_block(i, state, on_diagonal):
-            cols = wide_rows(i)
-            result = []
+    NB = S // PAIR
+    starts = [sum(NB - k for k in range(j)) for j in range(NB)]
+    pairs = NB * (NB + 1) // 2
+    jobs = {
+        2: [lambda: core_sum(1), lambda: release(freed_again)],
+        min(3, pairs - 2): [lambda: side_sum_1(0)],
+        min(7, pairs - 2): [lambda: side_sum_1(2)],
+    }
+    dkt, dvt = ref["dkt"], ref["dvt"]
+
+    def attend_back(n, carried):
+        j = sum(jnp.where(n >= start, 1, 0) for start in starts[1:])
+        start = sum(jnp.where(n >= starts[k], starts[k] - starts[k - 1], 0) for k in range(1, NB))
+        i = n - start + j
+        here, cols = wide_rows(j), wide_rows(i)
+
+        def block(on_diagonal):
             for hd in range(HG):
-                dk, dv = state[hd]
                 head = pl.ds(hd * HD, HD)
                 score = dot(keys[hd, here, :], qt[hd, :, cols])
                 if on_diagonal:
@@ -929,24 +973,33 @@
                 d_out = dot_t[head, cols]
                 dp = dot(vals[hd, here, 0:HD], d_out)
                 ds = (p * (dp - delta[hd, 0:1, cols])).astype(BF16)
-                dv = dv + dot_nt(d_out, p.astype(BF16))
-                dk = dk + dot_nt(qt[hd, 0:HD, cols], ds)
+                dv = dot_nt(d_out, p.astype(BF16))
+                dk = dot_nt(qt[hd, 0:HD, cols], ds)
+                if on_diagonal:
+                    dvt[head, :], dkt[head, :] = dv, dk
+                else:
+                    dvt[head, :] += dv
+                    dkt[head, :] += dk
                 dqt[head, cols] += dot(kt[hd, :, here], ds)
-                result.append((dk, dv))
-            return tuple(result)
-
-        zero = jnp.zeros((HD, SQ), F32)
-        state = query_block(j, tuple((zero, zero) for _ in range(HG)), True)
-        state = lax.fori_loop(j + 1, S // PAIR, functools.partial(query_block, on_diagonal=False), state)
-        for hd in range(HG):
-            dk, dv = state[hd]
-            dqkvt[pl.ds(E + hd * HD, HD), here] = dk.astype(BF16)
-            dqkvt[pl.ds(2 * E + hd * HD, HD), here] = dv.astype(BF16)
-        for n in range(4):
-            pl.when(j == n)(functools.partial(after_back, n))
-        return carried
-
-    lax.fori_loop(0, S // PAIR, attend_back, 0)
+
+        pl.when(i == j)(lambda: block(True))
+        pl.when(i != j)(lambda: block(False))
+
+        def keep():
+            dqkvt[E : 2 * E, here] = dkt[...].astype(BF16)
+            dqkvt[2 * E : 3 * E, here] = dvt[...].astype(BF16)
+
+        pl.when(i == NB - 1)(keep)
+        for m, todo in jobs.items():
+
+            def run(todo=todo):
+                for job in todo:
+                    job()
+
+            pl.when(n == m)(run)
+        return carried
+
+    lax.fori_loop(0, pairs, attend_back, 0)
     if CW > 3 * E:
         dqkvt[3 * E :, :] = jnp.zeros((CW - 3 * E, T), BF16)
 
@@ -966,9 +1019,10 @@
     lax.fori_loop(0, NW, qkv_grad, 0)
     QR = q * SR
     line_q = Line(
-        lambda d: gq.at[pl.ds(pl.multiple_of(d * QR, 16), QR)], lambda slot: cqu.at[slot]
+        lambda d: gq.at[pl.ds(pl.multiple_of(d * QR, 16), QR)],
+        lambda slot: cqu.at[slot],
+        "q_rows",
     )
-    line_q.near_name = "q_rows"
     line_q.begin()
 
     for group in (own_x, pass_x, sib_x):
@@ -976,6 +1030,56 @@
             moved.sent()
             links.copies.remove(moved)
 
+    ones = jnp.ones((8, T), BF16)
+    head_sums = dot_nt(ones, dqkvt[...])
+    small[pl.ds(8 + g, 1), 0:CW] = head_sums[0:1]
+    small[5:6, 0:E] = jnp.transpose(jnp.broadcast_to(scale_terms, (E, 128)))[0:1, :]
+    sums, landed, late, late_landed = (ref[k] for k in ("sums", "landed", "late", "late_landed"))
+
+    class Total:
+        def __init__(self, held, arrivals, stages):
+            self.held, self.arrivals, self.stages, count = held, arrivals, [], 0
+            for n, stage in enumerate(stages):
+                moves_n = []
+                for to in stage:
+                    copy = links.copy(held.at[n], arrivals.at[count], to)
+                    moves_n.append((copy, count))
+                    count += 1
+                self.stages.append(moves_n)
+
+        def begin(self, n):
+            for moved, _ in self.stages[n]:
+                moved.start()
+
+        def end(self, n):
+            total = self.held[n]
+            for moved, at in self.stages[n]:
+                moved.arrived()
+                total = total + self.arrivals[at]
+            self.held[n + 1] = total
+
+    on_b = [peer(u, c, b_off[db]) for db in range(1, q)]
+    on_u = [peer(u_off[du], c, b) for du in range(1, U)]
+    on_a = [[device(r, across(k), b)] for k in strides]
+    total = Total(sums, landed, on_a + [on_b, on_u, [sibling]])
+    line_all = [device(r, (a + k) % A, b) for k in range(1, A)]
+    wide_u = [device(u2 * 2 + c, (a + k) % A, b) for u2 in u_off for k in range(A)][1:]
+    late_stages = [wide_u] if U * A <= 16 else [line_all, on_u]
+    late_total = Total(late, late_landed, late_stages + [on_b, [sibling]])
+
+    def late_step(n):
+        late_total.end(n)
+        if n + 1 < len(late_total.stages):
+            late_total.begin(n + 1)
+
+    sums[0] = small[...]
+    total.begin(0)
+
+    def total_step(n):
+        total.end(n)
+        if n + 1 < len(total.stages):
+            total.begin(n + 1)
+
     ags, arc = ref["ags"], ref["arc"]
 
     def slot_of(n, rows):
@@ -983,14 +1087,21 @@
         return w3.at[page, row : row + rows]
 
     order = [(u2, b2) for u2 in range(U) for b2 in range(q)]
-    slots_used = 2 * U * q
+    taken = {0: 0, 1: 0, 2: 0}
+    if H > 1:
+        taken[2] = 3 * um * A2 * q * SRH
+    usable = [
+        n
+        for n in range(2 * U * q, 3 * D // HALF)
+        if n * HALF % D >= taken[n * HALF // D]
+        and (n * HALF // D != 1 or n * HALF % D + HALF <= D - 3 * qm * A2 * SR)
+    ]
     core_a = {}
     for n, (u2, b2) in enumerate(order):
         core_a[u2, b2] = links.copy(ags.at[pl.ds(n * L, L)], slot_of(2 * n, L), sibling)
     dtok = ref["dtok"]
-    side_sum_2(2)
-    lines[2].begin()
-    release(freed_again)
+    side_sum_2(0)
+    lines[0].begin()
     pl.semaphore_wait(freed_again, len(writers))
 
     def partial_rows(m, carried, others):
@@ -1016,10 +1127,7 @@
     afb, afu, asb, asu, landing = {}, {}, {}, {}, {}
 
     def land(key):
-        nonlocal slots_used
-        landing[key] = slot_of(slots_used, HALF)
-        slots_used += 1
-        assert slots_used * HALF <= 3 * D
+        landing[key] = slot_of(usable.pop(0), HALF)
         return landing[key]
 
     for db in range(1, q):
@@ -1040,12 +1148,18 @@
 
         lax.fori_loop(0, count // STEP, step, 0)
 
+    side_sum_2(2)
+    lines[2].begin()
+    side_sum_1(1)
     for u2, b2 in order:
         core_a[u2, b2].arrived()
 
         add_rows(arc.at[rows_of(u2 * q + b2)], slot_of(2 * order.index((u2, b2)), L), L)
     for moved in list(afb.values()) + list(afu.values()):
         moved.start()
+    lines[0].step(0)
+    line_q.step(0)
+    lines[2].step(0)
 
     for db in range(1, q):
         for u2 in range(U):
@@ -1057,17 +1171,80 @@
             add_rows(part(u, b2, 1), landing["fu", du, b2], HALF)
     for moved in list(asb.values()) + list(asu.values()):
         moved.start()
-    line_q.step(1)
-    for t in range(1, A):
-        for line in lines:
-            line.step(t)
-        if t > 1:
-            line_q.step(t)
-
-    ones = jnp.ones((8, T), BF16)
-    head_sums = dot_nt(ones, dqkvt[...])
-    small[pl.ds(8 + g, 1), 0:CW] = head_sums[0:1]
-    small[5:6, 0:E] = jnp.transpose(jnp.broadcast_to(scale_terms, (E, 128)))[0:1, :]
+
+    wide, q_across, q_core = {}, [], []
+    for db in range(1, q):
+        at = gq.at[pl.ds(pl.multiple_of(a * QR + b_off[db] * SR, 16), SR)]
+        wide[db] = links.copy(at, gall.at[g], device(r, a, b_off[db]))
+    here = pl.ds(r * q, q)
+    for du in range(1, U):
+        q_across.append(links.copy(gall.at[here], gall.at[here], peer(u_off[du], c, b)))
+    for du in range(U):
+        here = pl.ds((u_from[du] * 2 + c) * q, q)
+        q_core.append(links.copy(gall.at[here], gall.at[here], sibling))
+
+    def own_q():
+        for db in range(1, q):
+            wide[db].start()
+        gall[g] = gq[pl.ds(pl.multiple_of(a * QR + b * SR, 16), SR), :]
+
+    def across_q():
+        for db in range(1, q):
+            wide[db].arrived()
+        for moved in q_across:
+            moved.start()
+        q_core[0].start()
+
+    def core_q():
+        for du in range(1, U):
+            q_across[du - 1].arrived()
+            q_core[du].start()
+
+    go = ref["go"]
+    spread, core_go, partials = {}, {}, {}
+    for w in range(3):
+        piece = rc.at[w, a, b, my_rows]
+        for du in range(1, U):
+            to = peer(u_off[du], c, b)
+            if H > 1:
+                spread[w, du] = links.copy(piece, go.at[w, my_rows, own_half], to)
+            else:
+                partials[w, du] = links.copy(piece, ref["ru"].at[du - 1, w], to)
+        at = go.at[w, :, own_half]
+        core_go[w] = links.copy(at, at, sibling)
+
+    def own_go(w):
+        for (w2, du), moved in partials.items():
+            if w2 == w:
+                moved.start()
+        for (w2, du), moved in partials.items():
+            if w2 == w:
+                moved.arrived()
+                moved.sent()
+                links.copies.remove(moved)
+        for (w2, du), moved in partials.items():
+            if w2 == w:
+                add_into(rc.at[w, a, b, my_rows], near(ref["ru"].at[du - 1, w], "c_rows", 7))
+        for (w2, du), moved in spread.items():
+            if w2 == w:
+                moved.start()
+        go[w, my_rows, own_half] = rc[w, a, b, my_rows]
+
+    def last_lines(w):
+        for n in range(1, len(strides)):
+            lines[w].step(n)
+        own_go(w)
+
+    def core_go_on(w):
+        for (w2, du), moved in spread.items():
+            if w2 == w:
+                moved.arrived()
+        core_go[w].start()
+
+    total_step(0)
+    side_sum_2(1)
+    lines[1].begin()
+    last_lines(0)
 
     for db in range(1, q):
         asb[db].arrived()
@@ -1075,6 +1252,7 @@
     for du in range(1, U):
         asu[du].arrived()
         add_rows(part(u, b, 0), landing["su", du], HALF)
+    small[0:1, :] = jnp.zeros((1, D), F32)
 
     def tok_back(i, carried):
         x = tok[strip(i), :].astype(F32)
@@ -1088,7 +1266,9 @@
         return carried
 
     lax.fori_loop(0, L // STEP, tok_back, 0)
-    back_tok = links.copy(ref["gtb"], ref["gtok"], home, moves, moves)
+    late[0] = small[0:1, :]
+    late_total.begin(0)
+    back_tok = links.copy(ref["gtb"], ref["gtok"], origin, moves, moves)
     back_tok.start()
 
     def keep_tok():
@@ -1097,108 +1277,30 @@
         kept.wait()
 
     pl.when(stays)(keep_tok)
-
-    stages = [
-        [sibling],
-        [peer(u, c, b_off[db]) for db in range(1, q)],
-        [peer(u_off[du], c, b) for du in range(1, U)],
-        [device(r, (a + k) % A, b) for k in range(1, A)],
-    ]
-    stages = [stage for stage in stages if stage]
-    sums, landed = ref["sums"], ref["landed"]
-    count, moved_small = 0, []
-    for n, stage in enumerate(stages):
-        moved_small.append(
-            [links.copy(sums.at[n], landed.at[count + k], to) for k, to in enumerate(stage)]
-        )
-        count += len(stage)
-
-    def small_stage(n):
-        for moved in moved_small[n]:
-            moved.arrived()
-        total = sums[n]
-        first = sum(len(stage) for stage in stages[:n])
-        for k in range(len(stages[n])):
-            total = total + landed[first + k]
-        return total
-
-    sums[0] = small[...]
-    for moved in moved_small[0]:
-        moved.start()
-
-    wide = {}
-    for db in range(1, q):
-        at = gq.at[pl.ds(pl.multiple_of(a * QR + b_off[db] * SR, 16), SR)]
-        wide[db] = links.copy(at, gall.at[g], device(r, a, b_off[db]))
-        wide[db].start()
-    gall[g] = gq[pl.ds(pl.multiple_of(a * QR + b * SR, 16), SR), :]
-    go = ref["go"]
-    piece = rc.at[:, a, b, my_rows]
-    spread = []
-    if H > 1:
-        at = go.at[:, my_rows, own_half]
-        for du in range(U):
-            for dc in range(2):
-                if du or dc:
-                    spread.append(links.copy(piece, at, peer(u_off[du], (c + dc) % 2, b)))
-    else:
-        partials = [
-            links.copy(piece, ref["ru"].at[du - 1], peer(u_off[du], c, b)) for du in range(1, U)
-        ]
-        for moved in partials:
-            moved.start()
-        for moved in partials:
-            moved.arrived()
-        for moved in partials:
-            moved.sent()
-            links.copies.remove(moved)
-        for k in range(U - 1):
-            for w in range(3):
-                add_into(rc.at[w, a, b, my_rows], near(ref["ru"].at[k, w], "c_rows", 7))
-        spread.append(links.copy(piece, go.at[:, :, own_half], sibling))
-    for moved in spread:
-        moved.start()
-    go[:, my_rows, own_half] = piece[...]
-
-    if len(stages) > 1:
-        sums[1] = small_stage(0)
-        for moved in moved_small[1]:
-            moved.start()
-    q_across, q_core = [], []
-    for db in range(1, q):
-        wide[db].arrived()
-    here = pl.ds(r * q, q)
-    for du in range(1, U):
-        q_across.append(links.copy(gall.at[here], gall.at[here], peer(u_off[du], c, b)))
-        q_across[-1].start()
-    for du in range(U):
-        here = pl.ds((u_from[du] * 2 + c) * q, q)
-        q_core.append(links.copy(gall.at[here], gall.at[here], sibling))
-    q_core[0].start()
-    for n in range(1, len(stages) - 1):
-        sums[n + 1] = small_stage(n)
-        for moved in moved_small[n + 1]:
-            moved.start()
-    for moved in spread:
-        moved.arrived()
-    for du in range(1, U):
-        q_across[du - 1].arrived()
-        q_core[du].start()
-    ref["g_small"][...] = small_stage(len(stages) - 1)
+    for n in range(1, len(strides)):
+        line_q.step(n)
+    own_q()
+    lines[1].step(0)
+    last_lines(2)
+    across_q()
+    core_go_on(0)
+    last_lines(1)
+    core_go_on(2)
+    late_step(0)
+    total_step(1)
+    late_step(1)
+    core_q()
+    core_go_on(1)
+    for n in range(2, len(late_total.stages)):
+        late_step(n)
+    for n in range(2, len(total.stages)):
+        total_step(n)
+    ref["g_small"][...] = sums[len(total.stages)]
+    ref["g_small"][0:1, :] = late[len(late_total.stages)]
+    for w in range(3):
+        core_go[w].arrived()
     for moved in q_core:
         moved.arrived()
-    unpacked = [ref[name].at[pl.ds(0, SR)] for name in ("mid", "up", "mg")]
-    for g2 in range(S):
-        mine = gall[g2]
-        for n in range(3):
-            unpacked[n][:, g2 * E : (g2 + 1) * E] = mine[:, n * E : (n + 1) * E].astype(F32)
-    written = [
-        local(unpacked[n], ref[name], n) for n, name in enumerate(("g_query", "g_key", "g_value"))
-    ]
-    for copy in written:
-        copy.start()
-    for copy in written:
-        copy.wait()
     back_out.arrived()
     back_tok.arrived()
 
@@ -1209,8 +1311,6 @@
         return carried
 
     lax.fori_loop(1, S, m_sent, 0)
-    for line in lines + [line_q]:
-        line.finish()
     for moved in links.copies:
         moved.sent()
     return links.used
@@ -1251,34 +1351,19 @@
     segments = lengths.shape[1]
     dims = dict(R=R, S=S, L=L, D=D, HG=HG, E=E, CW=CW, SR=SR, H=H, SRH=SRH, segments=segments)
 
-    tab = jnp.pad(
-        jnp.concatenate([lengths, parents], axis=0).astype(F32), ((0, 6), (0, 128 - segments))
-    )
-    by_group = [w.reshape(SR, S, E) for w in (w_query, w_key, w_value)]
-    wcat = jnp.pad(jnp.concatenate(by_group, axis=2), ((0, 0), (0, 0), (0, CW - 3 * E)))
-    wcat = wcat.transpose(1, 0, 2)
-    bias_rows = [bias_query.reshape(S, E), jnp.zeros((S, E), F32), bias_value.reshape(S, E)]
-    biascat = jnp.pad(jnp.concatenate(bias_rows, axis=1), ((0, 0), (0, CW - 3 * E)))
-    biascat = jnp.broadcast_to(biascat[:, None, :], (S, 8, CW))
-    query_gain = query_base * jax.nn.softplus(query_scale) / math.sqrt(HEAD_DIM)
-    qgain = jnp.pad(jnp.tile(query_gain, HG), (0, CW - E), constant_values=1.0)
-    qgain = jnp.broadcast_to(qgain[None, :], (8, CW))
-    zero_row = jnp.zeros_like(gain_attn)
-    gains = jnp.stack(
-        [gain_attn, gain_ff, bias_out, bias_up, bias_down, zero_row, zero_row, zero_row]
-    )
-
     operands = dict(
-        tokens=tokens, cotangent=cotangent, tab=tab, wcat=wcat, w_out=w_out, w_up=w_up,
-        w_down=w_down, biascat=biascat, qgain=qgain, gains=gains,
+        tokens=tokens, cotangent=cotangent, w_query=w_query, w_key=w_key, w_value=w_value,
+        w_out=w_out, w_up=w_up, w_down=w_down, lengths=lengths, parents=parents,
+        gain_attn=gain_attn, gain_ff=gain_ff, query_scale=query_scale, bias_query=bias_query,
+        bias_value=bias_value, bias_out=bias_out, bias_up=bias_up, bias_down=bias_down,
     )
     outputs = dict(
-        out=((L, D), BF16), gtok=((L, D), BF16), g_query=((SR, D), F32), g_key=((SR, D), F32),
-        g_value=((SR, D), F32), go=((3, SR, D), BF16),
-        g_small=((NS, D), F32),
+        out=((L, D), BF16), gtok=((L, D), BF16), go=((3, SR, D), BF16),
+        gall=((S, SR, CW), BF16), g_small=((NS, D), F32),
     )
     um = max(U - 1, 1)
-    peers = 1 + (q - 1) + (U - 1) + (A - 1)
+    peers = q + U + A + (U * A if U * A <= 16 else 0)
+    line_steps = A.bit_length() - 1
     scratch = dict(
         tok=((L, D), BF16), cot=((L, D), BF16), tabs=((8, 128), F32),
         wq=((D, CW), BF16), w3=((3, D, D), BF16), xa=((T, D), BF16),
@@ -1291,24 +1376,26 @@
         mg=((L, D), F32), og=((L, D), BF16), mgt=((D, L), BF16), dot_t=((E, T), BF16),
         small=((NS, D), F32), gp=((3, D, DH), BF16),
         rc=((3, A, q, SR, DH), BF16),
-        cu=((A + 1, 3, SRH, DH), BF16), delta=((HG, 8, T), F32), dqkvt=((CW, T), BF16),
+        cu=((A - 1, 3, SRH, DH), BF16), delta=((HG, 8, T), F32), dqkvt=((CW, T), BF16),
+        dkt=((E, 2 * L), F32), dvt=((E, 2 * L), F32),
+        gains=((8, D), F32), biascat=((8, CW), F32), qgain=((8, CW), F32), tab=((8, 128), F32),
         ags=((T // 2, D), BF16), arc=((T // 2, D), BF16),
         dtok=((L, CW), BF16),
-        gq=((D, CW), BF16), cqu=((A + 1, q * SR, CW), BF16),
-        gall=((S, SR, CW), BF16),
-        sums=((5, NS, D), F32), landed=((peers, NS, D), F32),
+        gq=((D, CW), BF16), cqu=((A - 1, q * SR, CW), BF16),
+        sums=((line_steps + 4, NS, D), F32), landed=((line_steps + q + U, NS, D), F32),
+        late=((5, 1, D), F32), late_landed=((peers, 1, D), F32),
     )
     if H == 1:
         scratch["ru"] = ((um, 3, SR, DH), BF16)
-    held = [jax.ShapeDtypeStruct(*v) for v in scratch.values()]
+    held = [jax.ShapeDtypeStruct(*v) for k, v in scratch.items() if k not in ("ags", "arc")]
     dims["fits"] = sum(v.size * v.dtype.itemsize for v in held) <= VMEM_BYTES - (6 << 20)
     results = len(outputs)
-    distant = ["out", "gtok", "g_query", "g_key", "g_value"]
+    distant = ["out", "gtok"]
     if dims["fits"]:
         scratch.pop("ags")
         scratch.pop("arc")
     else:
-        for name in ("xa", "cu", "ru"):
+        for name in [k for k in ("xa", "cu", "ru") if k in scratch]:
             outputs[name] = scratch.pop(name)
             distant.append(name)
         scratch["x_rows"] = ((L, D), BF16)
@@ -1330,7 +1417,7 @@
         counted[0] = layer_kernel(dims, named)
 
     whole = pl.BlockSpec(memory_space=pltpu.VMEM)
-    far = ("tokens", "cotangent", "wcat", "w_out", "w_up", "w_down")
+    far = ("tokens", "cotangent", "w_query", "w_key", "w_value", "w_out", "w_up", "w_down")
     def call(*operands):
         return pl.pallas_call(
         kernel,
@@ -1348,29 +1435,36 @@
 
     jax.eval_shape(call, *operands.values())
     made = call(*operands.values())
-    out, gtok, g_query, g_key, g_value, go, g_small = made[:results]
-    g_out, g_up, g_down = (go[w].astype(F32) for w in range(3))
-    scale = jnp.sum(g_small[5, :E].reshape(HG, HEAD_DIM), axis=0)
-    scale = scale * query_base * jax.nn.sigmoid(query_scale) / math.sqrt(HEAD_DIM)
-    by_head = g_small[8:, : 3 * E]
-    return (
-        out,
-        gtok,
-        g_query,
-        g_key,
-        g_value,
-        g_out,
-        g_up,
-        g_down,
-        g_small[0],
-        g_small[1],
-        scale,
-        by_head[:, :E].reshape(D),
-        by_head[:, 2 * E :].reshape(D),
-        g_small[2],
-        g_small[3],
-        g_small[4],
-    )
+    out, gtok, go, gall, g_small = made[:results]
+
+    def finish(out, gtok, go, gall, sums, scale, *refs):
+        made_out, made_gtok, grads, vectors = refs[0], refs[1], refs[2:8], refs[8:16]
+        made_out[...] = out[...]
+        made_gtok[...] = gtok[...]
+        for g2 in range(S):
+            mine = gall[g2]
+            for n in range(3):
+                grads[n][:, g2 * E : (g2 + 1) * E] = mine[:, n * E : (n + 1) * E].astype(F32)
+        for w in range(3):
+            grads[3 + w][...] = go[w].astype(F32)
+        for n, at in ((0, 0), (1, 1), (5, 2), (6, 3), (7, 4)):
+            vectors[n][...] = sums[at : at + 1, :].reshape(D)
+        for n, at in ((3, 0), (4, 2 * E)):
+            whole = jnp.concatenate([sums[8 + k : 9 + k, at : at + E] for k in range(S)], axis=1)
+            vectors[n][...] = whole.reshape(D)
+        terms = sum(sums[5:6, hd * HEAD_DIM : (hd + 1) * HEAD_DIM] for hd in range(HG))
+        gate = jax.nn.sigmoid(scale[...].reshape(1, HEAD_DIM)) * (query_base / math.sqrt(HEAD_DIM))
+        vectors[2][...] = (terms * gate).reshape(HEAD_DIM)
+
+    final = [((L, D), BF16)] * 2 + [((SR, D), F32)] * 6 + [((D,), F32)] * 8
+    final[10] = ((HEAD_DIM,), F32)
+    return pl.pallas_call(
+        finish,
+        out_shape=[jax.ShapeDtypeStruct(*shape) for shape in final],
+        in_specs=[whole] * 6,
+        out_specs=[whole] * 16,
+        compiler_params=pltpu.CompilerParams(vmem_limit_bytes=VMEM_BYTES),
+    )(out, gtok, go, gall, g_small, query_scale)
 
 
 def solution(mesh):

time: 325 us -> 253 us (0.78); the launches traced: 321 us -> 253 us
  Pallas kernels: 292 us -> 252 us
  local copies, waits for them, and re-layouts: 21.1 us -> 0 us
  other arithmetic: 7.31 us -> 0 us
    pallas_call x1, Pallas kernels: 292 us -> 247 us  [call(): pl.pallas_call(kernel, out_shape=[jax.ShapeDtypeStruct(*shape) for shape...]
    reshape x10 -> x0, local copies, waits for them, and re-layouts: 6.74 us -> none  [the longest x6 3.86 us: shards(): by_group = [w.reshape(SR, S, E) for w in (w_query, w_key, w_value)]]
    pallas_call x0 -> x1, Pallas kernels: none -> 5.85 us  [shards(): pl.pallas_call(finish, out_shape=[jax.ShapeDtypeStruct(*shape) for shape...]
    unnamed x19 -> x0, local copies, waits for them, and re-layouts: 4.87 us -> none
    another operation x11 -> x0, local copies, waits for them, and re-layouts: 4.36 us -> none  [the longest x8 4.19 us: shards(): jnp.stack([gain_attn, gain_ff, bias_out, bias_up, bias_down, zero_row, ze...]
    convert_element_type x2 -> x0, other arithmetic: 3.49 us -> none  [the longest x1 2.8 us: shards(): g_out, g_up, g_down = (go[w].astype(F32) for w in range(3))]
where the time goes in v3:
time: 253 us
  Pallas kernels  252 us (100%)
    pallas_call x1, Pallas kernels, call(): pl.pallas_call(kernel, out_shape=[jax.ShapeDtypeStruct(*shape) for shape...  247 us
    pallas_call x1, Pallas kernels, shards(): pl.pallas_call(finish, out_shape=[jax.ShapeDtypeStruct(*shape) for shape...  5.85 us

profile of v3, /device:TPU:1, one launch (start us, length us, event | category | flops | bytes accessed | tf_op | source)
XLA Modules:
  0.0 253.3 jit_solution(248282311356529495)
XLA Ops:
  0.7 246.6 %shard_map.297 = (bf16[256,1280]{1,0:T(8,128)(2,1)}, bf16[256,1280]{1,0:T(8,128)(2,1)}, bf16[3,160,1280]{2,1,0:T(8,128)(2,1)}, bf16[8,160,512]{2,1,0:T(8,128)(2,1)}, f32[16,1280]{1,0:T(8,128)}) custom-call(bf16[256,1280]{1,0:T(8,128)(2,1)} %refs_0_.1, bf16[256,1280]{1,0:T(8,128)(2,1)} %refs_1_.1, bf16[160,1280]{1,0:T(8,128)(2,1)} %refs_2_.1, ...), custom_call_target="tpu_custom_call" | custom-call | tf_op jit(solution)/shard_map/pallas_call | solution.py:1422
  247.3 5.9 %shard_map.298 = (bf16[256,1280]{1,0:T(8,128)(2,1)}, bf16[256,1280]{1,0:T(8,128)(2,1)}, f32[160,1280]{1,0:T(8,128)}, f32[160,1280]{1,0:T(8,128)}, f32[160,1280]{...) custom-call(bf16[256,1280]{1,0:T(8,128)(2,1)} %get-tuple-element.21., ...), custom_call_target="tpu_custom_call" | custom-call | tf_op jit(solution)/shard_map/pallas_call | solution.py:1461

commit v4 on v3

--- a/solution.py
+++ b/solution.py
@@ -19,6 +19,19 @@
 masked_score = -1e30
 LABELS = 16
 VMEM_BYTES = 64 << 20
+SECOND = (
+    "wg0", "wg2", "cs0", "wg1", "mwait", "delta", "B2", "cs2", "B6", "cs1", "B9", "release", "f2",
+    "f0", "BX", "t", "qg", "ago", "t0", "g2", "agm", "ac", "g0", "Q0", "ab", "f1", "h00", "h01",
+    "Q1", "h20", "au", "g1", "Q2", "h10", "h21", "t1", "k0", "end", "h11", "t2", "L0", "k1", "Q3",
+    "L1", "t3", "k2", "t4", "L2",
+)
+FIRST = (
+    "wcat", "tok", "carry", "n0", "wcat2", "own", "n1", "l2", "xb0", "tables", "xu0", "l1", "q0",
+    "l0", "xu1", "q1", "l20", "q2", "l10", "coth", "xb1", "xp0", "l00", "l21", "l11", "turnq",
+    "l01", "xp1", "s0", "s20", "project", "l02", "s00", "s10", "s02", "c00", "s01", "s2", "A0",
+    "l12", "cot", "c10", "A1", "A2", "l22", "s21", "s11", "s12", "c01", "c20", "A3", "s1", "AX",
+    "c02", "c12", "c11", "c21", "s22", "owait", "F0", "F1", "F2", "c22",
+)
 
 
 def dot(left, right):
@@ -128,6 +141,18 @@
     stays = jnp.logical_and(home_r == r, home_a == a)
     moves = jnp.logical_not(stays)
     apart = jnp.logical_or(home_r != origin_r, home_a != origin_a)
+    by_u = U == 2
+
+    def crosses(r2, a2):
+        layer = rho(r2)
+        return jnp.logical_and(place_of(a2, layer) // 2 != r2 // 2, layer != a2) if by_u else False
+
+    next_r = (1 - u) * 2 + c
+    next_home = device(place_of(a, rho(next_r)), rho(next_r), b)
+    carrier = device((1 - origin_r // 2) * 2 + origin_r % 2, origin_a, b)
+    i_cross, i_carry, carried_in = crosses(r, a), crosses(next_r, a), crosses(origin_r, origin_a)
+    direct = jnp.logical_and(moves, jnp.logical_not(i_cross))
+    direct_in = jnp.logical_and(moves, jnp.logical_not(carried_in))
     sibling = peer(u, 1 - c, b)
     above = device(r, jnp.minimum(a + 1, A - 1), b)
     below = device(r, jnp.maximum(a - 1, 0), b)
@@ -135,6 +160,29 @@
     other_half = pl.ds(pl.multiple_of((1 - c) * DH, 128), DH)
 
     links = Links(ref["send_sems"], ref["recv_sems"])
+    events = {}
+
+    def event(name, job):
+        events[name] = job
+
+    def play(names):
+        for name in names:
+            events.pop(name)()
+
+    def segments_of(order, first, last):
+        parts, at = {None: []}, None
+        for name in order:
+            if name[:1] == first and (name[1:].isdigit() or name == last):
+                at = name
+                parts[at] = []
+            else:
+                parts[at].append(name)
+        return parts
+
+    def start_all(*copies):
+        for moved in copies:
+            moved.start()
+
 
     local_sems = ref["local_sems"]
 
@@ -177,6 +225,9 @@
         greet(device(u2 * 2 + c, (a + k) % A, b))
     pl.when(moves)(lambda: greet(home))
     pl.when(apart)(lambda: greet(origin))
+    if by_u:
+        pl.when(i_carry)(lambda: greet(next_home))
+        pl.when(carried_in)(lambda: greet(carrier))
 
     gains, biascat, qgain, tab = ref["gains"], ref["biascat"], ref["qgain"], ref["tab"]
     rows = ("gain_attn", "gain_ff", "bias_out", "bias_up", "bias_down", "bias_query", "bias_value")
@@ -216,20 +267,63 @@
         pl.when(r == r2)(functools.partial(cut_columns, r2))
     wq[shard_rows(a, b), :] = wcat[b]
     others = S - 1 + A - 1 + len(spread_out) + jnp.where(moves, 1, 0) + jnp.where(apart, 1, 0)
+    if by_u:
+        others = others + jnp.where(i_carry, 1, 0) + jnp.where(carried_in, 1, 0)
     pl.semaphore_wait(barrier, others)
 
-    swaps = []
     for copy in near_rows:
         copy.wait()
-    for name, there in (("otok", "tok"), ("tab", "tabs"), ("og", "cot")):
-        swaps.append(links.copy(ref[name], ref[there], home, moves, moves))
+    swap_tab = links.copy(ref["tab"], ref["tabs"], home, moves, moves)
+    swap_rows, swap_cot = [], []
+    for name, there, pieces in (("otok", "tok", swap_rows), ("og", "cot", swap_cot)):
+        for h in range(2):
+            here = pl.ds(h * HALF, HALF)
+            src, dst = ref[name].at[here], ref[there].at[here]
+            piece = [links.copy(src, dst, home, direct, direct_in)]
+            if by_u:
+                lent = ref["lent_" + there].at[here]
+                piece.append(links.copy(src, lent, peer(1 - u, c, b), i_cross, i_carry))
+                piece.append(links.copy(lent, dst, next_home, i_carry, carried_in))
+            pieces.append(piece)
+
+    def swap_begin(pieces):
+        for piece in pieces:
+            for moved in piece[:2]:
+                moved.start()
+
+    def swap_carry(pieces):
+        for piece in pieces:
+            if by_u:
+                piece[1].arrived()
+                piece[2].start()
+
+    def swap_end(piece):
+        for moved in piece[0::2]:
+            moved.arrived()
+
+    def swap_sent(pieces):
+        for moved in [m for piece in pieces for m in piece[:2]]:
+            moved.sent()
+            links.copies.remove(moved)
 
     def keep_rows():
         for name, there in (("otok", "tok"), ("tab", "tabs"), ("og", "cot")):
             ref[there][...] = ref[name][...]
 
-    swaps[1].start()
-    swaps[0].start()
+
+    def tok_begin():
+        swap_tab.start()
+        swap_begin(swap_rows)
+
+    event("tok", tok_begin)
+    event("coth", lambda: start_all(*[piece[1] for piece in swap_cot if by_u]))
+    event("carry", lambda: swap_carry(swap_rows))
+
+    def cot_on():
+        start_all(*[piece[0] for piece in swap_cot])
+        swap_carry(swap_cot)
+
+    event("cot", cot_on)
 
     wq_rows = shard_rows
     wcat_b = {}
@@ -237,7 +331,6 @@
         wcat_b[db] = links.copy(
             wcat.at[b_off[db]], wq.at[wq_rows(a, b)], device(r, a, b_off[db])
         )
-        wcat_b[db].start()
     up_q, down_q = {}, {}
     for k in range(A - 1):
         for db in range(q):
@@ -252,9 +345,17 @@
                 wq.at[slot], wq.at[slot], below,
                 jnp.logical_and(a + k <= A - 1, a > 0), a + 1 + k <= A - 1,
             )
-    up_q[0, 0].start()
-    down_q[0, 0].start()
-
+
+    def wq_begin():
+        start_all(*wcat_b.values(), up_q[0, 0], down_q[0, 0])
+
+    def wq_side():
+        for db in range(1, q):
+            wcat_b[db].arrived()
+            start_all(up_q[0, db], down_q[0, db])
+
+    event("wcat", wq_begin)
+    event("wcat2", wq_side)
     def wq_pass(k):
         for db in range(q):
             up_q[k, db].arrived()
@@ -262,6 +363,9 @@
             if k + 1 < A - 1:
                 up_q[k + 1, db].start()
                 down_q[k + 1, db].start()
+
+    for k in range(A - 1):
+        event(f"q{k}", functools.partial(wq_pass, k))
 
     def piece_rows(a2, b2, u2):
         if H == 1:
@@ -317,9 +421,6 @@
             at = w3.at[w, shard_rows(a, b_from[db]), own_half]
             core_own[w, db] = links.copy(at, at, sibling)
 
-    for moved in own_w.values():
-        moved.start()
-
     def w3_line(w, k):
         if k < 0:
             up_w[w, 0].start()
@@ -359,6 +460,15 @@
                         side_w[w, slot, du, db].arrived()
                         side_w[w, slot, du, -db].arrived()
             core_w[w, slot].start()
+
+    event("own", lambda: start_all(*own_w.values()))
+    for w in range(3):
+        event(f"l{w}", functools.partial(w3_line, w, -1))
+        event(f"s{w}", functools.partial(w3_side, w, -1))
+        for k in range(A - 1):
+            event(f"l{w}{k}", functools.partial(w3_line, w, k))
+            event(f"s{w}{k}", functools.partial(w3_side, w, k))
+            event(f"c{w}{k}", functools.partial(w3_core, w, k))
 
     def w3_whole(w):
         for db in range(1, q):
@@ -396,16 +506,10 @@
                 at = xa.at[half_rows(block_of(u_from[du], c, b_from[db]), h)]
                 sib_x[h, du, db] = links.copy(at, at, sibling)
 
-    for db in range(1, q):
-        wcat_b[db].arrived()
-        up_q[0, db].start()
-        down_q[0, db].start()
-    for w in range(3):
-        w3_line(w, -1)
-    swaps[0].arrived()
-    for h in range(2):
-
-        def norm_step(i, carried, h=h):
+    def norm_half(h):
+        swap_end(swap_rows[h])
+
+        def norm_step(i, carried):
             here = pl.ds(pl.multiple_of(h * HALF + i * STEP, STEP), STEP)
             x = tok[here, :].astype(F32)
             there = pl.ds(pl.multiple_of(blk * L + h * HALF + i * STEP, STEP), STEP)
@@ -422,64 +526,61 @@
             out_of = local(ref["x_rows"].at[here], xa.at[half_rows(blk, h)], 7)
             out_of.start()
             out_of.wait()
-        for moved in [m for (h2, *_), m in own_x.items() if h2 == h]:
-            moved.start()
-        sib_x[h, 0, 0].start()
-    wq_pass(0)
-
-    swaps[1].arrived()
-    lane = lax.broadcasted_iota(jnp.int32, (LABELS, 128), 1)
-    row = lax.broadcasted_iota(jnp.int32, (LABELS, 128), 0)
-    lengths = jnp.broadcast_to(ref["tabs"][0:1, :], (LABELS, 128))
-    seg_start = jnp.sum(jnp.where(lane < row, lengths, 0.0), axis=1, keepdims=True)
-    seg_end = jnp.sum(jnp.where(lane <= row, lengths, 0.0), axis=1, keepdims=True)
-    lane = lax.broadcasted_iota(jnp.int32, (128, 128), 1)
-    row = lax.broadcasted_iota(jnp.int32, (128, 128), 0)
-    parents = jnp.broadcast_to(ref["tabs"][1:2, :], (128, 128))
-    is_parent = (parents == row.astype(F32)) & (lane > 0) & (lane < segments)
-    reach = jnp.where((lane == row) | is_parent, 1.0, 0.0)
-    for _ in range(max(1, (segments - 1).bit_length())):
-        reach = jnp.minimum(dot(reach.astype(BF16), reach.astype(BF16)), 1.0)
-    blocked = ((1.0 - reach[:LABELS, :LABELS]) * masked_score).astype(BF16)
-
-    for db in range(1, q):
-        own_x[0, 0, db].arrived()
+        start_all(*[m for (h2, *_), m in own_x.items() if h2 == h], sib_x[h, 0, 0])
+
+    def rows_on_b(h):
+        for db in range(1, q):
+            own_x[h, 0, db].arrived()
+            if h == 0:
+                start_all(*[pass_x[0, du, db] for du in range(1, U)])
+            sib_x[h, 0, db].start()
+
+    def rows_on_u(h):
         for du in range(1, U):
-            pass_x[0, du, db].start()
-        sib_x[0, 0, db].start()
-    for du in range(1, U):
-        own_x[1, du, 0].arrived()
-        for db in range(1, q):
-            pass_x[1, du, db].start()
-        sib_x[1, du, 0].start()
-    for k in range(1, A - 2):
-        wq_pass(k)
-    for w in range(3):
-        w3_line(w, 0)
-    for db in range(1, q):
-        own_x[1, 0, db].arrived()
-        sib_x[1, 0, db].start()
-    for du in range(1, U):
-        own_x[0, du, 0].arrived()
-        sib_x[0, du, 0].start()
-    for w in range(3):
-        w3_side(w, -1)
-    if A > 2:
-        for w in range(3):
-            w3_line(w, 1)
-    for h in range(2):
+            own_x[h, du, 0].arrived()
+            if h == 1:
+                start_all(*[pass_x[1, du, db] for db in range(1, q)])
+            sib_x[h, du, 0].start()
+
+    def rows_passed(h):
         for du in range(1, U):
             for db in range(1, q):
                 pass_x[h, du, db].arrived()
                 sib_x[h, du, db].start()
-    wq_pass(A - 2)
+
+    for h in range(2):
+        event(f"n{h}", functools.partial(norm_half, h))
+        event(f"xb{h}", functools.partial(rows_on_b, h))
+        event(f"xu{h}", functools.partial(rows_on_u, h))
+        event(f"xp{h}", functools.partial(rows_passed, h))
+
+    tables = {}
+
+    def make_tables():
+        swap_tab.arrived()
+        lane = lax.broadcasted_iota(jnp.int32, (LABELS, 128), 1)
+        row = lax.broadcasted_iota(jnp.int32, (LABELS, 128), 0)
+        lengths = jnp.broadcast_to(ref["tabs"][0:1, :], (LABELS, 128))
+        seg_start = jnp.sum(jnp.where(lane < row, lengths, 0.0), axis=1, keepdims=True)
+        seg_end = jnp.sum(jnp.where(lane <= row, lengths, 0.0), axis=1, keepdims=True)
+        lane = lax.broadcasted_iota(jnp.int32, (128, 128), 1)
+        row = lax.broadcasted_iota(jnp.int32, (128, 128), 0)
+        parents = jnp.broadcast_to(ref["tabs"][1:2, :], (128, 128))
+        is_parent = (parents == row.astype(F32)) & (lane > 0) & (lane < segments)
+        reach = jnp.where((lane == row) | is_parent, 1.0, 0.0)
+        for _ in range(max(1, (segments - 1).bit_length())):
+            reach = jnp.minimum(dot(reach.astype(BF16), reach.astype(BF16)), 1.0)
+        blocked = ((1.0 - reach[:LABELS, :LABELS]) * masked_score).astype(BF16)
+        tables["start"], tables["end"], tables["blocked"] = seg_start, seg_end, blocked
+
+    event("tables", make_tables)
 
     def turn_wq(i, carried):
         here = pl.ds(pl.multiple_of(i * W, W), W)
         wqt[:, here] = wq[here, :].T
         return carried
 
-    lax.fori_loop(0, NW, turn_wq, 0)
+    event("turnq", lambda: lax.fori_loop(0, NW, turn_wq, 0))
     bias_col = jnp.transpose(biascat[...])[:, 0:1]
     qgain_col = jnp.transpose(qgain[...])[:, 0:1]
     qkvf, qpre, qt, keys, kt, vals, vt = (
@@ -503,8 +604,8 @@
         qkvf[...] = dot_nt(wqt[...], x) + bias_col
         place = block * L + lax.broadcasted_iota(jnp.int32, (LABELS, L), 1)
         place = place.astype(F32)
-        onehot = jnp.where((place >= seg_start) & (place < seg_end), 1.0, 0.0)
-        far = dot(blocked, onehot.astype(BF16)).astype(BF16)
+        onehot = jnp.where((place >= tables["start"]) & (place < tables["end"]), 1.0, 0.0)
+        far = dot(tables["blocked"], onehot.astype(BF16)).astype(BF16)
         for hd in range(HG):
             head = pl.ds(hd * HD, HD)
             pre = qkvf[head, :]
@@ -522,7 +623,7 @@
             vals[hd, cols, :] = wide.T.astype(BF16)
         return carried
 
-    lax.fori_loop(0, S, project, 0)
+    event("project", lambda: lax.fori_loop(0, S, project, 0))
 
     ot, otb, lse, oa = ref["ot"], ref["otb"], ref["lse"], ref["oa"]
     first_o = links.block(S)
@@ -540,29 +641,6 @@
     diagonal = lax.broadcasted_iota(jnp.int32, (SQ, SQ), 0) <= lax.broadcasted_iota(
         jnp.int32, (SQ, SQ), 1
     )
-    for w in range(3):
-        w3_side(w, 0)
-
-    def after_block(i):
-        if A <= 2:
-            return
-        if i == 0:
-            for w in range(3):
-                w3_line(w, 2)
-        elif i == 1:
-            w3_core(0, 0)
-            w3_side(0, 1)
-            w3_core(1, 0)
-        elif i == 2:
-            w3_side(1, 1)
-            w3_core(2, 0)
-            w3_core(0, 1)
-            w3_side(2, 1)
-        elif i == 3:
-            w3_side(0, 2)
-            w3_core(1, 1)
-            w3_side(1, 2)
-
     def wide_rows(i):
         return pl.ds(pl.multiple_of(i * SQ, SQ), SQ)
 
@@ -611,33 +689,31 @@
 
             pl.when(block == blk)(keep_block)
             pl.when(block != blk)(lambda block=block: o_copy(block).start())
-        for j in range(4):
-            pl.when(i == j)(functools.partial(after_block, j))
-        return carried
-
-    lax.fori_loop(0, S // PAIR, attend, 0)
-    swaps[2].start()
+        for j in range(S // PAIR):
+            if order.get(f"A{j}"):
+                pl.when(i == j)(functools.partial(play, order[f"A{j}"]))
+        return carried
+
     def o_arrived(k, carried):
         links.copy(
             otb.at[:, rows_of(0)], oa.at[o_slot], sibling, index=first_o + k, keep=False
         ).make().wait_recv()
         return carried
 
-    lax.fori_loop(1, S, o_arrived, 0)
-    def w3_rest(w):
-        if A > 2:
-            if w == 2:
-                w3_core(w, 1)
-                w3_side(w, 2)
-            w3_core(w, 2)
-        else:
-            w3_core(w, 0)
-        for k in range(3, A - 1):
-            w3_line(w, k)
-            w3_side(w, k)
-            w3_core(w, k)
-        w3_whole(w)
-
+    event("owait", lambda: lax.fori_loop(1, S, o_arrived, 0))
+
+    names = [name for name in FIRST if name in events or name[0] in "AF"]
+    for k in range(A - 1):
+        for at, name in [("turnq", f"q{k}")] + [
+            (f"F{w}", f"{kind}{w}{k}") for w in range(3) for kind in "lsc"
+        ]:
+            if name not in names:
+                names.insert(names.index(at), name)
+    ff_order = segments_of(names, "F", "FX")
+    order = segments_of(ff_order.pop(None), "A", "AX")
+    play(order[None])
+    lax.fori_loop(0, S // PAIR, attend, 0)
+    play(order["AX"])
     def o_sent(i, carried):
         pl.when(i != blk)(lambda: o_copy(i).sent())
         return carried
@@ -653,10 +729,10 @@
         otok[:, tile(n)] = oa[tile(n), :].T
         return carried
 
-    swaps[0].sent()
-    links.copies.remove(swaps[0])
+    swap_sent(swap_rows)
     lax.fori_loop(0, NW, turn_o, 0)
-    w3_rest(0)
+    play(ff_order["F0"])
+    w3_whole(0)
 
     def out_step(n, carried):
         added = dot(otok[...], w3[0, :, tile(n)]) + gains[2:3, tile(n)]
@@ -674,7 +750,8 @@
         return carried
 
     lax.fori_loop(0, L // STEP, ff_norm, 0)
-    w3_rest(1)
+    play(ff_order["F1"])
+    w3_whole(1)
 
     def up_step(n, carried):
         pre = dot(ffin[...], w3[1, :, tile(n)]) + gains[3:4, tile(n)]
@@ -683,7 +760,8 @@
         return carried
 
     lax.fori_loop(0, NW, up_step, 0)
-    w3_rest(2)
+    play(ff_order["F2"])
+    w3_whole(2)
 
     def down_step(n, carried):
         added = dot(hid[...], w3[2, :, tile(n)]) + gains[4:5, tile(n)]
@@ -700,9 +778,9 @@
         kept.wait()
 
     pl.when(stays)(keep_out)
-    swaps[2].arrived()
-    swaps[2].sent()
-    links.copies.remove(swaps[2])
+    for piece in swap_cot:
+        swap_end(piece)
+    swap_sent(swap_cot)
     small[...] = jnp.zeros_like(small)
 
     def up_back(n, carried):
@@ -888,16 +966,23 @@
                     second_u[w, du, a2].arrived()
                     add_into(rc.at[w, a2, b, my_rows], t2u(w, du, a2))
 
-    weight_grad(0, None, og)
-    pl.semaphore_wait(freed, len(writers))
-    core_g[0].start()
-    weight_grad(2, hid, cot)
-    core_g[2].start()
-    core_sum(0)
-    weight_grad(1, ffin, ug)
-    core_g[1].start()
-    core_sum(2)
-    lax.fori_loop(1, S, m_arrived, 0)
+    def first_grad():
+        weight_grad(0, None, og)
+        pl.semaphore_wait(freed, len(writers))
+        core_g[0].start()
+
+    def next_grad(w, left, right):
+        weight_grad(w, left, right)
+        core_g[w].start()
+
+    event("wg0", first_grad)
+    event("wg1", lambda: next_grad(1, ffin, ug))
+    event("wg2", lambda: next_grad(2, hid, cot))
+    event("release", lambda: release(freed_again))
+    event("mwait", lambda: lax.fori_loop(1, S, m_arrived, 0))
+    for w in range(3):
+        event(f"cs{w}", functools.partial(core_sum, w))
+        event(f"f{w}", functools.partial(side_sum_1, w))
 
     assert A & (A - 1) == 0
     strides = [1 << n for n in range(A.bit_length() - 1)]
@@ -941,20 +1026,26 @@
             )
         )
 
+    def line_begin(w):
+        side_sum_2(w)
+        lines[w].begin()
+
+    for w in range(3):
+        event(f"g{w}", functools.partial(line_begin, w))
+        event(f"h{w}0", functools.partial(lines[w].step, 0))
+
     delta, dqt, dqkvt = ref["delta"], ref["dqt"], ref["dqkvt"]
-    for hd in range(HG):
-        head = slice(hd * HD, (hd + 1) * HD)
-        total = jnp.sum(dot_t[head, :].astype(F32) * ot[head, :], axis=0, keepdims=True)
-        delta[hd, :, :] = jnp.broadcast_to(total, (8, T))
-    dqt[...] = jnp.zeros_like(dqt)
+    def make_delta():
+        for hd in range(HG):
+            head = slice(hd * HD, (hd + 1) * HD)
+            total = jnp.sum(dot_t[head, :].astype(F32) * ot[head, :], axis=0, keepdims=True)
+            delta[hd, :, :] = jnp.broadcast_to(total, (8, T))
+        dqt[...] = jnp.zeros_like(dqt)
+
+    event("delta", make_delta)
     NB = S // PAIR
     starts = [sum(NB - k for k in range(j)) for j in range(NB)]
     pairs = NB * (NB + 1) // 2
-    jobs = {
-        2: [lambda: core_sum(1), lambda: release(freed_again)],
-        min(3, pairs - 2): [lambda: side_sum_1(0)],
-        min(7, pairs - 2): [lambda: side_sum_1(2)],
-    }
     dkt, dvt = ref["dkt"], ref["dvt"]
 
     def attend_back(n, carried):
@@ -990,15 +1081,15 @@
             dqkvt[2 * E : 3 * E, here] = dvt[...].astype(BF16)
 
         pl.when(i == NB - 1)(keep)
-        for m, todo in jobs.items():
-
-            def run(todo=todo):
-                for job in todo:
-                    job()
-
-            pl.when(n == m)(run)
-        return carried
-
+        for m in range(pairs):
+            if back_order.get(f"B{m}"):
+                pl.when(n == m)(functools.partial(play, back_order[f"B{m}"]))
+        return carried
+
+    names = [name for name in SECOND if name in events or name[0] == "B"]
+    first_part = names[: names.index("BX")]
+    back_order = segments_of(first_part, "B", "BX")
+    play(back_order[None])
     lax.fori_loop(0, pairs, attend_back, 0)
     if CW > 3 * E:
         dqkvt[3 * E :, :] = jnp.zeros((CW - 3 * E, T), BF16)
@@ -1016,24 +1107,25 @@
         gq[tile(n), :] = dot(dqkvt[...], near(xa.at[:, tile(n)], "x_cols", 7)[...]).T.astype(BF16)
         return carried
 
-    lax.fori_loop(0, NW, qkv_grad, 0)
     QR = q * SR
     line_q = Line(
         lambda d: gq.at[pl.ds(pl.multiple_of(d * QR, 16), QR)],
         lambda slot: cqu.at[slot],
         "q_rows",
     )
-    line_q.begin()
-
-    for group in (own_x, pass_x, sib_x):
-        for moved in group.values():
-            moved.sent()
-            links.copies.remove(moved)
-
-    ones = jnp.ones((8, T), BF16)
-    head_sums = dot_nt(ones, dqkvt[...])
-    small[pl.ds(8 + g, 1), 0:CW] = head_sums[0:1]
-    small[5:6, 0:E] = jnp.transpose(jnp.broadcast_to(scale_terms, (E, 128)))[0:1, :]
+
+    def q_grads():
+        lax.fori_loop(0, NW, qkv_grad, 0)
+        line_q.begin()
+
+    def q_last():
+        for n in range(1, len(strides)):
+            line_q.step(n)
+        own_q()
+
+    event("qg", q_grads)
+    event("Q0", lambda: line_q.step(0))
+    event("Q1", q_last)
     sums, landed, late, late_landed = (ref[k] for k in ("sums", "landed", "late", "late_landed"))
 
     class Total:
@@ -1072,13 +1164,25 @@
         if n + 1 < len(late_total.stages):
             late_total.begin(n + 1)
 
-    sums[0] = small[...]
-    total.begin(0)
+
+    def total_begin():
+        ones = jnp.ones((8, T), BF16)
+        head_sums = dot_nt(ones, dqkvt[...])
+        small[pl.ds(8 + g, 1), 0:CW] = head_sums[0:1]
+        small[5:6, 0:E] = jnp.transpose(jnp.broadcast_to(scale_terms, (E, 128)))[0:1, :]
+        sums[0] = small[...]
+        total.begin(0)
 
     def total_step(n):
         total.end(n)
         if n + 1 < len(total.stages):
             total.begin(n + 1)
+
+    event("t", total_begin)
+    for n in range(len(total.stages)):
+        event(f"t{n}", functools.partial(total_step, n))
+    for n in range(len(late_total.stages)):
+        event(f"L{n}", functools.partial(late_step, n))
 
     ags, arc = ref["ags"], ref["arc"]
 
@@ -1100,9 +1204,6 @@
     for n, (u2, b2) in enumerate(order):
         core_a[u2, b2] = links.copy(ags.at[pl.ds(n * L, L)], slot_of(2 * n, L), sibling)
     dtok = ref["dtok"]
-    side_sum_2(0)
-    lines[0].begin()
-    pl.semaphore_wait(freed_again, len(writers))
 
     def partial_rows(m, carried, others):
         block = block_of(m // q, 1 - c if others else c, m % q)
@@ -1117,8 +1218,16 @@
                 pl.when(m == j)(core_a[key].start)
         return carried
 
-    lax.fori_loop(0, U * q, functools.partial(partial_rows, others=True), 0)
-    lax.fori_loop(0, U * q, functools.partial(partial_rows, others=False), 0)
+    def partial_others():
+        for group in (own_x, pass_x, sib_x):
+            for moved in group.values():
+                moved.sent()
+                links.copies.remove(moved)
+        pl.semaphore_wait(freed_again, len(writers))
+        lax.fori_loop(0, U * q, functools.partial(partial_rows, others=True), 0)
+
+    event("ago", partial_others)
+    event("agm", lambda: lax.fori_loop(0, U * q, functools.partial(partial_rows, others=False), 0))
 
 
     def part(u2, b2, h):
@@ -1148,29 +1257,29 @@
 
         lax.fori_loop(0, count // STEP, step, 0)
 
-    side_sum_2(2)
-    lines[2].begin()
-    side_sum_1(1)
-    for u2, b2 in order:
-        core_a[u2, b2].arrived()
-
-        add_rows(arc.at[rows_of(u2 * q + b2)], slot_of(2 * order.index((u2, b2)), L), L)
-    for moved in list(afb.values()) + list(afu.values()):
-        moved.start()
-    lines[0].step(0)
-    line_q.step(0)
-    lines[2].step(0)
-
-    for db in range(1, q):
-        for u2 in range(U):
-            afb[db, u2].arrived()
-            add_rows(part(u2, b, 0), landing["fb", db, u2], HALF)
-    for du in range(1, U):
-        for b2 in range(q):
-            afu[du, b2].arrived()
-            add_rows(part(u, b2, 1), landing["fu", du, b2], HALF)
-    for moved in list(asb.values()) + list(asu.values()):
-        moved.start()
+    def rows_core():
+        for u2, b2 in order:
+            core_a[u2, b2].arrived()
+            add_rows(arc.at[rows_of(u2 * q + b2)], slot_of(2 * order.index((u2, b2)), L), L)
+        start_all(*afb.values(), *afu.values())
+
+    def rows_on_b_1():
+        for db in range(1, q):
+            for u2 in range(U):
+                afb[db, u2].arrived()
+                add_rows(part(u2, b, 0), landing["fb", db, u2], HALF)
+        start_all(*asu.values())
+
+    def rows_on_u_1():
+        for du in range(1, U):
+            for b2 in range(q):
+                afu[du, b2].arrived()
+                add_rows(part(u, b2, 1), landing["fu", du, b2], HALF)
+        start_all(*asb.values())
+
+    event("ac", rows_core)
+    event("ab", rows_on_b_1)
+    event("au", rows_on_u_1)
 
     wide, q_across, q_core = {}, [], []
     for db in range(1, q):
@@ -1199,6 +1308,9 @@
         for du in range(1, U):
             q_across[du - 1].arrived()
             q_core[du].start()
+
+    event("Q2", across_q)
+    event("Q3", core_q)
 
     go = ref["go"]
     spread, core_go, partials = {}, {}, {}
@@ -1241,18 +1353,23 @@
                 moved.arrived()
         core_go[w].start()
 
-    total_step(0)
-    side_sum_2(1)
-    lines[1].begin()
-    last_lines(0)
-
-    for db in range(1, q):
-        asb[db].arrived()
-        add_rows(part(u, b, 1), landing["sb", db], HALF)
-    for du in range(1, U):
-        asu[du].arrived()
-        add_rows(part(u, b, 0), landing["su", du], HALF)
-    small[0:1, :] = jnp.zeros((1, D), F32)
+    for w in range(3):
+        event(f"h{w}1", functools.partial(last_lines, w))
+        event(f"k{w}", functools.partial(core_go_on, w))
+
+    def rows_end():
+        for db in range(1, q):
+            asb[db].arrived()
+            add_rows(part(u, b, 1), landing["sb", db], HALF)
+        for du in range(1, U):
+            asu[du].arrived()
+            add_rows(part(u, b, 0), landing["su", du], HALF)
+        small[0:1, :] = jnp.zeros((1, D), F32)
+        lax.fori_loop(0, L // STEP, tok_back, 0)
+        late[0] = small[0:1, :]
+        late_total.begin(0)
+        back_tok.start()
+        pl.when(stays)(keep_tok)
 
     def tok_back(i, carried):
         x = tok[strip(i), :].astype(F32)
@@ -1265,36 +1382,16 @@
         ref["gtb"][strip(i), :] = (mg[strip(i), :] + inverse * (scaled - normed * mean)).astype(BF16)
         return carried
 
-    lax.fori_loop(0, L // STEP, tok_back, 0)
-    late[0] = small[0:1, :]
-    late_total.begin(0)
     back_tok = links.copy(ref["gtb"], ref["gtok"], origin, moves, moves)
-    back_tok.start()
 
     def keep_tok():
         kept = local(ref["gtb"], ref["gtok"], 0)
         kept.start()
         kept.wait()
 
-    pl.when(stays)(keep_tok)
-    for n in range(1, len(strides)):
-        line_q.step(n)
-    own_q()
-    lines[1].step(0)
-    last_lines(2)
-    across_q()
-    core_go_on(0)
-    last_lines(1)
-    core_go_on(2)
-    late_step(0)
-    total_step(1)
-    late_step(1)
-    core_q()
-    core_go_on(1)
-    for n in range(2, len(late_total.stages)):
-        late_step(n)
-    for n in range(2, len(total.stages)):
-        total_step(n)
+    event("end", rows_end)
+    names = [name for name in SECOND[SECOND.index("BX") + 1 :] if name in events]
+    play(names + [name for name in events if name not in names])
     ref["g_small"][...] = sums[len(total.stages)]
     ref["g_small"][0:1, :] = late[len(late_total.stages)]
     for w in range(3):
@@ -1401,6 +1498,8 @@
         scratch["x_rows"] = ((L, D), BF16)
         scratch["x_cols"] = ((T, 256), BF16)
         scratch["c_rows"] = ((SRH, DH), BF16)
+    if U == 2:
+        scratch["lent_tok"] = scratch["lent_cot"] = ((L, D), BF16)
     names = list(operands) + list(outputs) + list(scratch)
     names += ["send_sems", "recv_sems", "local_sems", "freed", "freed_again"]
 

time: 253 us -> 240 us (0.949)
  Pallas kernels: 252 us -> 239 us
    pallas_call x1, Pallas kernels: 247 us -> 233 us  [call(): pl.pallas_call(kernel, out_shape=[jax.ShapeDtypeStruct(*shape) for shape...]
where the time goes in v4:
time: 240 us; the launch traced here: 239 us
  Pallas kernels  239 us (100%)
    pallas_call x1, Pallas kernels, call(): pl.pallas_call(kernel, out_shape=[jax.ShapeDtypeStruct(*shape) for shape...  233 us
    pallas_call x1, Pallas kernels, shards(): pl.pallas_call(finish, out_shape=[jax.ShapeDtypeStruct(*shape) for shape...  5.85 us

profile of v4, /device:TPU:1, one launch (start us, length us, event | category | flops | bytes accessed | tf_op | source)
XLA Modules:
  0.0 239.4 jit_solution(570026748301353341)
XLA Ops:
  0.7 232.7 %shard_map.297 = (bf16[256,1280]{1,0:T(8,128)(2,1)}, bf16[256,1280]{1,0:T(8,128)(2,1)}, bf16[3,160,1280]{2,1,0:T(8,128)(2,1)}, bf16[8,160,512]{2,1,0:T(8,128)(2,1)}, f32[16,1280]{1,0:T(8,128)}) custom-call(bf16[256,1280]{1,0:T(8,128)(2,1)} %refs_0_.1, bf16[256,1280]{1,0:T(8,128)(2,1)} %refs_1_.1, bf16[160,1280]{1,0:T(8,128)(2,1)} %refs_2_.1, ...), custom_call_target="tpu_custom_call" | custom-call | tf_op jit(solution)/shard_map/pallas_call | solution.py:1521
  233.4 5.9 %shard_map.298 = (bf16[256,1280]{1,0:T(8,128)(2,1)}, bf16[256,1280]{1,0:T(8,128)(2,1)}, f32[160,1280]{1,0:T(8,128)}, f32[160,1280]{1,0:T(8,128)}, f32[160,1280]{...) custom-call(bf16[256,1280]{1,0:T(8,128)(2,1)} %get-tuple-element.21., ...), custom_call_target="tpu_custom_call" | custom-call | tf_op jit(solution)/shard_map/pallas_call | solution.py:1560

commit v5 on v4

--- a/solution.py
+++ b/solution.py
@@ -20,17 +20,17 @@
 LABELS = 16
 VMEM_BYTES = 64 << 20
 SECOND = (
-    "wg0", "wg2", "cs0", "wg1", "mwait", "delta", "B2", "cs2", "B6", "cs1", "B9", "release", "f2",
-    "f0", "BX", "t", "qg", "ago", "t0", "g2", "agm", "ac", "g0", "Q0", "ab", "f1", "h00", "h01",
-    "Q1", "h20", "au", "g1", "Q2", "h10", "h21", "t1", "k0", "end", "h11", "t2", "L0", "k1", "Q3",
-    "L1", "t3", "k2", "t4", "L2",
+    "wg0", "wg2", "out", "cs0", "mwait", "wg1", "delta", "B1", "cs2", "B2", "cs1", "release", "BX",
+    "qg0", "t", "qg1", "f2", "ago", "f0", "agm", "t0", "g2", "ac", "Q00", "f1", "g0", "Q01", "ab",
+    "Q10", "Q11", "h00", "g1", "Q20", "au", "Q21", "h20", "Q30", "h01", "t1", "h10", "end", "h21",
+    "h11", "t2", "L0", "L1", "k0", "t3", "k1", "Q31", "L2", "t4", "k2",
 )
 FIRST = (
-    "wcat", "tok", "carry", "n0", "wcat2", "own", "n1", "l2", "xb0", "tables", "xu0", "l1", "q0",
-    "l0", "xu1", "q1", "l20", "q2", "l10", "coth", "xb1", "xp0", "l00", "l21", "l11", "turnq",
-    "l01", "xp1", "s0", "s20", "project", "l02", "s00", "s10", "s02", "c00", "s01", "s2", "A0",
-    "l12", "cot", "c10", "A1", "A2", "l22", "s21", "s11", "s12", "c01", "c20", "A3", "s1", "AX",
-    "c02", "c12", "c11", "c21", "s22", "owait", "F0", "F1", "F2", "c22",
+    "tok", "wcat", "own", "carry", "l2", "l1", "coth", "n0", "wcat2", "l0", "n1", "xu0", "s0", "q0",
+    "xb0", "xu1", "l10", "l11", "l00", "l12", "tables", "q1", "l20", "l01", "xp1", "xp0", "q2",
+    "turnq", "xb1", "s00", "s20", "s10", "l21", "l02", "s12", "project", "l22", "s02", "cot", "A0",
+    "A1", "c02", "s21", "s01", "c10", "A2", "c00", "A3", "c01", "s11", "s22", "AX", "c21", "c20",
+    "c12", "owait", "F0", "s1", "F1", "s2", "c11", "c22", "F2",
 )
 
 
@@ -392,29 +392,42 @@
             down_w[w, k] = links.copy(
                 at, at, below, jnp.logical_and(a + k <= A - 1, a > 0), a + 1 + k <= A - 1
             )
+        by_place = {}
+
+        def sems(kind, place):
+            if kind not in by_place:
+                by_place[kind] = links.block(A)
+            return by_place[kind] + place
+
         for slot in slots:
             valid = a + slot <= A - 1 if slot > 0 else a + slot >= 0
             a0 = jnp.clip(a + slot, 0, A - 1)
             at = w3.at[w, piece_rows(a0, b, u), own_half]
             for db in range(1, q):
-                side_w[w, slot, 0, db] = links.copy(at, at, peer(u, c, b_off[db]), valid, valid)
+                side_w[w, slot, 0, db] = links.copy(
+                    at, at, peer(u, c, b_off[db]), valid, valid, index=sems(("b", db), a0)
+                )
             if H > 1:
                 for du in range(1, U):
-                    side_w[w, slot, du, 0] = links.copy(at, at, peer(u_off[du], c, b), valid, valid)
+                    side_w[w, slot, du, 0] = links.copy(
+                        at, at, peer(u_off[du], c, b), valid, valid, index=sems(("u", du), a0)
+                    )
                     for db in range(1, q):
                         sent, came = b_then_u(u, w), b_then_u(u_from[du], w)
                         at = w3.at[w, piece_rows(a0, b_from[db], u), own_half]
                         side_w[w, slot, du, db] = links.copy(
                             at, at, peer(u_off[du], c, b),
                             jnp.logical_and(valid, sent), jnp.logical_and(valid, came),
+                            index=sems(("bu", du, db), a0),
                         )
                         at = w3.at[w, piece_rows(a0, b, u_from[du]), own_half]
                         other = jnp.logical_and(valid, jnp.logical_not(came))
                         side_w[w, slot, du, -db] = links.copy(
-                            at, at, peer(u, c, b_off[db]), other, other
+                            at, at, peer(u, c, b_off[db]), other, other,
+                            index=sems(("ub", du, db), a0),
                         )
             at = w3.at[w, pl.ds(pl.multiple_of(a0 * q * SR, 16), q * SR), own_half]
-            core_w[w, slot] = links.copy(at, at, sibling, valid, valid)
+            core_w[w, slot] = links.copy(at, at, sibling, valid, valid, index=sems("core", a0))
         for db in range(1, q):
             at = w3.at[w, shard_rows(a, b), own_half]
             own_w[w, db] = links.copy(at, at, peer(u, c, b_off[db]))
@@ -770,14 +783,17 @@
 
     lax.fori_loop(0, NW, down_step, 0)
     back_out = links.copy(outb, ref["out"], origin, moves, moves)
-    back_out.start()
 
     def keep_out():
         kept = local(outb, ref["out"], 0)
         kept.start()
         kept.wait()
 
-    pl.when(stays)(keep_out)
+    def out_back():
+        back_out.start()
+        pl.when(stays)(keep_out)
+
+    event("out", out_back)
     for piece in swap_cot:
         swap_end(piece)
     swap_sent(swap_cot)
@@ -1103,29 +1119,37 @@
 
     gq, cqu, gall = ref["gq"], ref["cqu"], ref["gall"]
 
-    def qkv_grad(n, carried):
-        gq[tile(n), :] = dot(dqkvt[...], near(xa.at[:, tile(n)], "x_cols", 7)[...]).T.astype(BF16)
+    CH = CW // 2
+    lanes = [pl.ds(k * CH, CH) for k in range(2)]
+
+    def qkv_grad(n, carried, k):
+        x = near(xa.at[:, tile(n)], "x_cols", 7)[...]
+        gq[tile(n), lanes[k]] = dot(dqkvt[lanes[k], :], x).T.astype(BF16)
         return carried
 
     QR = q * SR
-    line_q = Line(
-        lambda d: gq.at[pl.ds(pl.multiple_of(d * QR, 16), QR)],
-        lambda slot: cqu.at[slot],
-        "q_rows",
-    )
-
-    def q_grads():
-        lax.fori_loop(0, NW, qkv_grad, 0)
-        line_q.begin()
-
-    def q_last():
+    line_q = [
+        Line(
+            lambda d, k=k: gq.at[pl.ds(pl.multiple_of(d * QR, 16), QR), lanes[k]],
+            lambda slot, k=k: cqu.at[slot, :, lanes[k]],
+            "q_rows",
+        )
+        for k in range(2)
+    ]
+
+    def q_grads(k):
+        lax.fori_loop(0, NW, functools.partial(qkv_grad, k=k), 0)
+        line_q[k].begin()
+
+    def q_last(k):
         for n in range(1, len(strides)):
-            line_q.step(n)
-        own_q()
-
-    event("qg", q_grads)
-    event("Q0", lambda: line_q.step(0))
-    event("Q1", q_last)
+            line_q[k].step(n)
+        own_q(k)
+
+    for k in range(2):
+        event(f"qg{k}", functools.partial(q_grads, k))
+        event(f"Q0{k}", functools.partial(line_q[k].step, 0))
+        event(f"Q1{k}", functools.partial(q_last, k))
     sums, landed, late, late_landed = (ref[k] for k in ("sums", "landed", "late", "late_landed"))
 
     class Total:
@@ -1168,7 +1192,14 @@
     def total_begin():
         ones = jnp.ones((8, T), BF16)
         head_sums = dot_nt(ones, dqkvt[...])
-        small[pl.ds(8 + g, 1), 0:CW] = head_sums[0:1]
+        biascat[...] = head_sums
+
+        def place_sums(k):
+            small[6:7, k * E : (k + 1) * E] = biascat[0:1, 0:E]
+            small[7:8, k * E : (k + 1) * E] = biascat[0:1, 2 * E : 3 * E]
+
+        for k in range(S):
+            pl.when(g == k)(functools.partial(place_sums, k))
         small[5:6, 0:E] = jnp.transpose(jnp.broadcast_to(scale_terms, (E, 128)))[0:1, :]
         sums[0] = small[...]
         total.begin(0)
@@ -1281,36 +1312,39 @@
     event("ab", rows_on_b_1)
     event("au", rows_on_u_1)
 
-    wide, q_across, q_core = {}, [], []
-    for db in range(1, q):
-        at = gq.at[pl.ds(pl.multiple_of(a * QR + b_off[db] * SR, 16), SR)]
-        wide[db] = links.copy(at, gall.at[g], device(r, a, b_off[db]))
-    here = pl.ds(r * q, q)
-    for du in range(1, U):
-        q_across.append(links.copy(gall.at[here], gall.at[here], peer(u_off[du], c, b)))
-    for du in range(U):
-        here = pl.ds((u_from[du] * 2 + c) * q, q)
-        q_core.append(links.copy(gall.at[here], gall.at[here], sibling))
-
-    def own_q():
+    wide, q_across, q_core = {}, {}, {}
+    for k in range(2):
         for db in range(1, q):
-            wide[db].start()
-        gall[g] = gq[pl.ds(pl.multiple_of(a * QR + b * SR, 16), SR), :]
-
-    def across_q():
+            rows = pl.ds(pl.multiple_of(a * QR + b_off[db] * SR, 16), SR)
+            wide[k, db] = links.copy(
+                gq.at[rows, lanes[k]], gall.at[g, :, lanes[k]], device(r, a, b_off[db])
+            )
+        at = gall.at[pl.ds(r * q, q), :, lanes[k]]
+        for du in range(1, U):
+            q_across[k, du] = links.copy(at, at, peer(u_off[du], c, b))
+        for du in range(U):
+            at = gall.at[pl.ds((u_from[du] * 2 + c) * q, q), :, lanes[k]]
+            q_core[k, du] = links.copy(at, at, sibling)
+
+    def own_q(k):
         for db in range(1, q):
-            wide[db].arrived()
-        for moved in q_across:
-            moved.start()
-        q_core[0].start()
-
-    def core_q():
+            wide[k, db].start()
+        rows = pl.ds(pl.multiple_of(a * QR + b * SR, 16), SR)
+        gall[g, :, lanes[k]] = gq[rows, lanes[k]]
+
+    def across_q(k):
+        for db in range(1, q):
+            wide[k, db].arrived()
+        start_all(*[q_across[k, du] for du in range(1, U)], q_core[k, 0])
+
+    def core_q(k):
         for du in range(1, U):
-            q_across[du - 1].arrived()
-            q_core[du].start()
-
-    event("Q2", across_q)
-    event("Q3", core_q)
+            q_across[k, du].arrived()
+            q_core[k, du].start()
+
+    for k in range(2):
+        event(f"Q2{k}", functools.partial(across_q, k))
+        event(f"Q3{k}", functools.partial(core_q, k))
 
     go = ref["go"]
     spread, core_go, partials = {}, {}, {}
@@ -1396,7 +1430,7 @@
     ref["g_small"][0:1, :] = late[len(late_total.stages)]
     for w in range(3):
         core_go[w].arrived()
-    for moved in q_core:
+    for moved in q_core.values():
         moved.arrived()
     back_out.arrived()
     back_tok.arrived()
@@ -1444,7 +1478,7 @@
     H = U if SR % (16 * U) == 0 else 1
     SRH = SR // H
     DH = D // 2
-    NS = 8 + S
+    NS = 8
     segments = lengths.shape[1]
     dims = dict(R=R, S=S, L=L, D=D, HG=HG, E=E, CW=CW, SR=SR, H=H, SRH=SRH, segments=segments)
 
@@ -1537,31 +1571,44 @@
     out, gtok, go, gall, g_small = made[:results]
 
     def finish(out, gtok, go, gall, sums, scale, *refs):
-        made_out, made_gtok, grads, vectors = refs[0], refs[1], refs[2:8], refs[8:16]
-        made_out[...] = out[...]
-        made_gtok[...] = gtok[...]
-        for g2 in range(S):
-            mine = gall[g2]
-            for n in range(3):
-                grads[n][:, g2 * E : (g2 + 1) * E] = mine[:, n * E : (n + 1) * E].astype(F32)
-        for w in range(3):
-            grads[3 + w][...] = go[w].astype(F32)
-        for n, at in ((0, 0), (1, 1), (5, 2), (6, 3), (7, 4)):
+        outs, vectors, held, sems = refs[0:8], refs[8:16], refs[16:26], refs[26]
+        came = [out, gtok, gall, go]
+        loads = [pltpu.make_async_copy(came[n], held[n], sems.at[n]) for n in range(4)]
+        left = [held[0], held[1], *held[4:10]]
+        stores = [pltpu.make_async_copy(left[n], outs[n], sems.at[4 + n]) for n in range(8)]
+        for n in (2, 3, 0, 1):
+            loads[n].start()
+        for n, at in ((0, 0), (1, 1), (3, 6), (4, 7), (5, 2), (6, 3), (7, 4)):
             vectors[n][...] = sums[at : at + 1, :].reshape(D)
-        for n, at in ((3, 0), (4, 2 * E)):
-            whole = jnp.concatenate([sums[8 + k : 9 + k, at : at + E] for k in range(S)], axis=1)
-            vectors[n][...] = whole.reshape(D)
         terms = sum(sums[5:6, hd * HEAD_DIM : (hd + 1) * HEAD_DIM] for hd in range(HG))
         gate = jax.nn.sigmoid(scale[...].reshape(1, HEAD_DIM)) * (query_base / math.sqrt(HEAD_DIM))
         vectors[2][...] = (terms * gate).reshape(HEAD_DIM)
-
+        loads[2].wait()
+        for n in range(3):
+            for g2 in range(S):
+                mine = held[2][g2, :, n * E : (n + 1) * E]
+                held[4 + n][:, g2 * E : (g2 + 1) * E] = mine.astype(F32)
+            stores[2 + n].start()
+        loads[3].wait()
+        for w in range(3):
+            held[7 + w][...] = held[3][w].astype(F32)
+            stores[5 + w].start()
+        for n in range(2):
+            loads[n].wait()
+            stores[n].start()
+        for copy in stores:
+            copy.wait()
+
+    distant = pl.BlockSpec(memory_space=pl.ANY)
     final = [((L, D), BF16)] * 2 + [((SR, D), F32)] * 6 + [((D,), F32)] * 8
     final[10] = ((HEAD_DIM,), F32)
+    held = [((L, D), BF16)] * 2 + [((S, SR, CW), BF16), ((3, SR, D), BF16)] + [((SR, D), F32)] * 6
     return pl.pallas_call(
         finish,
         out_shape=[jax.ShapeDtypeStruct(*shape) for shape in final],
-        in_specs=[whole] * 6,
-        out_specs=[whole] * 16,
+        in_specs=[distant] * 4 + [whole] * 2,
+        out_specs=[distant] * 8 + [whole] * 8,
+        scratch_shapes=[pltpu.VMEM(*shape) for shape in held] + [pltpu.SemaphoreType.DMA((12,))],
         compiler_params=pltpu.CompilerParams(vmem_limit_bytes=VMEM_BYTES),
     )(out, gtok, go, gall, g_small, query_scale)
 

time: 240 us -> 225 us (0.938)
  Pallas kernels: 239 us -> 224 us
    pallas_call x1, Pallas kernels: 233 us -> 218 us  [call(): pl.pallas_call(kernel, out_shape=[jax.ShapeDtypeStruct(*shape) for shape...]
where the time goes in v5:
time: 225 us
  Pallas kernels  224 us (100%)
    pallas_call x1, Pallas kernels, call(): pl.pallas_call(kernel, out_shape=[jax.ShapeDtypeStruct(*shape) for shape...  218 us
    pallas_call x1, Pallas kernels, shards(): pl.pallas_call(finish, out_shape=[jax.ShapeDtypeStruct(*shape) for shape...  5.7 us

profile of v5, /device:TPU:1, one launch (start us, length us, event | category | flops | bytes accessed | tf_op | source)
XLA Modules:
  0.0 224.7 jit_solution(16921293883862778446)
XLA Ops:
  0.7 218.2 %shard_map.297 = (bf16[256,1280]{1,0:T(8,128)(2,1)}, bf16[256,1280]{1,0:T(8,128)(2,1)}, bf16[3,160,1280]{2,1,0:T(8,128)(2,1)}, bf16[8,160,512]{2,1,0:T(8,128)(2,1)}, f32[8,1280]{1,0:T(8,128)}) custom-call(bf16[256,1280]{1,0:T(8,128)(2,1)} %refs_0_.1, bf16[256,1280]{1,0:T(8,128)(2,1)} %refs_1_.1, bf16[160,1280]{1,0:T(8,128)(2,1)} %refs_2_.1, ...), custom_call_target="tpu_custom_call" | custom-call | tf_op jit(solution)/shard_map/pallas_call | solution.py:1555
  218.9 5.7 %shard_map.298 = (bf16[256,1280]{1,0:T(8,128)(2,1)}, bf16[256,1280]{1,0:T(8,128)(2,1)}, f32[160,1280]{1,0:T(8,128)}, f32[160,1280]{1,0:T(8,128)}, f32[160,1280]{...) custom-call(bf16[256,1280]{1,0:T(8,128)(2,1)} %get-tuple-element.21., ...), custom_call_target="tpu_custom_call" | custom-call | tf_op jit(solution)/shard_map/pallas_call | solution.py:1606

commit v6 on v5

--- a/solution.py
+++ b/solution.py
@@ -1,5 +1,6 @@
 import functools
 import math
+import types
 
 import jax
 import jax.numpy as jnp
@@ -42,6 +43,11 @@
     return lax.dot_general(left, right, (((1,), (1,)), ((), ())), preferred_element_type=F32)
 
 
+def steps(count, body):
+    for i in range(count):
+        body(i, 0)
+
+
 def when(condition, body):
     if condition is True:
         body()
@@ -93,8 +99,8 @@
 
 
 def layer_kernel(dims, refs):
-    R, S, L, D = dims["R"], dims["S"], dims["L"], dims["D"]
-    HG, E, CW, SR, H, SRH = (dims[k] for k in ("HG", "E", "CW", "SR", "H", "SRH"))
+    R, S, L, D = dims.R, dims.S, dims.L, dims.D
+    HG, E, CW, SR, H, SRH = dims.HG, dims.E, dims.CW, dims.SR, dims.H, dims.SRH
     q, U, A, T = S // R, R // 2, R, S * L
     HD = HEAD_DIM
     HALF, DH = L // 2, D // 2
@@ -159,7 +165,7 @@
     own_half = pl.ds(pl.multiple_of(c * DH, 128), DH)
     other_half = pl.ds(pl.multiple_of((1 - c) * DH, 128), DH)
 
-    links = Links(ref["send_sems"], ref["recv_sems"])
+    links = Links(ref.send_sems, ref.recv_sems)
     events = {}
 
     def event(name, job):
@@ -184,29 +190,30 @@
             moved.start()
 
 
-    local_sems = ref["local_sems"]
+    local_sems = ref.local_sems
 
     def local(src, dst, n):
         return pltpu.make_async_copy(src, dst, local_sems.at[n])
 
     def near(src, name, n):
-        if dims["fits"] or name == "q_rows":
+        if dims.fits or name == "q_rows":
             return src
-        copy = local(src, ref[name], n)
+        copy = local(src, getattr(ref, name), n)
         copy.start()
         copy.wait()
-        return ref[name]
+        return getattr(ref, name)
 
     def shard_rows(a2, b2):
         return pl.ds(pl.multiple_of((a2 * q + b2) * SR, 16), SR)
 
-    w3 = ref["w3"]
-    names = ("w_query", "w_key", "w_value")
-    parts = [ref[name].at[pl.ds(0, SR)] for name in ("hid", "ffin", "outb")]
-    near_parts = [local(ref[names[n]], parts[n], n) for n in range(3)]
-    names = ("w_out", "w_up", "w_down")
-    own_shards = [local(ref[names[w]], w3.at[w, shard_rows(a, b)], 4 + w) for w in range(3)]
-    near_rows = [local(ref["tokens"], ref["otok"], 3), local(ref["cotangent"], ref["og"], 7)]
+    w3 = ref.w3
+    parts = [held.at[pl.ds(0, SR)] for held in (ref.hid, ref.ffin, ref.outb)]
+    near_parts = [local(w, parts[n], n) for n, w in enumerate((ref.w_query, ref.w_key, ref.w_value))]
+    own_shards = [
+        local(shard, w3.at[w, shard_rows(a, b)], 4 + w)
+        for w, shard in enumerate((ref.w_out, ref.w_up, ref.w_down))
+    ]
+    near_rows = [local(ref.tokens, ref.otok, 3), local(ref.cotangent, ref.og, 7)]
     for copy in near_rows[:1] + near_parts + own_shards + near_rows[1:]:
         copy.start()
 
@@ -229,14 +236,15 @@
         pl.when(i_carry)(lambda: greet(next_home))
         pl.when(carried_in)(lambda: greet(carrier))
 
-    gains, biascat, qgain, tab = ref["gains"], ref["biascat"], ref["qgain"], ref["tab"]
-    rows = ("gain_attn", "gain_ff", "bias_out", "bias_up", "bias_down", "bias_query", "bias_value")
-    for n, name in enumerate(rows):
-        gains[n : n + 1, :] = ref[name][...].reshape(1, D)
-    segments = dims["segments"]
+    gains, biascat, qgain, tab = ref.gains, ref.biascat, ref.qgain, ref.tab
+    rows = [ref.gain_attn, ref.gain_ff, ref.bias_out, ref.bias_up, ref.bias_down]
+    rows += [ref.bias_query, ref.bias_value]
+    for n, row in enumerate(rows):
+        gains[n : n + 1, :] = row[...].reshape(1, D)
+    segments = dims.segments
     tab[...] = jnp.zeros((8, 128), F32)
-    tab[0:1, 0:segments] = ref["lengths"][...].astype(F32)
-    tab[1:2, 0:segments] = ref["parents"][...].astype(F32)
+    tab[0:1, 0:segments] = ref.lengths[...].astype(F32)
+    tab[1:2, 0:segments] = ref.parents[...].astype(F32)
     biascat[...] = jnp.zeros((8, CW), F32)
 
     def bias_slice(k):
@@ -245,13 +253,13 @@
 
     for k in range(S):
         pl.when(g == k)(functools.partial(bias_slice, k))
-    scale = ref["query_scale"][...].reshape(1, HD)
+    scale = ref.query_scale[...].reshape(1, HD)
     soft = jnp.maximum(scale, 0.0) + jnp.log(1.0 + jnp.exp(-jnp.abs(scale)))
     qgain[...] = jnp.ones((8, CW), F32)
     for hd in range(HG):
         qgain[0:1, hd * HD : (hd + 1) * HD] = soft * (query_base / math.sqrt(HD))
 
-    wq, wqt, wcat = ref["wq"], ref["wqt"], ref["gall"]
+    wq, wqt, wcat = ref.wq, ref.wqt, ref.gall
     for copy in near_parts:
         copy.wait()
 
@@ -273,15 +281,19 @@
 
     for copy in near_rows:
         copy.wait()
-    swap_tab = links.copy(ref["tab"], ref["tabs"], home, moves, moves)
+    swap_tab = links.copy(ref.tab, ref.tabs, home, moves, moves)
     swap_rows, swap_cot = [], []
-    for name, there, pieces in (("otok", "tok", swap_rows), ("og", "cot", swap_cot)):
+    lent_tok, lent_cot = (ref.lent_tok, ref.lent_cot) if by_u else (None, None)
+    for left, there, lent_to, pieces in (
+        (ref.otok, ref.tok, lent_tok, swap_rows),
+        (ref.og, ref.cot, lent_cot, swap_cot),
+    ):
         for h in range(2):
             here = pl.ds(h * HALF, HALF)
-            src, dst = ref[name].at[here], ref[there].at[here]
+            src, dst = left.at[here], there.at[here]
             piece = [links.copy(src, dst, home, direct, direct_in)]
             if by_u:
-                lent = ref["lent_" + there].at[here]
+                lent = lent_to.at[here]
                 piece.append(links.copy(src, lent, peer(1 - u, c, b), i_cross, i_carry))
                 piece.append(links.copy(lent, dst, next_home, i_carry, carried_in))
             pieces.append(piece)
@@ -307,8 +319,8 @@
             links.copies.remove(moved)
 
     def keep_rows():
-        for name, there in (("otok", "tok"), ("tab", "tabs"), ("og", "cot")):
-            ref[there][...] = ref[name][...]
+        for left, there in ((ref.otok, ref.tok), (ref.tab, ref.tabs), (ref.og, ref.cot)):
+            there[...] = left[...]
 
 
     def tok_begin():
@@ -489,7 +501,7 @@
         for slot in slots:
             core_w[w, slot].arrived()
 
-    tok, cot, xa = ref["tok"], ref["cot"], ref["xa"]
+    tok, cot, xa = ref.tok, ref.cot, ref.xa
     gain_attn, gain_ff = gains[0:1, :], gains[1:2, :]
     STEP = 32
 
@@ -527,16 +539,16 @@
             x = tok[here, :].astype(F32)
             there = pl.ds(pl.multiple_of(blk * L + h * HALF + i * STEP, STEP), STEP)
             row = (x * unit(x) * gain_attn).astype(BF16)
-            if dims["fits"]:
+            if dims.fits:
                 xa[there, :] = row
             else:
-                ref["x_rows"][here, :] = row
+                ref.x_rows[here, :] = row
             return carried
 
-        lax.fori_loop(0, HALF // STEP, norm_step, 0)
-        if not dims["fits"]:
+        steps(HALF // STEP, norm_step)
+        if not dims.fits:
             here = pl.ds(h * HALF, HALF)
-            out_of = local(ref["x_rows"].at[here], xa.at[half_rows(blk, h)], 7)
+            out_of = local(ref.x_rows.at[here], xa.at[half_rows(blk, h)], 7)
             out_of.start()
             out_of.wait()
         start_all(*[m for (h2, *_), m in own_x.items() if h2 == h], sib_x[h, 0, 0])
@@ -567,24 +579,24 @@
         event(f"xu{h}", functools.partial(rows_on_u, h))
         event(f"xp{h}", functools.partial(rows_passed, h))
 
-    tables = {}
+    tables = types.SimpleNamespace()
 
     def make_tables():
         swap_tab.arrived()
         lane = lax.broadcasted_iota(jnp.int32, (LABELS, 128), 1)
         row = lax.broadcasted_iota(jnp.int32, (LABELS, 128), 0)
-        lengths = jnp.broadcast_to(ref["tabs"][0:1, :], (LABELS, 128))
+        lengths = jnp.broadcast_to(ref.tabs[0:1, :], (LABELS, 128))
         seg_start = jnp.sum(jnp.where(lane < row, lengths, 0.0), axis=1, keepdims=True)
         seg_end = jnp.sum(jnp.where(lane <= row, lengths, 0.0), axis=1, keepdims=True)
         lane = lax.broadcasted_iota(jnp.int32, (128, 128), 1)
         row = lax.broadcasted_iota(jnp.int32, (128, 128), 0)
-        parents = jnp.broadcast_to(ref["tabs"][1:2, :], (128, 128))
+        parents = jnp.broadcast_to(ref.tabs[1:2, :], (128, 128))
         is_parent = (parents == row.astype(F32)) & (lane > 0) & (lane < segments)
         reach = jnp.where((lane == row) | is_parent, 1.0, 0.0)
         for _ in range(max(1, (segments - 1).bit_length())):
             reach = jnp.minimum(dot(reach.astype(BF16), reach.astype(BF16)), 1.0)
         blocked = ((1.0 - reach[:LABELS, :LABELS]) * masked_score).astype(BF16)
-        tables["start"], tables["end"], tables["blocked"] = seg_start, seg_end, blocked
+        tables.start, tables.end, tables.blocked = seg_start, seg_end, blocked
 
     event("tables", make_tables)
 
@@ -593,12 +605,11 @@
         wqt[:, here] = wq[here, :].T
         return carried
 
-    event("turnq", lambda: lax.fori_loop(0, NW, turn_wq, 0))
+    event("turnq", lambda: steps(NW, turn_wq))
     bias_col = jnp.transpose(biascat[...])[:, 0:1]
     qgain_col = jnp.transpose(qgain[...])[:, 0:1]
-    qkvf, qpre, qt, keys, kt, vals, vt = (
-        ref[k] for k in ("qkvf", "qpre", "qt", "keys", "kt", "vals", "vt")
-    )
+    qkvf, qpre, qt, keys = ref.qkvf, ref.qpre, ref.qt, ref.keys
+    kt, vals, vt = ref.kt, ref.vals, ref.vt
 
     def project(k, carried):
         for j in range(S):
@@ -617,8 +628,8 @@
         qkvf[...] = dot_nt(wqt[...], x) + bias_col
         place = block * L + lax.broadcasted_iota(jnp.int32, (LABELS, L), 1)
         place = place.astype(F32)
-        onehot = jnp.where((place >= tables["start"]) & (place < tables["end"]), 1.0, 0.0)
-        far = dot(tables["blocked"], onehot.astype(BF16)).astype(BF16)
+        onehot = jnp.where((place >= tables.start) & (place < tables.end), 1.0, 0.0)
+        far = dot(tables.blocked, onehot.astype(BF16)).astype(BF16)
         for hd in range(HG):
             head = pl.ds(hd * HD, HD)
             pre = qkvf[head, :]
@@ -636,9 +647,9 @@
             vals[hd, cols, :] = wide.T.astype(BF16)
         return carried
 
-    event("project", lambda: lax.fori_loop(0, S, project, 0))
-
-    ot, otb, lse, oa = ref["ot"], ref["otb"], ref["lse"], ref["oa"]
+    event("project", lambda: steps(S, project))
+
+    ot, otb, lse, oa = ref.ot, ref.otb, ref.lse, ref.oa
     first_o = links.block(S)
     o_slot = pl.ds(pl.multiple_of(g * E, 16), E)
 
@@ -731,9 +742,9 @@
         pl.when(i != blk)(lambda: o_copy(i).sent())
         return carried
 
-    otok, mid, ffin, up, hid, outb = (ref[k] for k in ("otok", "mid", "ffin", "up", "hid", "outb"))
-    ug, fg, mg, og, mgt = (ref[k] for k in ("ug", "fg", "mg", "og", "mgt"))
-    small = ref["small"]
+    otok, mid, ffin, up, hid, outb = ref.otok, ref.mid, ref.ffin, ref.up, ref.hid, ref.outb
+    ug, fg, mg, og, mgt = ref.ug, ref.fg, ref.mg, ref.og, ref.mgt
+    small = ref.small
 
     def tile(n):
         return pl.ds(pl.multiple_of(n * W, W), W)
@@ -743,7 +754,7 @@
         return carried
 
     swap_sent(swap_rows)
-    lax.fori_loop(0, NW, turn_o, 0)
+    steps(NW, turn_o)
     play(ff_order["F0"])
     w3_whole(0)
 
@@ -752,7 +763,7 @@
         mid[:, tile(n)] = tok[:, tile(n)].astype(F32) + added
         return carried
 
-    lax.fori_loop(0, NW, out_step, 0)
+    steps(NW, out_step)
 
     def strip(i):
         return pl.ds(pl.multiple_of(i * STEP, STEP), STEP)
@@ -762,7 +773,7 @@
         ffin[strip(i), :] = (x * unit(x) * gain_ff).astype(BF16)
         return carried
 
-    lax.fori_loop(0, L // STEP, ff_norm, 0)
+    steps(L // STEP, ff_norm)
     play(ff_order["F1"])
     w3_whole(1)
 
@@ -772,7 +783,7 @@
         hid[:, tile(n)] = (pre * jax.nn.sigmoid(pre)).astype(BF16)
         return carried
 
-    lax.fori_loop(0, NW, up_step, 0)
+    steps(NW, up_step)
     play(ff_order["F2"])
     w3_whole(2)
 
@@ -781,11 +792,11 @@
         outb[:, tile(n)] = (mid[:, tile(n)] + added).astype(BF16)
         return carried
 
-    lax.fori_loop(0, NW, down_step, 0)
-    back_out = links.copy(outb, ref["out"], origin, moves, moves)
+    steps(NW, down_step)
+    back_out = links.copy(outb, ref.out, origin, moves, moves)
 
     def keep_out():
-        kept = local(outb, ref["out"], 0)
+        kept = local(outb, ref.out, 0)
         kept.start()
         kept.wait()
 
@@ -808,13 +819,13 @@
         small[3:4, tile(n)] = jnp.sum(grad.astype(F32), axis=0, keepdims=True)
         return carried
 
-    lax.fori_loop(0, NW, up_back, 0)
+    steps(NW, up_back)
 
     def ff_back(n, carried):
         fg[:, tile(n)] = dot_nt(ug[...], w3[1, tile(n), :])
         return carried
 
-    lax.fori_loop(0, NW, ff_back, 0)
+    steps(NW, ff_back)
 
     def mid_back(i, carried):
         x, grad, above_grad = mid[strip(i), :], fg[strip(i), :], cot[strip(i), :].astype(F32)
@@ -831,9 +842,9 @@
         small[4:5, :] += jnp.sum(above_grad, axis=0, keepdims=True)
         return carried
 
-    lax.fori_loop(0, L // STEP, mid_back, 0)
-
-    dot_t = ref["dot_t"]
+    steps(L // STEP, mid_back)
+
+    dot_t = ref.dot_t
     first_m = links.block(S)
 
     def m_copy(k):
@@ -850,10 +861,11 @@
         pl.when(k < S)(lambda: m_copy(k).start())
         return carried
 
-    lax.fori_loop(1, S + 1, mixed_step, 0)
+    for k in range(1, S + 1):
+        mixed_step(k, 0)
     dot_t[:, rows_of(blk)] = mgt[pl.ds(pl.multiple_of(g * E, 16), E), :]
 
-    freed, freed_again = ref["freed"], ref["freed_again"]
+    freed, freed_again = ref.freed, ref.freed_again
     writers = [sibling] + [peer(u, c, v) for v in b_off[1:]] + [peer(v, c, b) for v in u_off[1:]]
 
     def release(sem):
@@ -866,7 +878,7 @@
             links.copies.remove(moved)
     release(freed)
 
-    gp, rc = ref["gp"], ref["rc"]
+    gp, rc = ref.gp, ref.rc
     rcin = [w3.at[0, :, 0:DH], w3.at[0, :, DH:D], w3.at[1, :, 0:DH]]
     core_g = [links.copy(gp.at[w], rcin[w], sibling) for w in range(3)]
 
@@ -877,7 +889,7 @@
                 oa[tile(n), :] = left[:, tile(n)].T
                 return carried
 
-            lax.fori_loop(0, NW, turn, 0)
+            steps(NW, turn)
 
         def step(n, carried):
             here = pl.ds(pl.multiple_of(n * SR, 16), SR)
@@ -886,7 +898,7 @@
             rc[w, n // q, n % q] = dot(side, right[:, own_half]).astype(BF16)
             return carried
 
-        lax.fori_loop(0, S, step, 0)
+        steps(S, step)
 
     def m_arrived(k, carried):
         m_copy(k).arrived()
@@ -951,7 +963,7 @@
             add_into(rc.at[w, a2, b2], rcin[w].at[here])
             return carried
 
-        lax.fori_loop(0, S, step, 0)
+        steps(S, step)
         for key, moved in list(first_b.items()) + list(first_u.items()):
             if key[0] == w:
                 moved.start()
@@ -1031,7 +1043,7 @@
             if n + 1 < len(self.steps):
                 self.begin(n + 1)
 
-    cu = ref["cu"]
+    cu = ref.cu
     lines = []
     for w in range(3):
         lines.append(
@@ -1050,7 +1062,7 @@
         event(f"g{w}", functools.partial(line_begin, w))
         event(f"h{w}0", functools.partial(lines[w].step, 0))
 
-    delta, dqt, dqkvt = ref["delta"], ref["dqt"], ref["dqkvt"]
+    delta, dqt, dqkvt = ref.delta, ref.dqt, ref.dqkvt
     def make_delta():
         for hd in range(HG):
             head = slice(hd * HD, (hd + 1) * HD)
@@ -1062,7 +1074,7 @@
     NB = S // PAIR
     starts = [sum(NB - k for k in range(j)) for j in range(NB)]
     pairs = NB * (NB + 1) // 2
-    dkt, dvt = ref["dkt"], ref["dvt"]
+    dkt, dvt = ref.dkt, ref.dvt
 
     def attend_back(n, carried):
         j = sum(jnp.where(n >= start, 1, 0) for start in starts[1:])
@@ -1115,9 +1127,11 @@
         dqkvt[0:E, cols] = (dqt[:, cols] * qgain_col[0:E]).astype(BF16)
         return carried + jnp.sum(dqt[:, cols] * qpre[:, cols], axis=1, keepdims=True)
 
-    scale_terms = lax.fori_loop(0, S, query_part, jnp.zeros((E, 1), F32))
-
-    gq, cqu, gall = ref["gq"], ref["cqu"], ref["gall"]
+    scale_terms = jnp.zeros((E, 1), F32)
+    for i in range(S):
+        scale_terms = query_part(i, scale_terms)
+
+    gq, cqu, gall = ref.gq, ref.cqu, ref.gall
 
     CH = CW // 2
     lanes = [pl.ds(k * CH, CH) for k in range(2)]
@@ -1138,7 +1152,7 @@
     ]
 
     def q_grads(k):
-        lax.fori_loop(0, NW, functools.partial(qkv_grad, k=k), 0)
+        steps(NW, functools.partial(qkv_grad, k=k))
         line_q[k].begin()
 
     def q_last(k):
@@ -1150,7 +1164,7 @@
         event(f"qg{k}", functools.partial(q_grads, k))
         event(f"Q0{k}", functools.partial(line_q[k].step, 0))
         event(f"Q1{k}", functools.partial(q_last, k))
-    sums, landed, late, late_landed = (ref[k] for k in ("sums", "landed", "late", "late_landed"))
+    sums, landed, late, late_landed = ref.sums, ref.landed, ref.late, ref.late_landed
 
     class Total:
         def __init__(self, held, arrivals, stages):
@@ -1215,7 +1229,7 @@
     for n in range(len(late_total.stages)):
         event(f"L{n}", functools.partial(late_step, n))
 
-    ags, arc = ref["ags"], ref["arc"]
+    ags, arc = ref.ags, ref.arc
 
     def slot_of(n, rows):
         page, row = divmod(n * HALF, D)
@@ -1234,7 +1248,7 @@
     core_a = {}
     for n, (u2, b2) in enumerate(order):
         core_a[u2, b2] = links.copy(ags.at[pl.ds(n * L, L)], slot_of(2 * n, L), sibling)
-    dtok = ref["dtok"]
+    dtok = ref.dtok
 
     def partial_rows(m, carried, others):
         block = block_of(m // q, 1 - c if others else c, m % q)
@@ -1255,10 +1269,10 @@
                 moved.sent()
                 links.copies.remove(moved)
         pl.semaphore_wait(freed_again, len(writers))
-        lax.fori_loop(0, U * q, functools.partial(partial_rows, others=True), 0)
+        steps(U * q, functools.partial(partial_rows, others=True))
 
     event("ago", partial_others)
-    event("agm", lambda: lax.fori_loop(0, U * q, functools.partial(partial_rows, others=False), 0))
+    event("agm", lambda: steps(U * q, functools.partial(partial_rows, others=False)))
 
 
     def part(u2, b2, h):
@@ -1286,7 +1300,7 @@
             add_into(target.at[strip(i)], other.at[strip(i)])
             return carried
 
-        lax.fori_loop(0, count // STEP, step, 0)
+        steps(count // STEP, step)
 
     def rows_core():
         for u2, b2 in order:
@@ -1346,7 +1360,7 @@
         event(f"Q2{k}", functools.partial(across_q, k))
         event(f"Q3{k}", functools.partial(core_q, k))
 
-    go = ref["go"]
+    go = ref.go
     spread, core_go, partials = {}, {}, {}
     for w in range(3):
         piece = rc.at[w, a, b, my_rows]
@@ -1355,7 +1369,7 @@
             if H > 1:
                 spread[w, du] = links.copy(piece, go.at[w, my_rows, own_half], to)
             else:
-                partials[w, du] = links.copy(piece, ref["ru"].at[du - 1, w], to)
+                partials[w, du] = links.copy(piece, ref.ru.at[du - 1, w], to)
         at = go.at[w, :, own_half]
         core_go[w] = links.copy(at, at, sibling)
 
@@ -1370,7 +1384,7 @@
                 links.copies.remove(moved)
         for (w2, du), moved in partials.items():
             if w2 == w:
-                add_into(rc.at[w, a, b, my_rows], near(ref["ru"].at[du - 1, w], "c_rows", 7))
+                add_into(rc.at[w, a, b, my_rows], near(ref.ru.at[du - 1, w], "c_rows", 7))
         for (w2, du), moved in spread.items():
             if w2 == w:
                 moved.start()
@@ -1399,7 +1413,7 @@
             asu[du].arrived()
             add_rows(part(u, b, 0), landing["su", du], HALF)
         small[0:1, :] = jnp.zeros((1, D), F32)
-        lax.fori_loop(0, L // STEP, tok_back, 0)
+        steps(L // STEP, tok_back)
         late[0] = small[0:1, :]
         late_total.begin(0)
         back_tok.start()
@@ -1413,21 +1427,21 @@
         small[0:1, :] += jnp.sum(grad * normed, axis=0, keepdims=True)
         scaled = grad * gain_attn
         mean = jnp.mean(scaled * normed, axis=-1, keepdims=True)
-        ref["gtb"][strip(i), :] = (mg[strip(i), :] + inverse * (scaled - normed * mean)).astype(BF16)
-        return carried
-
-    back_tok = links.copy(ref["gtb"], ref["gtok"], origin, moves, moves)
+        ref.gtb[strip(i), :] = (mg[strip(i), :] + inverse * (scaled - normed * mean)).astype(BF16)
+        return carried
+
+    back_tok = links.copy(ref.gtb, ref.gtok, origin, moves, moves)
 
     def keep_tok():
-        kept = local(ref["gtb"], ref["gtok"], 0)
+        kept = local(ref.gtb, ref.gtok, 0)
         kept.start()
         kept.wait()
 
     event("end", rows_end)
     names = [name for name in SECOND[SECOND.index("BX") + 1 :] if name in events]
     play(names + [name for name in events if name not in names])
-    ref["g_small"][...] = sums[len(total.stages)]
-    ref["g_small"][0:1, :] = late[len(late_total.stages)]
+    ref.g_small[...] = sums[len(total.stages)]
+    ref.g_small[0:1, :] = late[len(late_total.stages)]
     for w in range(3):
         core_go[w].arrived()
     for moved in q_core.values():
@@ -1480,7 +1494,7 @@
     DH = D // 2
     NS = 8
     segments = lengths.shape[1]
-    dims = dict(R=R, S=S, L=L, D=D, HG=HG, E=E, CW=CW, SR=SR, H=H, SRH=SRH, segments=segments)
+    dims = types.SimpleNamespace(R=R, S=S, L=L, D=D, HG=HG, E=E, CW=CW, SR=SR, H=H, SRH=SRH, segments=segments)
 
     operands = dict(
         tokens=tokens, cotangent=cotangent, w_query=w_query, w_key=w_key, w_value=w_value,
@@ -1519,34 +1533,32 @@
     if H == 1:
         scratch["ru"] = ((um, 3, SR, DH), BF16)
     held = [jax.ShapeDtypeStruct(*v) for k, v in scratch.items() if k not in ("ags", "arc")]
-    dims["fits"] = sum(v.size * v.dtype.itemsize for v in held) <= VMEM_BYTES - (6 << 20)
+    dims.fits = sum(v.size * v.dtype.itemsize for v in held) <= VMEM_BYTES - (6 << 20)
     results = len(outputs)
     distant = ["out", "gtok"]
-    if dims["fits"]:
+    if dims.fits:
         scratch.pop("ags")
         scratch.pop("arc")
     else:
         for name in [k for k in ("xa", "cu", "ru") if k in scratch]:
             outputs[name] = scratch.pop(name)
             distant.append(name)
-        scratch["x_rows"] = ((L, D), BF16)
-        scratch["x_cols"] = ((T, 256), BF16)
-        scratch["c_rows"] = ((SRH, DH), BF16)
+        scratch.update(x_rows=((L, D), BF16), x_cols=((T, 256), BF16), c_rows=((SRH, DH), BF16))
     if U == 2:
-        scratch["lent_tok"] = scratch["lent_cot"] = ((L, D), BF16)
+        scratch.update(lent_tok=((L, D), BF16), lent_cot=((L, D), BF16))
     names = list(operands) + list(outputs) + list(scratch)
     names += ["send_sems", "recv_sems", "local_sems", "freed", "freed_again"]
 
     counted = [1024]
 
     def kernel(*refs):
-        named = dict(zip(names, refs))
-        for later, earlier in (("fg", "up"), ("dqt", "ot"), ("ug", "otok"), ("gtb", "ffin")):
-            named[later] = named[earlier]
-        named["wqt"] = named["dqkvt"].at[:, 0:D]
-        if dims["fits"]:
-            named["ags"] = named["xa"].at[pl.ds(0, T // 2)]
-            named["arc"] = named["xa"].at[pl.ds(T // 2, T // 2)]
+        named = types.SimpleNamespace(**dict(zip(names, refs)))
+        named.fg, named.dqt = named.up, named.ot
+        named.ug, named.gtb = named.otok, named.ffin
+        named.wqt = named.dqkvt.at[:, 0:D]
+        if dims.fits:
+            named.ags = named.xa.at[pl.ds(0, T // 2)]
+            named.arc = named.xa.at[pl.ds(T // 2, T // 2)]
         counted[0] = layer_kernel(dims, named)
 
     whole = pl.BlockSpec(memory_space=pltpu.VMEM)

time: 225 us -> 221 us (0.982)
  Pallas kernels: 224 us -> 218 us
    pallas_call x1, Pallas kernels: 218 us -> 213 us  [call(): pl.pallas_call(kernel, out_shape=[jax.ShapeDtypeStruct(*shape) for shape...]
where the time goes in v6:
time: 221 us; the launch traced here: 219 us
  Pallas kernels  218 us (99%)
    pallas_call x1, Pallas kernels, call(): pl.pallas_call(kernel, out_shape=[jax.ShapeDtypeStruct(*shape) for shape...  213 us
    pallas_call x1, Pallas kernels, shards(): pl.pallas_call(finish, out_shape=[jax.ShapeDtypeStruct(*shape) for shape...  5.7 us

profile of v6, /device:TPU:1, one launch (start us, length us, event | category | flops | bytes accessed | tf_op | source)
XLA Modules:
  0.0 219.3 jit_solution(15121217798892958505)
XLA Ops:
  0.7 212.8 %shard_map.297 = (bf16[256,1280]{1,0:T(8,128)(2,1)}, bf16[256,1280]{1,0:T(8,128)(2,1)}, bf16[3,160,1280]{2,1,0:T(8,128)(2,1)}, bf16[8,160,512]{2,1,0:T(8,128)(2,1)}, f32[8,1280]{1,0:T(8,128)}) custom-call(bf16[256,1280]{1,0:T(8,128)(2,1)} %refs_0_.1, bf16[256,1280]{1,0:T(8,128)(2,1)} %refs_1_.1, bf16[160,1280]{1,0:T(8,128)(2,1)} %refs_2_.1, ...), custom_call_target="tpu_custom_call" | custom-call | tf_op jit(solution)/shard_map/pallas_call | solution.py:1567
  213.4 5.7 %shard_map.298 = (bf16[256,1280]{1,0:T(8,128)(2,1)}, bf16[256,1280]{1,0:T(8,128)(2,1)}, f32[160,1280]{1,0:T(8,128)}, f32[160,1280]{1,0:T(8,128)}, f32[160,1280]{...) custom-call(bf16[256,1280]{1,0:T(8,128)(2,1)} %get-tuple-element.21., ...), custom_call_target="tpu_custom_call" | custom-call | tf_op jit(solution)/shard_map/pallas_call | solution.py:1618
